TPU v7x, 32 devices: a whole 2x2x4 slice. The times are simulated.
32 devices in a mesh: groups: 2 (over y), slab: 4 (over z), chan: 4 (over x, core).
Axes of the slice: x: 2, y: 2, z: 4, core: 2. Of those that a mesh axis runs over, the one named last changes fastest.
Arguments:
- field: bfloat16 [8, 32, 128, 128, 128], P(('groups', 'chan'), None, 'slab'), parts along dimension 0, may hold values from -6 to 6
- cotangent: bfloat16 [8, 32, 128, 128, 128], P(('groups', 'chan'), None, 'slab'), parts along dimension 0, may hold values from -6 to 6
- spec_weight: bfloat16 [2, 16, 128, 32, 32], P(None, None, 'slab'), may hold values from -1 to 1
- point_weight: bfloat16 [32, 32], replicated, may hold values from -1 to 1
- bias: float32 [32], replicated, may hold values from -4 to 4
Outputs:
- field_grad: bfloat16 [8, 32, 128, 128, 128], P(('groups', 'chan'), None, 'slab'), parts along dimension 0
- spec_grad: float32 [4, 16, 128, 32, 32], P('groups', None, 'slab'), parts along dimension 0
- point_grad: float32 [64, 32], P('groups'), parts along dimension 0
- bias_grad: float32 [64], P('groups'), parts along dimension 0
There are 2 independent parts, one for each index of `groups`. A program takes and returns all parts, laid end to end along the dimension named above; an argument that names none is the same for every part. Nothing has to cross between parts.
All inputs are finite; a program needn't handle non-finite values.
Results may differ from a plain program's by a relative error of at most 0.0061.
Values sent between devices are 32-bit elements; how exact they have to be, the bound alone decides.
No kernel may reach another device: no remote copies, remote signals or barrier semaphores. Data moves between devices by JAX's collectives and lax.ppermute only.
A program may use at most 448 MiB of HBM per device.

v0:
```python
import math

import jax
import jax.numpy as jnp
from jax import lax
from jax.sharding import PartitionSpec as P

NX = 128
NY = 128
NZ = 128
MX = 16
MY = 16
MZ = 8


highest = lax.Precision.HIGHEST


def contract(form, left, right):
    return jnp.einsum(form, left, right, precision=highest)


def mode_tables(length, count_modes, signed):
    position = jnp.arange(length, dtype=jnp.int32)[:, None]
    mode_index = jnp.arange(count_modes, dtype=jnp.int32)[None, :]
    if signed:
        frequency = jnp.where(mode_index >= count_modes // 2, mode_index - count_modes, mode_index)
    else:
        frequency = mode_index
    phase = position * frequency % length
    phase_angle = phase.astype(jnp.float32) * (2.0 * math.pi / length)
    return (jnp.cos(phase_angle), -jnp.sin(phase_angle))


def gelu_slope(value):
    inner = 0.7978845608 * (value + 0.044715 * value * value * value)
    tanh_value = jnp.tanh(inner)
    return 0.5 * (1.0 + tanh_value) + 0.5 * value * (
        1.0 - tanh_value * tanh_value
    ) * 0.7978845608 * (1.0 + 0.134145 * value * value)


def x_forward(spectra, row_cos, row_sin):
    a_real, a_imag = (spectra[0], spectra[1])
    u_real = contract("scxk,xm->scmk", a_real, row_cos) - contract("scxk,xm->scmk", a_imag, row_sin)
    u_imag = contract("scxk,xm->scmk", a_imag, row_cos) + contract("scxk,xm->scmk", a_real, row_sin)
    return jnp.stack([u_real, u_imag])


def x_inverse(spectra, row_cos, row_sin):
    h_real, h_imag = (spectra[0], spectra[1])
    b_real = contract("scmk,xm->scxk", h_real, row_cos) + contract("scmk,xm->scxk", h_imag, row_sin)
    b_imag = contract("scmk,xm->scxk", h_imag, row_cos) - contract("scmk,xm->scxk", h_real, row_sin)
    return jnp.stack([b_real, b_imag])


def per_device(field, cotangent, spec_weight, point_weight, bias):
    samples, channels, cx_rows, ny_cells, nz_cells = field.shape
    ycos, ysin = mode_tables(NY, MY, True)
    zcos, zsin = mode_tables(NZ, MZ, False)
    xcos, xsin = mode_tables(NX, MX, True)
    ycos_half = ycos.astype(jnp.bfloat16)
    ysin_half = ysin.astype(jnp.bfloat16)
    y_table = jnp.concatenate([ycos_half, ysin_half], axis=1)
    z_table = jnp.concatenate([zcos, zsin], axis=1)
    scale_forward = 1.0 / math.sqrt(NX * NY * NZ)
    scale_inverse = 1.0 / math.sqrt(MX * MY * MZ)
    mode_pairs = MY * MZ

    def to_spectrum(values):
        q_both = jnp.einsum("scxyz,yk->scxkz", values, y_table, preferred_element_type=jnp.float32)
        z_real = contract("scxkz,zj->scxkj", q_both[:, :, :, :MY], z_table)
        z_imag = contract("scxkz,zj->scxkj", q_both[:, :, :, MY:], z_table)
        r_real = z_real[..., :MZ] - z_imag[..., MZ:]
        r_imag = z_real[..., MZ:] + z_imag[..., :MZ]
        local_spec = jnp.stack([r_real, r_imag]).reshape(2, samples, channels, cx_rows, mode_pairs)
        turned = lax.all_to_all(local_spec, "slab", split_axis=4, concat_axis=3, tiled=True)
        owned = x_forward(turned, xcos, xsin)
        return owned * scale_forward

    def from_spectrum(spectra):
        rows_all = x_inverse(spectra, xcos, xsin)
        local_spec = lax.all_to_all(rows_all, "slab", split_axis=3, concat_axis=4, tiled=True)
        b_real = local_spec[0].reshape(samples, channels, cx_rows, MY, MZ)
        b_imag = local_spec[1].reshape(samples, channels, cx_rows, MY, MZ)
        f_real = contract("scxkj,zj->scxkz", b_real, zcos) + contract(
            "scxkj,zj->scxkz", b_imag, zsin
        )
        f_imag = contract("scxkj,zj->scxkz", b_imag, zcos) - contract(
            "scxkj,zj->scxkz", b_real, zsin
        )
        f_both = jnp.concatenate([f_real, f_imag], axis=3).astype(jnp.bfloat16)
        result = jnp.einsum("scxkz,yk->scxyz", f_both, y_table, preferred_element_type=jnp.float32)
        return result * scale_inverse

    weights = spec_weight.astype(jnp.float32)
    w_real, w_imag = (weights[0], weights[1])
    uhat = to_spectrum(field)
    v_real = contract("scmk,mkco->somk", uhat[0], w_real) - contract(
        "scmk,mkco->somk", uhat[1], w_imag
    )
    v_imag = contract("scmk,mkco->somk", uhat[1], w_real) + contract(
        "scmk,mkco->somk", uhat[0], w_imag
    )
    spectral = from_spectrum(jnp.stack([v_real, v_imag]))
    pointwise = jnp.einsum(
        "co,scxyz->soxyz", point_weight, field, preferred_element_type=jnp.float32
    )
    pre = spectral + pointwise + bias[None, :, None, None, None]
    dpre = (cotangent.astype(jnp.float32) * gelu_slope(pre)).astype(jnp.bfloat16)
    ghat = to_spectrum(dpre)
    h_real = contract("somk,mkco->scmk", ghat[0], w_real) + contract(
        "somk,mkco->scmk", ghat[1], w_imag
    )
    h_imag = contract("somk,mkco->scmk", ghat[1], w_real) - contract(
        "somk,mkco->scmk", ghat[0], w_imag
    )
    back_spectral = from_spectrum(jnp.stack([h_real, h_imag]))
    back_point = jnp.einsum(
        "co,soxyz->scxyz", point_weight, dpre, preferred_element_type=jnp.float32
    )
    field_grad = (back_spectral + back_point).astype(jnp.bfloat16)
    dw_real = contract("scmk,somk->mkco", uhat[0], ghat[0]) + contract(
        "scmk,somk->mkco", uhat[1], ghat[1]
    )
    dw_imag = contract("scmk,somk->mkco", uhat[0], ghat[1]) - contract(
        "scmk,somk->mkco", uhat[1], ghat[0]
    )
    spec_grad = lax.psum(jnp.stack([dw_real, dw_imag]), "chan")
    point_part = jnp.einsum("scxyz,soxyz->co", field, dpre, preferred_element_type=jnp.float32)
    bias_part = jnp.sum(dpre.astype(jnp.float32), axis=(0, 2, 3, 4))
    point_total, bias_total = lax.psum((point_part, bias_part), ("slab", "chan"))
    norm_scale = 1.0 / math.sqrt(samples * lax.axis_size("chan") * NX * NY * NZ)
    return (field_grad, spec_grad, point_total * norm_scale, bias_total * norm_scale)


def solution(mesh):
    return jax.shard_map(
        per_device,
        mesh=mesh,
        in_specs=(
            P(("groups", "chan"), None, "slab", None, None),
            P(("groups", "chan"), None, "slab", None, None),
            P(None, None, "slab", None, None),
            P(),
            P(),
        ),
        out_specs=(
            P(("groups", "chan"), None, "slab", None, None),
            P("groups", None, "slab", None, None),
            P("groups", None),
            P("groups"),
        ),
        check_vma=False,
    )
```

profile of v0, /device:TPU:0, one launch (start us, length us, event | category | flops | bytes accessed | tf_op | source)
XLA Modules:
  0.0 1192.4 jit_solution(9803070952053069517)
XLA Ops:
  7.4 19.3 %convolution_bitcast_fusion.1 = f32[1,32,32,32,128]{4,3,2,1,0:T(8,128)} fusion(bf16[1,32,32,128,128]{4,3,2,1,0:T(8,128)(2,1)} %param.5, bf16[128,16]{0,1:T(8,128)(2,1)S(1)} %get-tuple-element.57, bf16[128,16]{0,1:T(8,128)(2,1)S(1)} %get-tuple-element.56), kind=kOutput, calls=%fused_computation.31 | convolution fusion | flops 1073758208 | bytes 50339840 | tf_op jit(solution)/shard_map/scxyz,yk->scxkz/dot_general | solution.py:71
  26.7 63.8 %fusion.35 = f32[1,32,32,16,16]{3,4,2,1,0:T(8,128)} fusion(f32[1,32,32,32,128]{4,3,2,1,0:T(8,128)} %convolution_bitcast_fusion.1, f32[128,8]{0,1:T(8,128)S(1)} %get-tuple-element.60, f32[128,8]{0,1:T(8,128)S(1)} %get-tuple-element.61), kind=kOutput, calls=%fused_computation.67 | convolution fusion | flops 402655232 | bytes 9445376 | tf_op jit(solution)/shard_map/scxkz,zj->scxkj/dot_general | solution.py:20
  90.5 61.1 %fusion.34 = f32[1,32,32,16,16]{3,4,2,1,0:T(8,128)} fusion(f32[1,32,32,32,128]{4,3,2,1,0:T(8,128)S(1)} %copy-done.2, f32[128,8]{0,1:T(8,128)S(1)} %get-tuple-element.60, f32[128,8]{0,1:T(8,128)S(1)} %get-tuple-element.61), kind=kOutput, calls=%fused_computation.66 | convolution fusion | flops 402655232 | bytes 9445376 | tf_op jit(solution)/shard_map/scxkz,zj->scxkj/dot_general | solution.py:20
  151.6 11.2 slice_subtract_fusion.1
  165.8 3.8 copy.128
  171.9 4.5 copy.260
  176.3 3.9 reshape.385
  180.2 31.8 %all_to_all.60 = f32[4,1,65536]{2,1,0:T(1,128)S(1)} all-to-all(f32[4,1,65536]{2,1,0:T(1,128)S(1)} %reshape.385), channel_id=1, replica_groups=mesh['groups'=2,'slab'=4,'chan'=4] {'slab'}, dimensions={0} | all-to-all | bytes 2097152 | tf_op jit(solution)/shard_map/all_to_all | solution.py:77
  219.8 5.7 copy.226
  225.5 4.8 fusion.240
  247.7 11.0 fusion.18
  263.7 4.4 copy.133
  268.1 4.8 reshape.387
  276.7 40.4 %fusion.14 = f32[32,128,128,32]{2,3,1,0:T(8,128)} fusion(bf16[32,32,128,128]{3,2,1,0:T(8,128)(2,1)} %bitcast.371, bf16[32,32]{1,0:T(8,128)(2,1)S(1)} %copy-done), kind=kOutput, calls=%fused_computation.19 | convolution fusion | flops 1073741824 | bytes 100665344 | tf_op jit(solution)/shard_map/co,scxyz->soxyz/dot_general | solution.py:106
  324.3 5.9 copy.227
  330.2 4.0 fusion.239
  341.9 15.5 %fusion.110 = f32[32,32,16,128]{3,2,1,0:T(8,128)S(1)} fusion(f32[32,32,16,8]{2,3,1,0:T(8,128)} %copy.138), kind=kOutput, calls=%fused_computation.164 | convolution fusion | flops 201340928 | bytes 8912896 | tf_op jit(solution)/shard_map/scxkj,zj->scxkz/dot_general | solution.py:20
  357.4 14.0 %fusion.112 = f32[32,32,16,128]{3,2,1,0:T(8,128)S(1)} fusion(f32[32,32,16,8]{2,3,1,0:T(8,128)S(1)} %copy-done.3), kind=kOutput, calls=%fused_computation.166 | convolution fusion | flops 201340928 | bytes 8912896 | tf_op jit(solution)/shard_map/scxkj,zj->scxkz/dot_general | solution.py:20
  371.5 14.0 %subtract_convert_fusion.1 = bf16[32,32,16,128]{3,2,1,0:T(8,128)(2,1)S(1)} fusion(f32[32,32,16,128]{3,2,1,0:T(8,128)S(1)} %fusion.110, f32[32,32,16,8]{2,3,1,0:T(8,128)S(1)} %copy-done.3), kind=kOutput, calls=%fused_computation.58 | convolution fusion | flops 205536256 | bytes 13107200 | tf_op jit(solution)/shard_map/scxkj,zj->scxkz/dot_general | solution.py:20
  385.6 14.1 %add_convert_fusion.1 = bf16[32,32,16,128]{3,2,1,0:T(8,128)(2,1)S(1)} fusion(f32[32,32,16,128]{3,2,1,0:T(8,128)S(1)} %fusion.112, f32[32,32,16,8]{2,3,1,0:T(8,128)S(1)} %copy-done.5), kind=kOutput, calls=%fused_computation.59 | convolution fusion | flops 205536256 | bytes 13107200 | tf_op jit(solution)/shard_map/scxkj,zj->scxkz/dot_general | solution.py:20
  399.7 67.6 %convert_reduce_fusion = (f32[32]{0:T(128)S(1)}, bf16[1,32,32,128,128]{4,3,2,1,0:T(8,128)(2,1)}) fusion(f32[32]{0:T(128)S(1)} %copy-done.21, f32[32,128,128,32]{2,3,1,0:T(8,128)} %fusion.14, bf16[32,32,16,128]{3,2,1,0:T(8,128)(2,1)S(1)} %subtract_convert_fusion.1, bf16[32,32,16,128]{3,2,1,0:T(8,128)(2,1)S(1)} %add_convert_fusion.1, ...), kind=kOutput, calls=%fused_computation.13 | convolution fusion | flops 1509965824 | bytes 142614784 | tf_op jit(solution)/shard_map/scxkz,yk->scxyz/dot_general | solution.py:93
  467.2 19.3 %convolution_bitcast_fusion = f32[1,32,32,32,128]{4,3,2,1,0:T(8,128)} fusion(bf16[1,32,32,128,128]{4,3,2,1,0:T(8,128)(2,1)} %get-tuple-element.59, bf16[128,16]{0,1:T(8,128)(2,1)S(1)} %get-tuple-element.57, bf16[128,16]{0,1:T(8,128)(2,1)S(1)} %get-tuple-element.56), kind=kOutput, calls=%fused_computation.30 | convolution fusion | flops 1073758208 | bytes 50339840 | tf_op jit(solution)/shard_map/scxyz,yk->scxkz/dot_general | solution.py:71
  486.6 63.7 %fusion.37 = f32[1,32,32,16,16]{3,4,2,1,0:T(8,128)} fusion(f32[1,32,32,32,128]{4,3,2,1,0:T(8,128)} %convolution_bitcast_fusion, f32[128,8]{0,1:T(8,128)S(1)} %copy-done.14, f32[128,8]{0,1:T(8,128)S(1)} %copy-done.16), kind=kOutput, calls=%fused_computation.69 | convolution fusion | flops 402655232 | bytes 9445376 | tf_op jit(solution)/shard_map/scxkz,zj->scxkj/dot_general | solution.py:20
  550.3 61.1 %fusion.36 = f32[1,32,32,16,16]{3,4,2,1,0:T(8,128)} fusion(f32[1,32,32,32,128]{4,3,2,1,0:T(8,128)S(1)} %copy-done.1, f32[128,8]{0,1:T(8,128)S(1)} %copy-done.14, f32[128,8]{0,1:T(8,128)S(1)} %copy-done.16), kind=kOutput, calls=%fused_computation.68 | convolution fusion | flops 402655232 | bytes 9445376 | tf_op jit(solution)/shard_map/scxkz,zj->scxkj/dot_general | solution.py:20
  611.3 11.2 slice_subtract_fusion
  631.6 4.5 copy.259
  636.0 4.8 reshape.389
  640.9 5.1 all-to-all-start.2
  645.9 40.3 %fusion.11 = f32[32,128,128,32]{2,3,1,0:T(8,128)} fusion(bf16[32,32,128,128]{3,2,1,0:T(8,128)(2,1)} %bitcast.373, bf16[32,32]{1,0:T(8,128)(2,1)S(1)} %copy-done), kind=kOutput, calls=%fused_computation.16 | convolution fusion | flops 1073741824 | bytes 100665344 | tf_op jit(solution)/shard_map/co,soxyz->scxyz/dot_general | solution.py:119
  686.3 60.2 %fusion.46 = f32[32,32]{0,1:T(8,128)S(1)} fusion(bf16[32,32,128,128]{3,2,1,0:T(8,128)(2,1)} %bitcast.372, bf16[32,32,128,128]{3,2,1,0:T(8,128)(2,1)} %bitcast.374), kind=kOutput, calls=%fused_computation.86 | convolution fusion | flops 1073741824 | bytes 67112960 | tf_op jit(solution)/shard_map/scxyz,soxyz->co/dot_general | solution.py:130
  746.4 59.7 %all-reduce = (f32[32,32]{0,1:T(8,128)S(1)}, f32[32]{0:T(128)S(1)}) all-reduce(f32[32,32]{0,1:T(8,128)S(1)} %fusion.46, f32[32]{0:T(128)S(1)} %get-tuple-element.58), channel_id=1, replica_groups=mesh['groups'=2,'slab'=4,'chan'=4] {'slab','chan'}, use_global_device_ids=true, to_apply=%region_1.2 | all-reduce | flops 1056 | bytes 8448 | tf_op jit(solution)/shard_map/psum | solution.py:132
  813.4 5.7 copy.229
  819.0 4.7 fusion.238
  841.7 11.3 fusion.22
  857.9 4.4 copy.150
  862.3 4.8 reshape.391
  872.0 4.8 add_bitcast_fusion
  876.8 7.9 pad_maximum_fusion
  884.7 7.7 all-to-all-done.3
  899.5 5.7 copy.230
  905.2 4.1 fusion.237
  917.0 15.8 %fusion.106 = f32[32,32,16,128]{3,2,1,0:T(8,128)S(1)} fusion(f32[32,32,16,8]{2,3,1,0:T(8,128)} %copy.155), kind=kOutput, calls=%fused_computation.160 | convolution fusion | flops 201340928 | bytes 8912896 | tf_op jit(solution)/shard_map/scxkj,zj->scxkz/dot_general | solution.py:20
  932.8 13.9 %fusion.108 = f32[32,32,16,128]{3,2,1,0:T(8,128)S(1)} fusion(f32[32,32,16,8]{2,3,1,0:T(8,128)S(1)} %copy-done.4), kind=kOutput, calls=%fused_computation.162 | convolution fusion | flops 201340928 | bytes 8912896 | tf_op jit(solution)/shard_map/scxkj,zj->scxkz/dot_general | solution.py:20
  946.7 14.4 %subtract_convert_fusion = bf16[32,32,16,128]{3,2,1,0:T(8,128)(2,1)S(1)} fusion(f32[32,32,16,128]{3,2,1,0:T(8,128)S(1)} %fusion.106, f32[32,32,16,8]{2,3,1,0:T(8,128)S(1)} %copy-done.4), kind=kOutput, calls=%fused_computation.56 | convolution fusion | flops 205536256 | bytes 13107200 | tf_op jit(solution)/shard_map/scxkj,zj->scxkz/dot_general | solution.py:20
  961.1 15.5 %add_convert_fusion = bf16[32,32,16,128]{3,2,1,0:T(8,128)(2,1)} fusion(f32[32,32,16,128]{3,2,1,0:T(8,128)S(1)} %fusion.108, f32[32,32,16,8]{2,3,1,0:T(8,128)S(1)} %copy-done.6), kind=kOutput, calls=%fused_computation.57 | convolution fusion | flops 205536256 | bytes 13107200 | tf_op jit(solution)/shard_map/scxkj,zj->scxkz/dot_general | solution.py:20
  976.6 49.7 %fusion.7 = bf16[1,32,32,128,128]{4,3,2,1,0:T(8,128)(2,1)} fusion(f32[32,128,128,32]{2,3,1,0:T(8,128)} %fusion.11, bf16[32,32,16,128]{3,2,1,0:T(8,128)(2,1)S(1)} %subtract_convert_fusion, bf16[32,32,16,128]{3,2,1,0:T(8,128)(2,1)} %add_convert_fusion, bf16[128,16]{0,1:T(8,128)(2,1)S(1)} %copy-done.20, bf16[128,16]{0,1:T(8,128)(2,1)S(1)} %copy-done.18), kind=kOutput, calls=%fused_computation.10 | convolution fusion | flops 1140867072 | bytes 109060096 | tf_op jit(solution)/shard_map/scxkz,yk->scxyz/dot_general | solution.py:93
  1026.3 147.3 %all-reduce.3.cloned.1.call-done = f32[2,16,32,32,32]{4,3,2,1,0:T(8,128)} async-done(((f32[2,16,32,32,32]{4,3,2,1,0:T(8,128)}), f32[2,16,32,32,32]{4,3,2,1,0:T(8,128)}) %all-reduce.3.cloned.1.call-update) | async-done | bytes 4194320 | tf_op jit(solution)/shard_map/psum | solution.py:129
  1173.6 11.7 copy.262
  (120 shorter events, 112.7 us)
Async XLA Ops:
  7.2 269.6 %copy-start = (bf16[32,32]{1,0:T(8,128)(2,1)S(1)}, bf16[32,32]{1,0:T(8,128)(2,1)}, u32[]{:S(2)}) copy-start(bf16[32,32]{1,0:T(8,128)(2,1)} %param.8) | copy-start | bytes 6148
  7.2 255.4 %copy-start.11 = (s32[16]{0:T(128)}, s32[16]{0:T(128)S(1)}, u32[]{:S(2)}) copy-start(s32[16]{0:T(128)S(1)} %compare_select_fusion) | copy-start | bytes 196
  7.3 83.3 %copy-start.13 = (f32[128,8]{0,1:T(8,128)}, f32[128,8]{0,1:T(8,128)S(1)}, u32[]{:S(2)}) copy-start(f32[128,8]{0,1:T(8,128)S(1)} %get-tuple-element.60) | copy-start | bytes 12292
  7.3 83.3 %copy-start.15 = (f32[128,8]{0,1:T(8,128)}, f32[128,8]{0,1:T(8,128)S(1)}, u32[]{:S(2)}) copy-start(f32[128,8]{0,1:T(8,128)S(1)} %get-tuple-element.61) | copy-start | bytes 12292
  7.4 459.8 %copy-start.17 = (bf16[128,16]{0,1:T(8,128)(2,1)}, bf16[128,16]{0,1:T(8,128)(2,1)S(1)}, u32[]{:S(2)}) copy-start(bf16[128,16]{0,1:T(8,128)(2,1)S(1)} %get-tuple-element.56) | copy-start | bytes 12292
  7.4 459.8 %copy-start.19 = (bf16[128,16]{0,1:T(8,128)(2,1)}, bf16[128,16]{0,1:T(8,128)(2,1)S(1)}, u32[]{:S(2)}) copy-start(bf16[128,16]{0,1:T(8,128)(2,1)S(1)} %get-tuple-element.57) | copy-start | bytes 12292
  26.7 63.8 %copy-start.2 = (f32[1,32,32,32,128]{4,3,2,1,0:T(8,128)S(1)}, f32[1,32,32,32,128]{4,3,2,1,0:T(8,128)}, u32[]{:S(2)}) copy-start(f32[1,32,32,32,128]{4,3,2,1,0:T(8,128)} %convolution_bitcast_fusion.1) | copy-start | bytes 50331652
  247.5 15.1 %copy-start.7 = (f32[16,32,32]{2,1,0:T(8,128)}, f32[16,32,32]{2,1,0:T(8,128)S(1)}, u32[]{:S(2)}) copy-start(f32[16,32,32]{2,1,0:T(8,128)S(1)} %copy.231) | copy-start | bytes 196612
  247.7 14.9 %copy-start.9 = (f32[16,32,32]{2,1,0:T(8,128)}, f32[16,32,32]{2,1,0:T(8,128)S(1)}, u32[]{:S(2)}) copy-start(f32[16,32,32]{2,1,0:T(8,128)S(1)} %copy.232) | copy-start | bytes 196612
  273.0 44.1 %all-to-all-start.1 = ((f32[4,1,65536]{2,1,0:T(1,128)}), f32[4,1,65536]{2,1,0:T(1,128)S(1)}, u32[]{:S(2)}, u32[]{:S(2)}) async-start(f32[4,1,65536]{2,1,0:T(1,128)} %reshape.387), calls=%async_computation.1 | async-start | bytes 2097152 | tf_op jit(solution)/shard_map/all_to_all | solution.py:83
  341.9 15.5 %copy-start.3 = (f32[32,32,16,8]{2,3,1,0:T(8,128)S(1)}, f32[32,32,16,8]{2,3,1,0:T(8,128)}, u32[]{:S(2)}) copy-start(f32[32,32,16,8]{2,3,1,0:T(8,128)} %copy.136) | copy-start | bytes 1572868
  371.5 14.1 %copy-start.5 = (f32[32,32,16,8]{2,3,1,0:T(8,128)S(1)}, f32[32,32,16,8]{2,3,1,0:T(8,128)}, u32[]{:S(2)}) copy-start(f32[32,32,16,8]{2,3,1,0:T(8,128)} %copy.138) | copy-start | bytes 1572868
  385.5 14.1 %copy-start.21 = (f32[32]{0:T(128)S(1)}, f32[32]{0:T(128)}, u32[]{:S(2)}) copy-start(f32[32]{0:T(128)} %param.9) | copy-start | bytes 388
  467.2 19.3 %copy-start.14 = (f32[128,8]{0,1:T(8,128)S(1)}, f32[128,8]{0,1:T(8,128)}, u32[]{:S(2)}) copy-start(f32[128,8]{0,1:T(8,128)} %copy-done.13) | copy-start | bytes 12292
  467.2 19.3 %copy-start.16 = (f32[128,8]{0,1:T(8,128)S(1)}, f32[128,8]{0,1:T(8,128)}, u32[]{:S(2)}) copy-start(f32[128,8]{0,1:T(8,128)} %copy-done.15) | copy-start | bytes 12292
  486.6 63.7 %copy-start.1 = (f32[1,32,32,32,128]{4,3,2,1,0:T(8,128)S(1)}, f32[1,32,32,32,128]{4,3,2,1,0:T(8,128)}, u32[]{:S(2)}) copy-start(f32[1,32,32,32,128]{4,3,2,1,0:T(8,128)} %convolution_bitcast_fusion) | copy-start | bytes 50331652
  640.9 165.3 %all-to-all-start.2 = ((f32[4,1,65536]{2,1,0:T(1,128)}), f32[4,1,65536]{2,1,0:T(1,128)S(1)}, u32[]{:S(2)}, u32[]{:S(2)}) async-start(f32[4,1,65536]{2,1,0:T(1,128)} %reshape.389), calls=%async_computation.2 | async-start | bytes 2097152 | tf_op jit(solution)/shard_map/all_to_all | solution.py:77
  819.0 8.8 copy-start.12
  856.8 15.2 %copy-start.8 = (f32[16,32,32]{2,1,0:T(8,128)S(1)}, f32[16,32,32]{2,1,0:T(8,128)}, u32[]{:S(2)}) copy-start(f32[16,32,32]{2,1,0:T(8,128)} %copy-done.7) | copy-start | bytes 196612
  856.8 15.2 %copy-start.10 = (f32[16,32,32]{2,1,0:T(8,128)S(1)}, f32[16,32,32]{2,1,0:T(8,128)}, u32[]{:S(2)}) copy-start(f32[16,32,32]{2,1,0:T(8,128)} %copy-done.9) | copy-start | bytes 196612
  867.2 25.1 %all-to-all-start.3 = ((f32[4,1,65536]{2,1,0:T(1,128)}), f32[4,1,65536]{2,1,0:T(1,128)S(1)}, u32[]{:S(2)}, u32[]{:S(2)}) async-start(f32[4,1,65536]{2,1,0:T(1,128)} %reshape.391), calls=%async_computation.3 | async-start | bytes 2097152 | tf_op jit(solution)/shard_map/all_to_all | solution.py:83
  870.7 302.9 %all-reduce.3.cloned.1.call-start = ((), (), s32[]{:S(2)}) async-start(), calls=%async_computation.4 | async-start | bytes 33554432 | tf_op jit(solution)/shard_map/psum | solution.py:129
  917.0 15.8 %copy-start.4 = (f32[32,32,16,8]{2,3,1,0:T(8,128)S(1)}, f32[32,32,16,8]{2,3,1,0:T(8,128)}, u32[]{:S(2)}) copy-start(f32[32,32,16,8]{2,3,1,0:T(8,128)} %copy.153) | copy-start | bytes 1572868
  946.7 14.4 %copy-start.6 = (f32[32,32,16,8]{2,3,1,0:T(8,128)S(1)}, f32[32,32,16,8]{2,3,1,0:T(8,128)}, u32[]{:S(2)}) copy-start(f32[32,32,16,8]{2,3,1,0:T(8,128)} %copy.155) | copy-start | bytes 1572868
  961.1 15.5 %copy-start.18 = (bf16[128,16]{0,1:T(8,128)(2,1)S(1)}, bf16[128,16]{0,1:T(8,128)(2,1)}, u32[]{:S(2)}) copy-start(bf16[128,16]{0,1:T(8,128)(2,1)} %copy-done.17) | copy-start | bytes 12292
  961.1 15.5 %copy-start.20 = (bf16[128,16]{0,1:T(8,128)(2,1)S(1)}, bf16[128,16]{0,1:T(8,128)(2,1)}, u32[]{:S(2)}) copy-start(bf16[128,16]{0,1:T(8,128)(2,1)} %copy-done.19) | copy-start | bytes 12292
Sparse Core Ops, SparseCore 0:
  884.8 288.7 all-reduce.2
where the time goes:
time: 1200 us; the launch traced here: 1190 us
  matrix products  690 us (58%)
  waiting for transfers between devices  155 us (13%)
  local copies, waits for them, and re-layouts  151 us (13%)
  blocking collectives  91.6 us (8%)
  other arithmetic  77.9 us (6%)
  between operations  15 us (1%)
  starting transfers between devices  12.4 us (1%)
    dot_general x28, matrix products, contract(): return jnp.einsum(form, left, right, precision=highest)  393 us
    psum x1, waiting for transfers between devices, per_device(): spec_grad = lax.psum(jnp.stack([dw_real, dw_imag]), 'chan')  147 us
    dot_general x2, matrix products, from_spectrum(): jnp.einsum('scxkz,yk->scxyz', f_both, y_table, preferred_element_type=jnp...  117 us
    dot_general x1, matrix products, per_device(): jnp.einsum('scxyz,soxyz->co', field, dpre, preferred_element_type=jnp.flo...  60.2 us
    psum x1, blocking collectives, per_device(): lax.psum((point_part, bias_part), ('slab', 'chan'))  59.7 us
    unnamed x60, local copies, waits for them, and re-layouts  45.5 us
    dot_general x1, matrix products, per_device(): jnp.einsum('co,scxyz->soxyz', point_weight, field, preferred_element_type...  40.4 us
    dot_general x1, matrix products, per_device(): jnp.einsum('co,soxyz->scxyz', point_weight, dpre, preferred_element_type=...  40.3 us
  transfers between devices with their start and end apart: 4, of which 2 were waited for; matrix products, arithmetic and copies ran while one was open for 24% of the time, Pallas kernels for 0%

commit v1 on v0

v1 whole, which is shorter than its diff:
```python
import functools
import math

import jax
import jax.numpy as jnp
import numpy as np
from jax import lax
from jax.experimental import pallas as pl
from jax.experimental.pallas import tpu as pltpu
from jax.sharding import PartitionSpec as P

NX = 128
NY = 128
NZ = 128
MX = 16
MY = 16
MZ = 8
LANES = 128
GROUP = 8

FIELD_CB = 4
GRAD_CB = 2

f32 = jnp.float32
bf16 = jnp.bfloat16

GA = 0.7978845608
GB = 0.044715
GK = (GA * GB) ** (1.0 / 3.0)
GALPHA = GA / GK

SCALE_FORWARD = 1.0 / math.sqrt(NX * NY * NZ)
SCALE_INVERSE = 1.0 / math.sqrt(MX * MY * MZ)


def mode_table(length, count, signed):
    position = np.arange(length)[:, None]
    index = np.arange(count)[None, :]
    frequency = np.where(index >= count // 2, index - count, index) if signed else index
    angle = (position * frequency % length).astype(np.float64) * (2.0 * math.pi / length)
    return np.cos(angle).astype(np.float32), (-np.sin(angle)).astype(np.float32)


def bf(value):
    return np.asarray(value, np.float32).astype(jnp.bfloat16)


def split_bf(value):
    high = bf(value)
    return high, bf(np.asarray(value, np.float32) - high.astype(np.float32))


def z_forward_table():
    zc, zs = mode_table(NZ, MZ, False)
    block = np.concatenate([zc, zs], axis=1)
    table = np.zeros((GROUP, NZ, GROUP, 2 * MZ), np.float32)
    for x in range(GROUP):
        table[x, :, x] = block
    return bf(table.reshape(GROUP * NZ, GROUP * 2 * MZ))


def z_inverse_table():
    zc, zs = mode_table(NZ, MZ, False)
    block = np.concatenate([zc, zs], axis=1).T
    table = np.zeros((GROUP // 2, GROUP, 2 * MZ, 2, NZ), np.float32)
    for x in range(GROUP):
        table[x // 2, x, :, x % 2] = block
    return bf(table.reshape(GROUP // 2, GROUP * 2 * MZ, 2 * NZ))


def y_tables():
    yc, ys = mode_table(NY, MY, True)
    forward = np.concatenate([yc.T, ys.T], axis=0)
    inverse = np.concatenate([yc, ys, yc, ys], axis=1)
    return bf(forward), bf(inverse)


def x_forward_table():
    xc, xs = mode_table(NX, MX, True)
    table = np.zeros((NX, 2, MZ, 2, MX, MZ), np.float32)
    for kz in range(MZ):
        table[:, 0, kz, 0, :, kz] = xc
        table[:, 1, kz, 0, :, kz] = -xs
        table[:, 0, kz, 1, :, kz] = xs
        table[:, 1, kz, 1, :, kz] = xc
    return table.reshape(NX * 2 * MZ, 2 * MX * MZ) * SCALE_FORWARD


def x_inverse_table(scale, ns):
    xc, xs = mode_table(NX, MX, True)
    table = np.zeros((2, MX, MZ, 2, NX, 2, MZ), np.float32)
    for kz in range(MZ):
        re_re, im_re = xc.T, xs.T
        re_im, im_im = -xs.T, xc.T
        table[0, :, kz, 0, :, 0, kz] = re_re
        table[1, :, kz, 0, :, 0, kz] = im_re
        table[0, :, kz, 0, :, 1, kz] = re_im
        table[1, :, kz, 0, :, 1, kz] = im_im
        table[0, :, kz, 1, :, 0, kz] = re_im
        table[1, :, kz, 1, :, 0, kz] = im_im
        table[0, :, kz, 1, :, 1, kz] = -re_re
        table[1, :, kz, 1, :, 1, kz] = -im_re
    table = table.reshape(2 * MX * MZ, 2, ns, NX // ns * 2 * MZ).transpose(2, 0, 1, 3)
    return table.reshape(ns, 2 * MX * MZ, -1) * scale


def dot(a, b):
    return jnp.dot(a, b, preferred_element_type=f32)


def parts(value):
    high = value.astype(bf16)
    return high, (value - high.astype(f32)).astype(bf16)


def dot3(a, bh, bl):
    ah, al = parts(a)
    return dot(ah, bh) + dot(al, bh) + dot(ah, bl)


def z_forward(tiles, zf):
    wide = jnp.concatenate(
        [
            jnp.concatenate(tiles[g : g + GROUP], axis=1)
            for g in range(0, len(tiles), GROUP)
        ],
        axis=0,
    )
    q = dot(wide, zf).astype(bf16)
    return [q[g : g + NY] for g in range(0, q.shape[0], NY)]


def y_forward(groups, yf):
    r = dot(yf, jnp.concatenate(groups, axis=1))
    top, bot = r[:MY], r[MY:]
    lanes = bot.shape[1]
    at = lax.broadcasted_iota(jnp.int32, top.shape, 1) % (2 * MZ)
    return jnp.where(
        at < MZ, top - pltpu.roll(bot, lanes - MZ, 1), top + pltpu.roll(bot, MZ, 1)
    )


def x_forward_out(me, ns, channels, r_scr, xfh, xfl, outs):
    rows = (MY // ns) * channels
    r = jnp.concatenate([r_scr[i] for i in range(r_scr.shape[0])], axis=1)
    width = xfh.shape[1]
    done = dot3(r, xfh[...], xfl[...])
    for i in range(width // LANES):
        r_scr[i] = done[:, i * LANES : (i + 1) * LANES]
    for k in range(ns):
        owner = lax.rem(me + k, ns)
        at = pl.ds(pl.multiple_of(owner * rows, rows), rows)
        for i in range(width // LANES):
            outs[k][:, :, i * LANES : (i + 1) * LANES] = r_scr[i, at, :].reshape(
                MY // ns, channels, LANES
            )


def x_inverse_in(me, ns, channels, ins, xih, xil, b_scr):
    rows = (MY // ns) * channels
    for k in range(ns):
        owner = lax.rem(me + ns - k, ns)
        h = ins[k][...].reshape(rows, -1)
        b = dot3(h, xih[0], xil[0])
        for i in range(b_scr.shape[0]):
            at = pl.ds(pl.multiple_of(owner * rows, rows), rows)
            b_scr[i, at, :] = b[:, i * LANES : (i + 1) * LANES]


def put_channel(scr, c, channels, value):
    for i in range(scr.shape[0]):
        scr[i, pl.ds(c, MY, stride=channels), :] = value[:, i * LANES : (i + 1) * LANES]


def get_channel(scr, c, channels, blocks):
    return jnp.concatenate(
        [scr[i, pl.ds(c, MY, stride=channels), :] for i in blocks], axis=1
    )


def y_inverse(bs, yi):
    lanes = bs[0].shape[1] // 2
    rhs = []
    for b in bs:
        high, low = parts(b)
        rhs.append(
            jnp.concatenate(
                [high[:, :lanes], high[:, lanes:], low[:, :lanes], low[:, lanes:]], axis=0
            )
        )
    return dot(yi, jnp.concatenate(rhs, axis=1)).astype(bf16)


def kron_halves(block):
    channels, _, lanes = block.shape
    wide = block.astype(f32).reshape(channels, 2, 8, lanes)
    return [wide[:, h].reshape(channels * 8, lanes).astype(bf16) for h in range(2)]


def row_pair(ref, y):
    return jnp.concatenate([ref[0, :, 0, y : y + 16, :], ref[0, :, 1, y : y + 16, :]], axis=2)


def whole_rows(value, at, lanes):
    size = value.shape[0] // 8
    two = [value[:, a : a + lanes].reshape(size, 8, lanes) for a in (at, at + lanes)]
    return jnp.concatenate(two, axis=1)


def put_rows(ref, y, value):
    value = value.astype(bf16)
    ref[0, :, 0, y : y + 16, :] = value[:, :, :NZ]
    ref[0, :, 1, y : y + 16, :] = value[:, :, NZ:]


def pick_rows(channels):
    row = lax.broadcasted_iota(jnp.int32, (channels * 8, channels), 0)
    col = lax.broadcasted_iota(jnp.int32, (channels * 8, channels), 1)
    return row // 8 == col


def same_cell(channels):
    size = channels * 8
    row = lax.broadcasted_iota(jnp.int32, (size, size), 0)
    col = lax.broadcasted_iota(jnp.int32, (size, size), 1)
    return row % 8 == col % 8


def kron_rows(point, turned):
    channels = point.shape[0]
    pick = jnp.where(pick_rows(channels), 1.0, 0.0).astype(bf16)
    nt = (((1,), (1,)), ((), ()))
    tn = (((1,), (0,)), ((), ()))
    left = lax.dot_general(pick, point, nt if turned else tn, preferred_element_type=f32)
    full = lax.dot_general(left.astype(bf16), pick, nt, preferred_element_type=f32)
    return jnp.where(same_cell(channels), full, 0.0).astype(bf16)


def field_kernel(ns, channels, me_ref, field, zf, yf, xfh, xfl, *rest):
    outs, r_scr = rest[:ns], rest[ns]
    step = pl.program_id(0)
    rows = field.shape[2]
    lanes = rows * 2 * MZ
    groups = []
    for i in range(FIELD_CB):
        groups += z_forward([field[0, i, x] for x in range(rows)], zf[...])
    spectra = y_forward(groups, yf[...])
    for i in range(FIELD_CB):
        put_channel(r_scr, step * FIELD_CB + i, channels, spectra[:, i * lanes : (i + 1) * lanes])

    @pl.when(step == pl.num_programs(0) - 1)
    def _():
        x_forward_out(me_ref[0], ns, channels, r_scr, xfh, xfl, outs)


def point_kernel(field, point, bias, out, kron):
    channels = field.shape[1]

    @pl.when(pl.program_id(0) == 0)
    def _():
        kron[...] = kron_rows(point[...], True)

    bias_rows = jnp.sum(jnp.where(pick_rows(channels), bias[...], 0.0), axis=1, keepdims=True) * GK
    bias_16 = jnp.concatenate([bias_rows.reshape(channels, 8, 1)] * 2, axis=1)

    halves = []
    for y in range(0, NY, 16):
        halves += kron_halves(row_pair(field, y))
    lanes = halves[0].shape[1]
    done = dot(kron[...], jnp.concatenate(halves, axis=1))
    for y in range(0, NY, 16):
        put_rows(out, y, whole_rows(done, y // 8 * lanes, lanes) * GK + bias_16)


def gelu_slope(v):
    n = v * v
    t = jnp.tanh(v * (n + GALPHA))
    d = v * (1.5 * n + 0.5 * GALPHA)
    return (1.0 + t) * (0.5 + (1.0 - t) * d)


def grad_kernel(ns, channels, me_ref, pre, cot, *rest):
    ins = rest[:ns]
    xih, xil, yi, zi, zf, yf, xfh, xfl = rest[ns : ns + 8]
    dpre = rest[ns + 8]
    outs = rest[ns + 9 : ns + 9 + ns]
    b_scr, r_scr = rest[ns + 9 + ns :]
    step = pl.program_id(0)
    rows = pre.shape[2]
    width = GROUP * 2 * MZ
    groups = rows // GROUP

    @pl.when(step == 0)
    def _():
        x_inverse_in(me_ref[0], ns, channels, ins, xih, xil, b_scr)

    lanes = rows * 2 * MZ
    blocks = range(b_scr.shape[0])
    wide = y_inverse(
        [get_channel(b_scr, step * GRAD_CB + i, channels, blocks) for i in range(GRAD_CB)], yi[...]
    )
    g_all = jnp.concatenate(
        [wide[:, g : g + width] for g in range(0, wide.shape[1], width)], axis=0
    )
    for j in range(GROUP // 2):
        v_all = dot(g_all, zi[j])
        for i in range(GRAD_CB):
            for g in range(groups):
                x = g * GROUP + 2 * j
                at = (i * groups + g) * NY
                v = v_all[at : at + NY]
                v = v + jnp.concatenate([pre[0, i, x], pre[0, i, x + 1]], axis=1).astype(f32)
                w = jnp.concatenate([cot[0, i, x], cot[0, i, x + 1]], axis=1).astype(f32)
                d = (w * gelu_slope(v)).astype(bf16)
                dpre[0, i, x] = d[:, :NZ]
                dpre[0, i, x + 1] = d[:, NZ:]
    done = []
    for i in range(GRAD_CB):
        done += z_forward([dpre[0, i, x] for x in range(rows)], zf[...])
    spectra = y_forward(done, yf[...])
    for i in range(GRAD_CB):
        put_channel(r_scr, step * GRAD_CB + i, channels, spectra[:, i * lanes : (i + 1) * lanes])

    @pl.when(step == pl.num_programs(0) - 1)
    def _():
        x_forward_out(me_ref[0], ns, channels, r_scr, xfh, xfl, outs)


def pair_kernel(field, dpre, out, acc):
    channels = field.shape[1]
    step = pl.program_id(0)

    @pl.when(step == 0)
    def _():
        acc[...] = jnp.zeros_like(acc)

    lefts, rights = [], []
    for y in range(0, NY, 16):
        lefts += kron_halves(row_pair(field, y))
        rights += kron_halves(row_pair(dpre, y))
    acc[...] += lax.dot_general(
        jnp.concatenate(lefts, axis=1),
        jnp.concatenate(rights, axis=1),
        (((1,), (1,)), ((), ())),
        preferred_element_type=f32,
    )

    @pl.when(step == pl.num_programs(0) - 1)
    def _():
        same = jnp.where(same_cell(channels), acc[...], 0.0)
        pick = jnp.where(pick_rows(channels), 1.0, 0.0)
        high = lax.Precision.HIGHEST
        left = jnp.dot(same, pick, precision=high, preferred_element_type=f32)
        out[...] = lax.dot_general(
            pick, left, (((0,), (0,)), ((), ())), precision=high, preferred_element_type=f32
        )


def back_kernel(ns, me_ref, dpre, point, *rest):
    ins = rest[:ns]
    xih, xil, yi, zi = rest[ns : ns + 4]
    out, b_scr, g_scr, kron = rest[ns + 4 :]
    channels = dpre.shape[1]
    step = pl.program_id(0)
    width = GROUP * 2 * MZ

    @pl.when(step == 0)
    def _():
        x_inverse_in(me_ref[0], ns, channels, ins, xih, xil, b_scr)
        kron[...] = kron_rows(point[...], False)

    per_group = GROUP // 2

    @pl.when(step % per_group == 0)
    def _():
        group = step // per_group
        turned = group + b_scr.shape[0] // 2
        wide = y_inverse(
            [get_channel(b_scr, c, channels, (group, turned)) for c in range(channels)], yi[...]
        )
        for c in range(channels):
            g_scr[c] = wide[:, c * width : (c + 1) * width]

    halves = []
    for y in range(0, NY, 16):
        halves += kron_halves(row_pair(dpre, y))
    lanes = halves[0].shape[1]
    point = dot(kron[...], jnp.concatenate(halves, axis=1))
    spec = dot(g_scr[...].reshape(channels * NY, width), zi[step % per_group])
    spec = spec.reshape(channels, NY, lanes)
    for y in range(0, NY, 16):
        put_rows(out, y, whole_rows(point, y // 8 * lanes, lanes) + spec[:, y : y + 16])


def mix_kernel(ns, adjoint, *refs):
    ins, weights, total, out = refs[:ns], refs[ns], refs[ns + 1], refs[ns + 2]
    channels = total.shape[1]
    u = ins[0][...]
    for k in range(1, ns):
        u = u + ins[k][...]
    total[...] = u
    half = total.shape[2] // 2
    if not adjoint:
        real = jnp.zeros((channels, half), f32)
        imag = jnp.zeros((channels, half), f32)
        for c in range(channels):
            a, b = total[0, pl.ds(c, 1), :half], total[0, pl.ds(c, 1), half:]
            wr, wi = weights[0, c, 0].astype(f32), weights[1, c, 0].astype(f32)
            real = real + (wr * a - wi * b)
            imag = imag + (wr * b + wi * a)
        out[0, :, :half] = real
        out[0, :, half:] = imag
    else:
        a, b = total[0, :, :half], total[0, :, half:]
        for c in range(channels):
            wr, wi = weights[0, c, 0].astype(f32), weights[1, c, 0].astype(f32)
            out[0, pl.ds(c, 1), :half] = jnp.sum(wr * a + wi * b, axis=0, keepdims=True)
            out[0, pl.ds(c, 1), half:] = jnp.sum(wr * b - wi * a, axis=0, keepdims=True)


def weight_kernel(weights, out, scr):
    _, kxs, kzs, channels, _ = weights.shape
    modes = kxs * kzs
    scr[:, :channels] = weights[...].astype(f32).reshape(modes * channels, channels)
    per = LANES // channels
    lane = lax.broadcasted_iota(jnp.int32, (modes, LANES), 1) // channels
    for c in range(0, channels, per):
        packed = scr[pl.ds(c, modes, stride=channels), :]
        for q in range(1, per):
            more = scr[pl.ds(c + q, modes, stride=channels), :]
            packed = jnp.where(lane == q, pltpu.roll(more, q * channels, 1), packed)
        turned = packed.T.astype(bf16)
        for q in range(per):
            out[0, c + q, 0] = turned[q * channels : (q + 1) * channels]


def outer_kernel(samples, *refs):
    us, gs, out, scr = refs[:samples], refs[samples : 2 * samples], refs[-2], refs[-1]
    channels = us[0].shape[1]
    modes = us[0].shape[2] // 2
    per = LANES // channels
    tn = (((0,), (0,)), ((), ()))

    def stack(refs):
        wide = jnp.concatenate([ref[0] for ref in refs], axis=1)
        return jnp.concatenate(parts(wide), axis=0)

    def table(lanes, of):
        row = lax.broadcasted_iota(jnp.int32, (2 * channels, lanes), 0) % channels
        col = lax.broadcasted_iota(jnp.int32, (2 * channels, lanes), 1)
        return jnp.where(row == of(col), 1.0, 0.0).astype(bf16)

    by_o = table(LANES, lambda col: col % channels)
    by_c = table(channels * channels, lambda col: col // channels)
    g_all = lax.dot_general(stack(gs), by_o, tn, preferred_element_type=f32)
    u_all = lax.dot_general(stack(us), by_c, tn, preferred_element_type=f32)
    for n in range(channels // per):
        real = imag = None
        for s in range(samples):
            at = 2 * s * modes
            gr, gi = g_all[at : at + modes], g_all[at + modes : at + 2 * modes]
            u = u_all[at : at + 2 * modes, n * LANES : (n + 1) * LANES]
            ur, ui = u[:modes], u[modes:]
            re, im = ur * gr + ui * gi, ur * gi - ui * gr
            real = re if real is None else real + re
            imag = im if imag is None else imag + im
        for p, value in enumerate((real, imag)):
            for q in range(per):
                one = value if q == 0 else pltpu.roll(value, LANES - q * channels, 1)
                scr[p, pl.ds(n * per + q, modes, stride=channels), :] = one
    out[...] = scr[:, :, :channels].reshape(out.shape)


def whole(shape):
    return pl.BlockSpec(shape, lambda *_: (0,) * len(shape))


def params(mib=60, axes=1):
    return pltpu.CompilerParams(
        dimension_semantics=("arbitrary",) * axes, vmem_limit_bytes=mib * 2**20
    )


def make_calls(ns, shape):
    _, channels, rows, _, _ = shape
    own_ky = MY // ns
    width = 2 * MX * MZ
    lanes = rows * 2 * MZ
    size = channels * 8

    zf = jnp.asarray(z_forward_table())
    zi = jnp.asarray(z_inverse_table())
    yf, yi = (jnp.asarray(t) for t in y_tables())
    xf = [jnp.asarray(t) for t in split_bf(x_forward_table())]
    xf_spec = [pl.BlockSpec((lanes, width), lambda i, at: (at[0], 0))] * 2
    xi_pre = [jnp.asarray(t) for t in split_bf(x_inverse_table(SCALE_INVERSE * GK, ns))]
    xi_back = [jnp.asarray(t) for t in split_bf(x_inverse_table(SCALE_INVERSE, ns))]
    xi_spec = [pl.BlockSpec((1, width, 2 * lanes), lambda i, at: (at[0], 0, 0))] * 2

    chunk = jax.ShapeDtypeStruct((own_ky, channels, width), f32)
    chunk_spec = whole(chunk.shape)

    def some_channels(count):
        return pl.BlockSpec((1, count, rows, NY, NZ), lambda c, *_: (0, c, 0, 0, 0))

    two_rows = pl.BlockSpec((1, channels, 2, NY, NZ), lambda x, *_: (0, 0, x, 0, 0))
    big = jax.ShapeDtypeStruct(shape, bf16)
    cells = channels * rows * NY * NZ
    r_scr = pltpu.VMEM((lanes // LANES, MY * channels, LANES), f32)
    b_scr = pltpu.VMEM((2 * lanes // LANES, MY * channels, LANES), f32)
    kron_scr = pltpu.VMEM((size, size), bf16)

    def cost(flops, moved):
        return pl.CostEstimate(flops=int(flops), bytes_accessed=int(moved), transcendentals=0)

    def tables(*arrays):
        return [whole(a.shape) for a in arrays]

    def field_call(me_arr, field):
        return pl.pallas_call(
            functools.partial(field_kernel, ns, channels),
            grid_spec=pltpu.PrefetchScalarGridSpec(
                num_scalar_prefetch=1,
                grid=(channels // FIELD_CB,),
                in_specs=[some_channels(FIELD_CB)] + tables(zf, yf) + xf_spec,
                out_specs=[chunk_spec] * ns,
                scratch_shapes=[r_scr],
            ),
            out_shape=[chunk] * ns,
            compiler_params=params(),
            cost_estimate=cost(cells * 512, cells * 2),
            name="field_spectrum",
        )(me_arr, field, zf, yf, *xf)

    def point_call(field, point_weight, bias):
        return pl.pallas_call(
            point_kernel,
            grid=(rows // 2,),
            in_specs=[two_rows] + tables(point_weight, bias[None]),
            out_specs=two_rows,
            out_shape=big,
            scratch_shapes=[kron_scr],
            compiler_params=params(),
            cost_estimate=cost(cells * 512, cells * 4),
            name="pointwise",
        )(field, point_weight, bias[None])

    def mix_call(adjoint, chunks, w):
        one_ky = pl.BlockSpec((1, channels, width), lambda k: (k, 0, 0))
        w_spec = pl.BlockSpec((2, channels, 1, channels, MX * MZ), lambda k: (0, 0, k, 0, 0))
        return pl.pallas_call(
            functools.partial(mix_kernel, ns, adjoint),
            grid=(own_ky,),
            in_specs=[one_ky] * ns + [w_spec],
            out_specs=[one_ky, one_ky],
            out_shape=[chunk, chunk],
            compiler_params=params(),
            name="mix_adjoint" if adjoint else "mix",
        )(*chunks, w)

    def grad_call(me_arr, pre, cotangent, chunks):
        return pl.pallas_call(
            functools.partial(grad_kernel, ns, channels),
            grid_spec=pltpu.PrefetchScalarGridSpec(
                num_scalar_prefetch=1,
                grid=(channels // GRAD_CB,),
                in_specs=[some_channels(GRAD_CB)] * 2
                + [chunk_spec] * ns
                + xi_spec
                + tables(yi, zi, zf, yf)
                + xf_spec,
                out_specs=[some_channels(GRAD_CB)] + [chunk_spec] * ns,
                scratch_shapes=[b_scr, r_scr],
            ),
            out_shape=[big] + [chunk] * ns,
            compiler_params=params(),
            cost_estimate=cost(cells * 1024, cells * 6),
            name="gelu_gradient",
        )(me_arr, pre, cotangent, *chunks, *xi_pre, yi, zi, zf, yf, *xf)

    def pair_call(field, dpre):
        return pl.pallas_call(
            pair_kernel,
            grid=(rows // 2,),
            in_specs=[two_rows, two_rows],
            out_specs=whole((channels, channels)),
            out_shape=jax.ShapeDtypeStruct((channels, channels), f32),
            scratch_shapes=[pltpu.VMEM((size, size), f32)],
            compiler_params=params(),
            cost_estimate=cost(cells * 512, cells * 4),
            name="point_gradient",
        )(field, dpre)

    def back_call(me_arr, dpre, point_weight, chunks):
        return pl.pallas_call(
            functools.partial(back_kernel, ns),
            grid_spec=pltpu.PrefetchScalarGridSpec(
                num_scalar_prefetch=1,
                grid=(rows // 2,),
                in_specs=[two_rows]
                + tables(point_weight)
                + [chunk_spec] * ns
                + xi_spec
                + tables(yi, zi),
                out_specs=two_rows,
                scratch_shapes=[b_scr, pltpu.VMEM((channels, NY, GROUP * 2 * MZ), bf16), kron_scr],
            ),
            out_shape=big,
            compiler_params=params(),
            cost_estimate=cost(cells * 1024, cells * 4),
            name="field_gradient",
        )(me_arr, dpre, point_weight, *chunks, *xi_back, yi, zi)

    modes = MX * MZ
    w_block = pl.BlockSpec((1, MX, MZ, channels, channels), lambda p, k: (p, 0, k, 0, 0))

    def weight_call(spec_weight):
        return pl.pallas_call(
            weight_kernel,
            grid=(2, own_ky),
            in_specs=[w_block],
            out_specs=pl.BlockSpec(
                (1, channels, 1, channels, modes), lambda p, k: (p, 0, k, 0, 0)
            ),
            out_shape=jax.ShapeDtypeStruct((2, channels, own_ky, channels, modes), bf16),
            scratch_shapes=[pltpu.VMEM((modes * channels, LANES), f32)],
            compiler_params=params(axes=2),
            cost_estimate=cost(0, 2 * own_ky * modes * channels * LANES * 2),
            name="weight_layout",
        )(spec_weight)

    def spec_call(us, gs):
        one_ky = pl.BlockSpec((1, channels, width), lambda k: (k, 0, 0))
        return pl.pallas_call(
            functools.partial(outer_kernel, len(us)),
            grid=(own_ky,),
            in_specs=[one_ky] * (2 * len(us)),
            out_specs=pl.BlockSpec((2, MX, MZ, channels, channels), lambda k: (0, 0, k, 0, 0)),
            out_shape=jax.ShapeDtypeStruct((2, MX, own_ky * MZ, channels, channels), f32),
            scratch_shapes=[pltpu.VMEM((2, modes * channels, LANES), f32)],
            compiler_params=params(),
            cost_estimate=cost(0, 2 * own_ky * modes * channels * LANES * 4),
            name="weight_gradient",
        )(*us, *gs)

    return {
        "field": field_call,
        "point": point_call,
        "mix": mix_call,
        "grad": grad_call,
        "pair": pair_call,
        "back": back_call,
        "weights": weight_call,
        "spec": spec_call,
    }


def fast_device(ns, nchan, field, cotangent, spec_weight, point_weight, bias):
    channels = field.shape[1]
    me = lax.axis_index("slab")
    me_arr = me[None].astype(jnp.int32)
    calls = make_calls(ns, field.shape)

    def swap(chunks, axis, size):
        got = [chunks[0]]
        for k in range(1, size):
            pairs = [(i, (i + k) % size) for i in range(size)]
            got.append(lax.ppermute(chunks[k], axis, pairs))
        return got

    field_chunks = calls["field"](me_arr, field)
    w = calls["weights"](spec_weight)
    pre = calls["point"](field, point_weight, bias)
    uhat, vhat = calls["mix"](False, swap(field_chunks, "slab", ns), w)
    vhats = swap([vhat] * ns, "slab", ns)
    dpre, *grad_chunks = calls["grad"](me_arr, pre, cotangent, vhats)
    u_all = swap([uhat] * nchan, "chan", nchan)

    point_part = calls["pair"](field, dpre)
    ghat, hhat = calls["mix"](True, swap(grad_chunks, "slab", ns), w)
    hhats = swap([hhat] * ns, "slab", ns)
    g_all = swap([ghat] * nchan, "chan", nchan)
    field_grad = calls["back"](me_arr, dpre, point_weight, hhats)

    spec_grad = calls["spec"](u_all, g_all)

    norm_scale = 1.0 / math.sqrt(nchan * NX * NY * NZ)
    dc = jnp.where(me == 0, ghat[0, :, 0], 0.0) * (1.0 / SCALE_FORWARD)
    tail = jnp.concatenate([point_part, dc[None, :]], axis=0)
    for axis, count in (("chan", nchan), ("slab", ns)):
        tail = sum(swap([tail] * count, axis, count))
    tail = tail * norm_scale
    return field_grad, spec_grad, tail[:channels], tail[channels]


def plain_device(field, cotangent, spec_weight, point_weight, bias):
    samples, channels, rows, _, _ = field.shape
    high = lax.Precision.HIGHEST

    def con(form, a, b):
        return jnp.einsum(form, a, b, precision=high)

    yc, ys = (jnp.asarray(t) for t in mode_table(NY, MY, True))
    zc, zs = (jnp.asarray(t) for t in mode_table(NZ, MZ, False))
    xc, xs = (jnp.asarray(t) for t in mode_table(NX, MX, True))
    y_table = jnp.concatenate([yc, ys], axis=1).astype(bf16)
    z_table = jnp.concatenate([zc, zs], axis=1)
    pairs = MY * MZ

    def to_spectrum(values):
        q = jnp.einsum("scxyz,yk->scxkz", values, y_table, preferred_element_type=f32)
        zr = con("scxkz,zj->scxkj", q[:, :, :, :MY], z_table)
        zm = con("scxkz,zj->scxkj", q[:, :, :, MY:], z_table)
        real = zr[..., :MZ] - zm[..., MZ:]
        imag = zr[..., MZ:] + zm[..., :MZ]
        local = jnp.stack([real, imag]).reshape(2, samples, channels, rows, pairs)
        a, b = lax.all_to_all(local, "slab", split_axis=4, concat_axis=3, tiled=True)
        real = con("scxk,xm->scmk", a, xc) - con("scxk,xm->scmk", b, xs)
        imag = con("scxk,xm->scmk", b, xc) + con("scxk,xm->scmk", a, xs)
        return real * SCALE_FORWARD, imag * SCALE_FORWARD

    def from_spectrum(a, b):
        real = con("scmk,xm->scxk", a, xc) + con("scmk,xm->scxk", b, xs)
        imag = con("scmk,xm->scxk", b, xc) - con("scmk,xm->scxk", a, xs)
        both = jnp.stack([real, imag])
        both = lax.all_to_all(both, "slab", split_axis=3, concat_axis=4, tiled=True)
        real, imag = both.reshape(2, samples, channels, rows, MY, MZ)
        fr = con("scxkj,zj->scxkz", real, zc) + con("scxkj,zj->scxkz", imag, zs)
        fi = con("scxkj,zj->scxkz", imag, zc) - con("scxkj,zj->scxkz", real, zs)
        f = jnp.concatenate([fr, fi], axis=3).astype(bf16)
        out = jnp.einsum("scxkz,yk->scxyz", f, y_table, preferred_element_type=f32)
        return out * SCALE_INVERSE

    wr, wi = spec_weight.astype(f32)
    ur, ui = to_spectrum(field)
    mix = functools.partial(con, "scmk,mkco->somk")
    spectral = from_spectrum(mix(ur, wr) - mix(ui, wi), mix(ui, wr) + mix(ur, wi))
    point = jnp.einsum("co,scxyz->soxyz", point_weight, field, preferred_element_type=f32)
    pre = (spectral + point + bias[None, :, None, None, None]) * GK
    dpre = (cotangent.astype(f32) * gelu_slope(pre)).astype(bf16)
    gr, gi = to_spectrum(dpre)
    mix = functools.partial(con, "somk,mkco->scmk")
    back = from_spectrum(mix(gr, wr) + mix(gi, wi), mix(gi, wr) - mix(gr, wi))
    point = jnp.einsum("co,soxyz->scxyz", point_weight, dpre, preferred_element_type=f32)
    field_grad = (back + point).astype(bf16)
    outer = functools.partial(con, "scmk,somk->mkco")
    dw = jnp.stack([outer(ur, gr) + outer(ui, gi), outer(ur, gi) - outer(ui, gr)])
    spec_grad = lax.psum(dw, "chan")
    point_part = jnp.einsum("scxyz,soxyz->co", field, dpre, preferred_element_type=f32)
    bias_part = jnp.sum(dpre.astype(f32), axis=(0, 2, 3, 4))
    point_part, bias_part = lax.psum((point_part, bias_part), ("slab", "chan"))
    scale = 1.0 / math.sqrt(samples * lax.axis_size("chan") * NX * NY * NZ)
    return field_grad, spec_grad, point_part * scale, bias_part * scale


def solution(mesh):
    ns, nchan = mesh.shape["slab"], mesh.shape["chan"]

    def per_device(field, *rest):
        samples, _, rows, _, _ = field.shape
        if MY % ns == 0 and rows % (2 * GROUP) == 0 and samples == 1:
            return fast_device(ns, nchan, field, *rest)
        return plain_device(field, *rest)

    return jax.shard_map(
        per_device,
        mesh=mesh,
        in_specs=(
            P(("groups", "chan"), None, "slab", None, None),
            P(("groups", "chan"), None, "slab", None, None),
            P(None, None, "slab", None, None),
            P(),
            P(),
        ),
        out_specs=(
            P(("groups", "chan"), None, "slab", None, None),
            P("groups", None, "slab", None, None),
            P("groups", None),
            P("groups"),
        ),
        check_vma=False,
    )
```

time: 1200 us -> 267 us (0.22)
  matrix products: 690 us -> 0 us
  Pallas kernels: 0 us -> 219 us
  local copies, waits for them, and re-layouts: 151 us -> 5.88 us
  waiting for transfers between devices: 155 us -> 14.3 us
  blocking collectives: 91.6 us -> 0 us
  other arithmetic: 77.9 us -> 2.29 us
  between operations: 15 us -> 0.84 us
    dot_general x35 -> x0, matrix products: 690 us -> none  [the longest x28 393 us: contract(): return jnp.einsum(form, left, right, precision=highest)]
    pallas_call x0 -> x9, Pallas kernels: none -> 219 us  [the longest x1 60.7 us: grad_call(): pl.pallas_call(functools.partial(grad_kernel, ns, channels), grid_spec=pl...]
    psum x1 -> x0, waiting for transfers between devices: 147 us -> none  [per_device(): spec_grad = lax.psum(jnp.stack([dw_real, dw_imag]), 'chan')]
    psum x1 -> x0, blocking collectives: 59.7 us -> none  [per_device(): lax.psum((point_part, bias_part), ('slab', 'chan'))]
    unnamed x60 -> x38, local copies, waits for them, and re-layouts: 45.5 us -> 4.76 us
    slice x12 -> x1, local copies, waits for them, and re-layouts: 34.9 us -> 0.61 us  [fast_device(): return (field_grad, spec_grad, tail[:channels], tail[channels])]
    another operation x12 -> x0, local copies, waits for them, and re-layouts: 32.4 us -> none
    all_to_all x1 -> x0, blocking collectives: 31.8 us -> none  [to_spectrum(): lax.all_to_all(local_spec, 'slab', split_axis=4, concat_axis=3, tiled=True)]
  transfers between devices with their start and end apart: 4 -> 24, of which waited for: 2 -> 6; matrix products, arithmetic and copies ran while one was open for 24% -> 0% of each run, Pallas kernels for 0% -> 41%
where the time goes in v1:
time: 267 us; the launch traced here: 266 us
  Pallas kernels  219 us (82%)
  starting transfers between devices  24.2 us (9%)
  waiting for transfers between devices  14.3 us (5%)
  local copies, waits for them, and re-layouts  5.88 us (2%)
    pallas_call x1, Pallas kernels, grad_call(): pl.pallas_call(functools.partial(grad_kernel, ns, channels), grid_spec=pl...  60.7 us
    pallas_call x1, Pallas kernels, back_call(): pl.pallas_call(functools.partial(back_kernel, ns), grid_spec=pltpu.Prefet...  35.3 us
    pallas_call x1, Pallas kernels, point_call(): pl.pallas_call(point_kernel, grid=(rows // 2,), in_specs=[two_rows] + tab...  32.5 us
    pallas_call x1, Pallas kernels, pair_call(): pl.pallas_call(pair_kernel, grid=(rows // 2,), in_specs=[two_rows, two_ro...  28 us
    ppermute x24, starting transfers between devices, swap(): got.append(lax.ppermute(chunks[k], axis, pairs))  24.2 us
    pallas_call x1, Pallas kernels, spec_call(): pl.pallas_call(functools.partial(outer_kernel, len(us)), grid=(own_ky,),...  21.7 us
    pallas_call x1, Pallas kernels, field_call(): pl.pallas_call(functools.partial(field_kernel, ns, channels), grid_spec=p...  18.5 us
    ppermute x24, waiting for transfers between devices, swap(): got.append(lax.ppermute(chunks[k], axis, pairs))  14.3 us
  transfers between devices with their start and end apart: 24, of which 6 were waited for; matrix products, arithmetic and copies ran while one was open for 0% of the time, Pallas kernels for 41%

profile of v1, /device:TPU:0, one launch (start us, length us, event | category | flops | bytes accessed | tf_op | source)
XLA Modules:
  0.0 266.1 jit_solution(14098229660499835461)
XLA Ops:
  0.6 18.5 %field_spectrum.1 = (f32[4,32,256]{2,1,0:T(8,128)}, f32[4,32,256]{2,1,0:T(8,128)}, f32[4,32,256]{2,1,0:T(8,128)}, f32[4,32,256]{2,1,0:T(8,128)}) custom-call(s32[1]{0:T(128)} %bitcast.me_ref, bf16[1,32,32,128,128]{4,3,2,1,0:T(8,128)(2,1)} %field.5, bf16[1024,128]{1,0:T(8,128)(2,1)} %constant.33.clone.zf.rest_8_, bf16[32,128]{1,0:T(8,128)(2,1)} %constant.35.clone.yf.rest_9_, ...), custom_call_target="tpu_custom_call" | custom-call | flops 8589934592 | bytes 33554432 | tf_op jit(solution)/shard_map/field_spectrum/pallas_call | solution.py:520
  19.1 3.0 %collective-permute-start = (f32[4,32,256]{2,1,0:T(8,128)}, f32[4,32,256]{2,1,0:T(8,128)S(1)}, u32[]{:S(2)}, u32[]{:S(2)}) collective-permute-start(f32[4,32,256]{2,1,0:T(8,128)} %get-tuple-element.18), channel_id=1, source_target_pairs={{0,4},{4,8},{8,12},{12,0},{1,5},{5,9},{9,13},{13,1},{2,6},{6,10},{... | collective-permute-start | bytes 393224 | tf_op jit(solution)/shard_map/ppermute | solution.py:668
  22.2 2.6 collective-permute-start.1
  24.7 1.3 collective-permute-start.2
  26.1 14.0 %weight_layout.1.refs_4_ = bf16[2,32,4,32,128]{4,3,2,1,0:T(8,128)(2,1)} custom-call(bf16[2,16,32,32,32]{4,3,2,1,0:T(8,128)(2,1)} %weights.1), custom_call_target="tpu_custom_call" | custom-call | bytes 8388608 | tf_op jit(solution)/shard_map/weight_layout/pallas_call | solution.py:618
  40.1 0.6 copy-done.14
  40.7 0.1 copy-done.18
  40.8 3.9 %mix.1 = (f32[4,32,256]{2,1,0:T(8,128)}, f32[4,32,256]{2,1,0:T(8,128)}) custom-call(f32[4,32,256]{2,1,0:T(8,128)} %get-tuple-element.17.refs_0_, f32[4,32,256]{2,1,0:T(8,128)} %copy-done.14, f32[4,32,256]{2,1,0:T(8,128)} %copy-done.16, f32[4,32,256]{2,1,0:T(8,128)} %copy-done.18, bf16[2,32,4,32,128]{4,3,2,1,0:T(8,128)(2,1)} %weight_layout.1.refs_4_), custom_call_target="tpu_custom_call" | custom-call | tf_op jit(solution)/shard_map/mix/pallas_call | solution.py:551
  44.7 0.4 collective-permute-start.5
  45.1 1.7 collective-permute-start.4
  46.9 32.5 %pointwise.1.pre = bf16[1,32,32,128,128]{4,3,2,1,0:T(8,128)(2,1)} custom-call(bf16[1,32,32,128,128]{4,3,2,1,0:T(8,128)(2,1)} %field.5, bf16[32,32]{1,0:T(8,128)(2,1)} %point.3, f32[1,32]{1,0:T(1,128)} %bitcast.7), custom_call_target="tpu_custom_call" | custom-call | flops 8589934592 | bytes 67108864 | tf_op jit(solution)/shard_map/pointwise/pallas_call | solution.py:536
  79.4 0.6 copy-done.10
  80.1 0.1 copy-done.11
  80.1 0.7 copy-done.12
  80.8 60.7 %gelu_gradient.1 = (bf16[1,32,32,128,128]{4,3,2,1,0:T(8,128)(2,1)}, f32[4,32,256]{2,1,0:T(8,128)}, f32[4,32,256]{2,1,0:T(8,128)}, f32[4,32,256]{2,1,0:T(8,128)}, f32[4,32,256]{2,1,0:T(8,128)}) custom-call(s32[1]{0:T(128)} %bitcast.me_ref, bf16[1,32,32,128,128]{4,3,2,1,0:T(8,128)(2,1)} %pointwise.1.pre, bf16[1,32,32,128,128]{4,3,2,1,0:T(8,128)(2,1)} %cot.1, ...), custom_call_target="tpu_custom_call" | custom-call | flops 17179869184 | bytes 100663296 | tf_op jit(solution)/shard_map/gelu_gradient/pallas_call | solution.py:562
  141.5 1.8 collective-permute-start.6
  143.3 2.6 collective-permute-start.7
  145.9 1.4 collective-permute-start.8
  147.2 28.0 %point_gradient.1 = f32[32,32]{1,0:T(8,128)} custom-call(bf16[1,32,32,128,128]{4,3,2,1,0:T(8,128)(2,1)} %field.5, bf16[1,32,32,128,128]{4,3,2,1,0:T(8,128)(2,1)} %get-tuple-element.22.dpre), custom_call_target="tpu_custom_call" | custom-call | flops 8589934592 | bytes 67108864 | tf_op jit(solution)/shard_map/point_gradient/pallas_call | solution.py:582
  175.3 0.6 copy-done.13
  175.9 0.0 copy-done.15
  176.0 4.0 %mix_adjoint.1 = (f32[4,32,256]{2,1,0:T(8,128)}, f32[4,32,256]{2,1,0:T(8,128)}) custom-call(f32[4,32,256]{2,1,0:T(8,128)} %get-tuple-element.23.refs_0_, f32[4,32,256]{2,1,0:T(8,128)} %copy-done.13, f32[4,32,256]{2,1,0:T(8,128)} %copy-done.15, f32[4,32,256]{2,1,0:T(8,128)} %copy-done.17, bf16[2,32,4,32,128]{4,3,2,1,0:T(8,128)(2,1)} %weight_layout.1.refs_4_), custom_call_target="tpu_custom_call" | custom-call | tf_op jit(solution)/shard_map/mix_adjoint/pallas_call | solution.py:551
  180.0 0.8 multiply_reduce_fusion
  180.8 0.7 pad_maximum_fusion
  181.5 1.5 collective-permute-start.19
  183.0 0.5 collective-permute-start.18
  183.5 1.8 collective-permute-done.19
  185.3 0.9 collective-permute-done.18
  186.2 0.7 add_add_fusion
  187.0 0.5 collective-permute-start.23
  187.4 1.7 collective-permute-start.22
  189.1 0.2 collective-permute-start.21
  189.3 0.6 collective-permute-start.13
  190.0 0.8 collective-permute-done.23
  190.7 3.0 %collective-permute-start.11 = (f32[4,32,256]{2,1,0:T(8,128)}, f32[4,32,256]{2,1,0:T(8,128)S(1)}, u32[]{:S(2)}, u32[]{:S(2)}) collective-permute-start(f32[4,32,256]{2,1,0:T(8,128)} %get-tuple-element.27.rest_0_), channel_id=1, source_target_pairs={{0,12},{4,0},{8,4},{12,8},{1,13},{5,1},{9,5},{13,9},{2,14},{6,2},{... | collective-permute-start | bytes 393224 | tf_op jit(solution)/shard_map/ppermute | solution.py:668
  193.7 0.1 collective-permute-start.10
  193.8 1.1 collective-permute-done.21
  194.9 0.6 slice.12
  195.5 0.5 slice_bitcast_fusion
  196.0 1.9 collective-permute-done.11.rest_3_
  198.0 7.8 %collective-permute-done.10.rest_2_ = f32[4,32,256]{2,1,0:T(8,128)S(1)} collective-permute-done((f32[4,32,256]{2,1,0:T(8,128)}, f32[4,32,256]{2,1,0:T(8,128)S(1)}, u32[]{:S(2)}, u32[]{:S(2)}) %collective-permute-start.10) | collective-permute-done | bytes 131104 | tf_op jit(solution)/shard_map/ppermute | solution.py:668
  205.7 1.3 collective-permute-start.16
  207.0 0.6 copy-done.6
  207.7 35.3 %field_gradient.1 = bf16[1,32,32,128,128]{4,3,2,1,0:T(8,128)(2,1)} custom-call(s32[1]{0:T(128)} %bitcast.me_ref, bf16[1,32,32,128,128]{4,3,2,1,0:T(8,128)(2,1)} %get-tuple-element.22.dpre, bf16[32,32]{1,0:T(8,128)(2,1)} %point.3, f32[4,32,256]{2,1,0:T(8,128)} %get-tuple-element.27.rest_0_, f32[4,32,256]{2,1,0:T(8,128)} %copy-done.6, ...), custom_call_target="tpu_custom_call" | custom-call | flops 17179869184 | bytes 67108864 | tf_op jit(solution)/shard_map/field_gradient/pallas_call | solution.py:595
  243.0 0.6 copy-done.2
  243.7 0.1 copy-done.7
  243.8 0.7 copy-done.9
  244.4 21.7 %weight_gradient.1 = f32[2,16,32,32,32]{4,3,2,1,0:T(8,128)} custom-call(f32[4,32,256]{2,1,0:T(8,128)} %get-tuple-element.28.refs_0_, f32[4,32,256]{2,1,0:T(8,128)} %copy-done.5, f32[4,32,256]{2,1,0:T(8,128)} %copy-done.2, f32[4,32,256]{2,1,0:T(8,128)} %copy-done.1, f32[4,32,256]{2,1,0:T(8,128)} %get-tuple-element.29.refs_4_, f32[4,32,256]{2,1,0:T(8,128)} %copy-done.9, ...), custom_call_target="tpu_custom_call" | custom-call | bytes 16777216 | tf_op jit(solution)/shard_map/weight_gradient/pallas_call | solution.py:634
  (53 shorter events, 0.3 us)
Async XLA Ops:
  19.1 20.9 %collective-permute-start = (f32[4,32,256]{2,1,0:T(8,128)}, f32[4,32,256]{2,1,0:T(8,128)S(1)}, u32[]{:S(2)}, u32[]{:S(2)}) collective-permute-start(f32[4,32,256]{2,1,0:T(8,128)} %get-tuple-element.18), channel_id=1, source_target_pairs={{0,4},{4,8},{8,12},{12,0},{1,5},{5,9},{9,13},{13,1},{2,6},{6,10},{... | collective-permute-start | bytes 393224 | tf_op jit(solution)/shard_map/ppermute | solution.py:668
  22.2 17.9 %collective-permute-start.1 = (f32[4,32,256]{2,1,0:T(8,128)}, f32[4,32,256]{2,1,0:T(8,128)S(1)}, u32[]{:S(2)}, u32[]{:S(2)}) collective-permute-start(f32[4,32,256]{2,1,0:T(8,128)} %get-tuple-element.19), channel_id=1, source_target_pairs={{0,8},{4,12},{8,0},{12,4},{1,9},{5,13},{9,1},{13,5},{2,10},{6,14},... | collective-permute-start | bytes 393224 | tf_op jit(solution)/shard_map/ppermute | solution.py:668
  24.7 15.3 %collective-permute-start.2 = (f32[4,32,256]{2,1,0:T(8,128)}, f32[4,32,256]{2,1,0:T(8,128)S(1)}, u32[]{:S(2)}, u32[]{:S(2)}) collective-permute-start(f32[4,32,256]{2,1,0:T(8,128)} %get-tuple-element.20), channel_id=1, source_target_pairs={{0,12},{4,0},{8,4},{12,8},{1,13},{5,1},{9,5},{13,9},{2,14},{6,2},{... | collective-permute-start | bytes 393224 | tf_op jit(solution)/shard_map/ppermute | solution.py:668
  40.1 0.7 copy-start.14
  40.1 0.7 copy-start.16
  40.1 0.7 copy-start.18
  44.7 34.7 %collective-permute-start.5 = (f32[4,32,256]{2,1,0:T(8,128)}, f32[4,32,256]{2,1,0:T(8,128)S(1)}, u32[]{:S(2)}, u32[]{:S(2)}) collective-permute-start(f32[4,32,256]{2,1,0:T(8,128)} %get-tuple-element.21.rest_0_), channel_id=1, source_target_pairs={{0,12},{4,0},{8,4},{12,8},{1,13},{5,1},{9,5},{13,9},{2,14},{6,2},{... | collective-permute-start | bytes 393224 | tf_op jit(solution)/shard_map/ppermute | solution.py:668
  45.1 34.3 %collective-permute-start.4 = (f32[4,32,256]{2,1,0:T(8,128)}, f32[4,32,256]{2,1,0:T(8,128)S(1)}, u32[]{:S(2)}, u32[]{:S(2)}) collective-permute-start(f32[4,32,256]{2,1,0:T(8,128)} %get-tuple-element.21.rest_0_), channel_id=1, source_target_pairs={{0,8},{4,12},{8,0},{12,4},{1,9},{5,13},{9,1},{13,5},{2,10},{6,14},... | collective-permute-start | bytes 393224 | tf_op jit(solution)/shard_map/ppermute | solution.py:668
  46.8 32.6 %collective-permute-start.3 = (f32[4,32,256]{2,1,0:T(8,128)}, f32[4,32,256]{2,1,0:T(8,128)S(1)}, u32[]{:S(2)}, u32[]{:S(2)}) collective-permute-start(f32[4,32,256]{2,1,0:T(8,128)} %get-tuple-element.21.rest_0_), channel_id=1, source_target_pairs={{0,4},{4,8},{8,12},{12,0},{1,5},{5,9},{9,13},{13,1},{2,6},{6,10},{... | collective-permute-start | bytes 393224 | tf_op jit(solution)/shard_map/ppermute | solution.py:668
  79.4 0.6 copy-start.10
  79.4 0.7 copy-start.11
  80.1 0.7 copy-start.12
  141.5 33.8 %collective-permute-start.6 = (f32[4,32,256]{2,1,0:T(8,128)}, f32[4,32,256]{2,1,0:T(8,128)S(1)}, u32[]{:S(2)}, u32[]{:S(2)}) collective-permute-start(f32[4,32,256]{2,1,0:T(8,128)} %get-tuple-element.24), channel_id=1, source_target_pairs={{0,4},{4,8},{8,12},{12,0},{1,5},{5,9},{9,13},{13,1},{2,6},{6,10},{... | collective-permute-start | bytes 393224 | tf_op jit(solution)/shard_map/ppermute | solution.py:668
  143.3 32.0 %collective-permute-start.7 = (f32[4,32,256]{2,1,0:T(8,128)}, f32[4,32,256]{2,1,0:T(8,128)S(1)}, u32[]{:S(2)}, u32[]{:S(2)}) collective-permute-start(f32[4,32,256]{2,1,0:T(8,128)} %get-tuple-element.25), channel_id=1, source_target_pairs={{0,8},{4,12},{8,0},{12,4},{1,9},{5,13},{9,1},{13,5},{2,10},{6,14},... | collective-permute-start | bytes 393224 | tf_op jit(solution)/shard_map/ppermute | solution.py:668
  145.9 29.4 %collective-permute-start.8 = (f32[4,32,256]{2,1,0:T(8,128)}, f32[4,32,256]{2,1,0:T(8,128)S(1)}, u32[]{:S(2)}, u32[]{:S(2)}) collective-permute-start(f32[4,32,256]{2,1,0:T(8,128)} %get-tuple-element.26), channel_id=1, source_target_pairs={{0,12},{4,0},{8,4},{12,8},{1,13},{5,1},{9,5},{13,9},{2,14},{6,2},{... | collective-permute-start | bytes 393224 | tf_op jit(solution)/shard_map/ppermute | solution.py:668
  147.2 42.1 %copy-start = (f32[4,32,256]{2,1,0:T(8,128)S(1)}, f32[4,32,256]{2,1,0:T(8,128)}, u32[]{:S(2)}) copy-start(f32[4,32,256]{2,1,0:T(8,128)} %get-tuple-element.28.refs_0_) | copy-start | bytes 393220
  175.3 0.7 copy-start.13
  175.3 0.7 copy-start.15
  175.3 0.7 copy-start.17
  181.5 3.8 %collective-permute-start.19 = (f32[33,32]{1,0:T(8,128)S(1)}, f32[33,32]{1,0:T(8,128)S(1)}, u32[]{:S(2)}, u32[]{:S(2)}) collective-permute-start(f32[33,32]{1,0:T(8,128)S(1)} %pad_maximum_fusion), channel_id=1, source_target_pairs={{0,2},{1,3},{2,0},{3,1},{4,6},{5,7},{6,4},{7,5},{8,10},{9,11},{10,... | collective-permute-start | bytes 12680 | tf_op jit(solution)/shard_map/ppermute | solution.py:668
  183.0 2.3 collective-permute-start.20
  183.0 3.2 %collective-permute-start.18 = (f32[33,32]{1,0:T(8,128)S(1)}, f32[33,32]{1,0:T(8,128)S(1)}, u32[]{:S(2)}, u32[]{:S(2)}) collective-permute-start(f32[33,32]{1,0:T(8,128)S(1)} %pad_maximum_fusion), channel_id=1, source_target_pairs={{0,1},{1,2},{2,3},{3,0},{4,5},{5,6},{6,7},{7,4},{8,9},{9,10},{10,1... | collective-permute-start | bytes 12680 | tf_op jit(solution)/shard_map/ppermute | solution.py:668
  187.0 3.8 %collective-permute-start.23 = (f32[33,32]{1,0:T(8,128)S(1)}, f32[33,32]{1,0:T(8,128)S(1)}, u32[]{:S(2)}, u32[]{:S(2)}) collective-permute-start(f32[33,32]{1,0:T(8,128)S(1)} %add_add_fusion), channel_id=1, source_target_pairs={{0,12},{4,0},{8,4},{12,8},{1,13},{5,1},{9,5},{13,9},{2,14},{6,2},{... | collective-permute-start | bytes 12680 | tf_op jit(solution)/shard_map/ppermute | solution.py:668
  187.4 6.3 %collective-permute-start.22 = (f32[33,32]{1,0:T(8,128)S(1)}, f32[33,32]{1,0:T(8,128)S(1)}, u32[]{:S(2)}, u32[]{:S(2)}) collective-permute-start(f32[33,32]{1,0:T(8,128)S(1)} %add_add_fusion), channel_id=1, source_target_pairs={{0,8},{4,12},{8,0},{12,4},{1,9},{5,13},{9,1},{13,5},{2,10},{6,14},... | collective-permute-start | bytes 12680 | tf_op jit(solution)/shard_map/ppermute | solution.py:668
  189.1 5.8 %collective-permute-start.21 = (f32[33,32]{1,0:T(8,128)S(1)}, f32[33,32]{1,0:T(8,128)S(1)}, u32[]{:S(2)}, u32[]{:S(2)}) collective-permute-start(f32[33,32]{1,0:T(8,128)S(1)} %add_add_fusion), channel_id=1, source_target_pairs={{0,4},{4,8},{8,12},{12,0},{1,5},{5,9},{9,13},{13,1},{2,6},{6,10},{... | collective-permute-start | bytes 12680 | tf_op jit(solution)/shard_map/ppermute | solution.py:668
  189.3 6.7 %collective-permute-start.14 = (f32[4,32,256]{2,1,0:T(8,128)S(1)}, f32[4,32,256]{2,1,0:T(8,128)S(1)}, u32[]{:S(2)}, u32[]{:S(2)}) collective-permute-start(f32[4,32,256]{2,1,0:T(8,128)S(1)} %copy-done), channel_id=1, source_target_pairs={{0,3},{1,0},{2,1},{3,2},{4,7},{5,4},{6,5},{7,6},{8,11},{9,8},{10,9... | collective-permute-start | bytes 393224 | tf_op jit(solution)/shard_map/ppermute | solution.py:668
  189.3 53.6 %collective-permute-start.13 = (f32[4,32,256]{2,1,0:T(8,128)S(1)}, f32[4,32,256]{2,1,0:T(8,128)S(1)}, u32[]{:S(2)}, u32[]{:S(2)}) collective-permute-start(f32[4,32,256]{2,1,0:T(8,128)S(1)} %copy-done), channel_id=1, source_target_pairs={{0,2},{1,3},{2,0},{3,1},{4,6},{5,7},{6,4},{7,5},{8,10},{9,11},{10,... | collective-permute-start | bytes 393224 | tf_op jit(solution)/shard_map/ppermute | solution.py:668
  190.7 7.2 %collective-permute-start.11 = (f32[4,32,256]{2,1,0:T(8,128)}, f32[4,32,256]{2,1,0:T(8,128)S(1)}, u32[]{:S(2)}, u32[]{:S(2)}) collective-permute-start(f32[4,32,256]{2,1,0:T(8,128)} %get-tuple-element.27.rest_0_), channel_id=1, source_target_pairs={{0,12},{4,0},{8,4},{12,8},{1,13},{5,1},{9,5},{13,9},{2,14},{6,2},{... | collective-permute-start | bytes 393224 | tf_op jit(solution)/shard_map/ppermute | solution.py:668
  193.7 12.0 %collective-permute-start.10 = (f32[4,32,256]{2,1,0:T(8,128)}, f32[4,32,256]{2,1,0:T(8,128)S(1)}, u32[]{:S(2)}, u32[]{:S(2)}) collective-permute-start(f32[4,32,256]{2,1,0:T(8,128)} %get-tuple-element.27.rest_0_), channel_id=1, source_target_pairs={{0,8},{4,12},{8,0},{12,4},{1,9},{5,13},{9,1},{13,5},{2,10},{6,14},... | collective-permute-start | bytes 393224 | tf_op jit(solution)/shard_map/ppermute | solution.py:668
  194.9 12.1 %collective-permute-start.9 = (f32[4,32,256]{2,1,0:T(8,128)}, f32[4,32,256]{2,1,0:T(8,128)S(1)}, u32[]{:S(2)}, u32[]{:S(2)}) collective-permute-start(f32[4,32,256]{2,1,0:T(8,128)} %get-tuple-element.27.rest_0_), channel_id=1, source_target_pairs={{0,4},{4,8},{8,12},{12,0},{1,5},{5,9},{9,13},{13,1},{2,6},{6,10},{... | collective-permute-start | bytes 393224 | tf_op jit(solution)/shard_map/ppermute | solution.py:668
  196.0 46.9 %copy-start.1 = (f32[4,32,256]{2,1,0:T(8,128)}, f32[4,32,256]{2,1,0:T(8,128)S(1)}, u32[]{:S(2)}) copy-start(f32[4,32,256]{2,1,0:T(8,128)S(1)} %collective-permute-done.14.refs_3_) | copy-start | bytes 393220
  196.0 46.9 %collective-permute-start.12 = (f32[4,32,256]{2,1,0:T(8,128)S(1)}, f32[4,32,256]{2,1,0:T(8,128)S(1)}, u32[]{:S(2)}, u32[]{:S(2)}) collective-permute-start(f32[4,32,256]{2,1,0:T(8,128)S(1)} %copy-done), channel_id=1, source_target_pairs={{0,1},{1,2},{2,3},{3,0},{4,5},{5,6},{6,7},{7,4},{8,9},{9,10},{10,1... | collective-permute-start | bytes 393224 | tf_op jit(solution)/shard_map/ppermute | solution.py:668
  198.0 9.1 %copy-start.3 = (f32[4,32,256]{2,1,0:T(8,128)}, f32[4,32,256]{2,1,0:T(8,128)S(1)}, u32[]{:S(2)}) copy-start(f32[4,32,256]{2,1,0:T(8,128)S(1)} %collective-permute-done.11.rest_3_) | copy-start | bytes 393220
  198.0 45.0 %collective-permute-start.17 = (f32[4,32,256]{2,1,0:T(8,128)}, f32[4,32,256]{2,1,0:T(8,128)S(1)}, u32[]{:S(2)}, u32[]{:S(2)}) collective-permute-start(f32[4,32,256]{2,1,0:T(8,128)} %get-tuple-element.29.refs_4_), channel_id=1, source_target_pairs={{0,3},{1,0},{2,1},{3,2},{4,7},{5,4},{6,5},{7,6},{8,11},{9,8},{10,9... | collective-permute-start | bytes 393224 | tf_op jit(solution)/shard_map/ppermute | solution.py:668
  205.7 1.3 copy-start.4
  205.7 37.3 %collective-permute-start.16 = (f32[4,32,256]{2,1,0:T(8,128)}, f32[4,32,256]{2,1,0:T(8,128)S(1)}, u32[]{:S(2)}, u32[]{:S(2)}) collective-permute-start(f32[4,32,256]{2,1,0:T(8,128)} %get-tuple-element.29.refs_4_), channel_id=1, source_target_pairs={{0,2},{1,3},{2,0},{3,1},{4,6},{5,7},{6,4},{7,5},{8,10},{9,11},{10,... | collective-permute-start | bytes 393224 | tf_op jit(solution)/shard_map/ppermute | solution.py:668
  207.0 0.7 copy-start.6
  207.0 36.0 %collective-permute-start.15 = (f32[4,32,256]{2,1,0:T(8,128)}, f32[4,32,256]{2,1,0:T(8,128)S(1)}, u32[]{:S(2)}, u32[]{:S(2)}) collective-permute-start(f32[4,32,256]{2,1,0:T(8,128)} %get-tuple-element.29.refs_4_), channel_id=1, source_target_pairs={{0,1},{1,2},{2,3},{3,0},{4,5},{5,6},{6,7},{7,4},{8,9},{9,10},{10,1... | collective-permute-start | bytes 393224 | tf_op jit(solution)/shard_map/ppermute | solution.py:668
  243.0 0.7 copy-start.2
  243.0 0.7 copy-start.5
  243.0 0.7 copy-start.7
  243.0 0.7 copy-start.8
  243.8 0.7 copy-start.9

commit v2 on v1

--- a/solution.py
+++ b/solution.py
@@ -19,7 +19,9 @@
 GROUP = 8
 
 FIELD_CB = 4
-GRAD_CB = 2
+PAD = 8
+ROWS = 4
+GRAD_CB = 4
 
 f32 = jnp.float32
 bf16 = jnp.bfloat16
@@ -28,6 +30,7 @@
 GB = 0.044715
 GK = (GA * GB) ** (1.0 / 3.0)
 GALPHA = GA / GK
+SLOPE = 1.5
 
 SCALE_FORWARD = 1.0 / math.sqrt(NX * NY * NZ)
 SCALE_INVERSE = 1.0 / math.sqrt(MX * MY * MZ)
@@ -75,7 +78,7 @@
     return bf(forward), bf(inverse)
 
 
-def x_forward_table():
+def x_forward_table(scale):
     xc, xs = mode_table(NX, MX, True)
     table = np.zeros((NX, 2, MZ, 2, MX, MZ), np.float32)
     for kz in range(MZ):
@@ -83,7 +86,7 @@
         table[:, 1, kz, 0, :, kz] = -xs
         table[:, 0, kz, 1, :, kz] = xs
         table[:, 1, kz, 1, :, kz] = xc
-    return table.reshape(NX * 2 * MZ, 2 * MX * MZ) * SCALE_FORWARD
+    return table.reshape(NX * 2 * MZ, 2 * MX * MZ) * (scale * SCALE_FORWARD)
 
 
 def x_inverse_table(scale, ns):
@@ -197,8 +200,8 @@
     return [wide[:, h].reshape(channels * 8, lanes).astype(bf16) for h in range(2)]
 
 
-def row_pair(ref, y):
-    return jnp.concatenate([ref[0, :, 0, y : y + 16, :], ref[0, :, 1, y : y + 16, :]], axis=2)
+def row_pair(ref, x, y):
+    return jnp.concatenate([ref[0, :, x + i, y : y + 16, :] for i in range(2)], axis=2)
 
 
 def whole_rows(value, at, lanes):
@@ -207,10 +210,10 @@
     return jnp.concatenate(two, axis=1)
 
 
-def put_rows(ref, y, value):
+def put_rows(ref, x, y, value):
     value = value.astype(bf16)
-    ref[0, :, 0, y : y + 16, :] = value[:, :, :NZ]
-    ref[0, :, 1, y : y + 16, :] = value[:, :, NZ:]
+    ref[0, :, x, y : y + 16, :] = value[:, :, :NZ]
+    ref[0, :, x + 1, y : y + 16, :] = value[:, :, NZ:]
 
 
 def pick_rows(channels):
@@ -263,20 +266,20 @@
     bias_rows = jnp.sum(jnp.where(pick_rows(channels), bias[...], 0.0), axis=1, keepdims=True) * GK
     bias_16 = jnp.concatenate([bias_rows.reshape(channels, 8, 1)] * 2, axis=1)
 
-    halves = []
-    for y in range(0, NY, 16):
-        halves += kron_halves(row_pair(field, y))
-    lanes = halves[0].shape[1]
-    done = dot(kron[...], jnp.concatenate(halves, axis=1))
-    for y in range(0, NY, 16):
-        put_rows(out, y, whole_rows(done, y // 8 * lanes, lanes) * GK + bias_16)
+    for x in range(0, field.shape[2], 2):
+        halves = []
+        for y in range(0, NY, 16):
+            halves += kron_halves(row_pair(field, x, y))
+        lanes = halves[0].shape[1]
+        done = dot(kron[...], jnp.concatenate(halves, axis=1))
+        for y in range(0, NY, 16):
+            put_rows(out, x, y, whole_rows(done, y // 8 * lanes, lanes) * GK + bias_16)
 
 
 def gelu_slope(v):
     n = v * v
     t = jnp.tanh(v * (n + GALPHA))
-    d = v * (1.5 * n + 0.5 * GALPHA)
-    return (1.0 + t) * (0.5 + (1.0 - t) * d)
+    return (1.0 + t) * (0.5 / SLOPE + (1.0 - t) * (v * (n + GALPHA / 3.0)))
 
 
 def grad_kernel(ns, channels, me_ref, pre, cot, *rest):
@@ -299,24 +302,30 @@
     wide = y_inverse(
         [get_channel(b_scr, step * GRAD_CB + i, channels, blocks) for i in range(GRAD_CB)], yi[...]
     )
-    g_all = jnp.concatenate(
-        [wide[:, g : g + width] for g in range(0, wide.shape[1], width)], axis=0
-    )
-    for j in range(GROUP // 2):
-        v_all = dot(g_all, zi[j])
-        for i in range(GRAD_CB):
-            for g in range(groups):
-                x = g * GROUP + 2 * j
-                at = (i * groups + g) * NY
-                v = v_all[at : at + NY]
-                v = v + jnp.concatenate([pre[0, i, x], pre[0, i, x + 1]], axis=1).astype(f32)
-                w = jnp.concatenate([cot[0, i, x], cot[0, i, x + 1]], axis=1).astype(f32)
-                d = (w * gelu_slope(v)).astype(bf16)
-                dpre[0, i, x] = d[:, :NZ]
-                dpre[0, i, x + 1] = d[:, NZ:]
+    pairs = GROUP // 2
+
+    def inverse(i, j):
+        first = i * groups * width
+        rows_of = [wide[:, first + g * width : first + (g + 1) * width] for g in range(groups)]
+        return dot(jnp.concatenate(rows_of, axis=0), zi[j])
+
+    def slope(i, j, v_all):
+        for g in range(groups):
+            x = g * GROUP + 2 * j
+            v = v_all[g * NY : (g + 1) * NY]
+            v = v + jnp.concatenate([pre[0, i, x], pre[0, i, x + 1]], axis=1).astype(f32)
+            w = jnp.concatenate([cot[0, i, x], cot[0, i, x + 1]], axis=1)
+            d = (w.astype(f32) * gelu_slope(v)).astype(bf16)
+            dpre[0, i, x] = d[:, :NZ]
+            dpre[0, i, x + 1] = d[:, NZ:]
+
     done = []
-    for i in range(GRAD_CB):
-        done += z_forward([dpre[0, i, x] for x in range(rows)], zf[...])
+    for i in range(GRAD_CB + 1):
+        for j in range(pairs):
+            if i < GRAD_CB:
+                slope(i, j, inverse(i, j))
+            if i and j == 0:
+                done += z_forward([dpre[0, i - 1, x] for x in range(rows)], zf[...])
     spectra = y_forward(done, yf[...])
     for i in range(GRAD_CB):
         put_channel(r_scr, step * GRAD_CB + i, channels, spectra[:, i * lanes : (i + 1) * lanes])
@@ -334,16 +343,17 @@
     def _():
         acc[...] = jnp.zeros_like(acc)
 
-    lefts, rights = [], []
-    for y in range(0, NY, 16):
-        lefts += kron_halves(row_pair(field, y))
-        rights += kron_halves(row_pair(dpre, y))
-    acc[...] += lax.dot_general(
-        jnp.concatenate(lefts, axis=1),
-        jnp.concatenate(rights, axis=1),
-        (((1,), (1,)), ((), ())),
-        preferred_element_type=f32,
-    )
+    for x in range(0, field.shape[2], 2):
+        lefts, rights = [], []
+        for y in range(0, NY, 16):
+            lefts += kron_halves(row_pair(field, x, y))
+            rights += kron_halves(row_pair(dpre, x, y))
+        acc[...] += lax.dot_general(
+            jnp.concatenate(lefts, axis=1),
+            jnp.concatenate(rights, axis=1),
+            (((1,), (1,)), ((), ())),
+            preferred_element_type=f32,
+        )
 
     @pl.when(step == pl.num_programs(0) - 1)
     def _():
@@ -353,7 +363,7 @@
         left = jnp.dot(same, pick, precision=high, preferred_element_type=f32)
         out[...] = lax.dot_general(
             pick, left, (((0,), (0,)), ((), ())), precision=high, preferred_element_type=f32
-        )
+        ) * SLOPE
 
 
 def back_kernel(ns, me_ref, dpre, point, *rest):
@@ -369,7 +379,7 @@
         x_inverse_in(me_ref[0], ns, channels, ins, xih, xil, b_scr)
         kron[...] = kron_rows(point[...], False)
 
-    per_group = GROUP // 2
+    per_group = GROUP // dpre.shape[2]
 
     @pl.when(step % per_group == 0)
     def _():
@@ -381,53 +391,61 @@
         for c in range(channels):
             g_scr[c] = wide[:, c * width : (c + 1) * width]
 
-    halves = []
-    for y in range(0, NY, 16):
-        halves += kron_halves(row_pair(dpre, y))
-    lanes = halves[0].shape[1]
-    point = dot(kron[...], jnp.concatenate(halves, axis=1))
-    spec = dot(g_scr[...].reshape(channels * NY, width), zi[step % per_group])
-    spec = spec.reshape(channels, NY, lanes)
-    for y in range(0, NY, 16):
-        put_rows(out, y, whole_rows(point, y // 8 * lanes, lanes) + spec[:, y : y + 16])
+    flat = g_scr[...].reshape(channels * NY, width)
+    pairs = dpre.shape[2] // 2
+    for p in range(pairs):
+        x = 2 * p
+        halves = []
+        for y in range(0, NY, 16):
+            halves += kron_halves(row_pair(dpre, x, y))
+        lanes = halves[0].shape[1]
+        point = dot(kron[...], jnp.concatenate(halves, axis=1))
+        spec = dot(flat, zi[step % per_group * pairs + p]).reshape(channels, NY, lanes)
+        for y in range(0, NY, 16):
+            one = whole_rows(point, y // 8 * lanes, lanes) * SLOPE
+            put_rows(out, x, y, one + spec[:, y : y + 16])
 
 
 def mix_kernel(ns, adjoint, *refs):
     ins, weights, total, out = refs[:ns], refs[ns], refs[ns + 1], refs[ns + 2]
-    channels = total.shape[1]
+    rows, channels, width = total.shape
+    half = width // 2
     u = ins[0][...]
     for k in range(1, ns):
         u = u + ins[k][...]
     total[...] = u
-    half = total.shape[2] // 2
-    if not adjoint:
-        real = jnp.zeros((channels, half), f32)
-        imag = jnp.zeros((channels, half), f32)
-        for c in range(channels):
-            a, b = total[0, pl.ds(c, 1), :half], total[0, pl.ds(c, 1), half:]
-            wr, wi = weights[0, c, 0].astype(f32), weights[1, c, 0].astype(f32)
-            real = real + (wr * a - wi * b)
-            imag = imag + (wr * b + wi * a)
-        out[0, :, :half] = real
-        out[0, :, half:] = imag
-    else:
-        a, b = total[0, :, :half], total[0, :, half:]
-        for c in range(channels):
-            wr, wi = weights[0, c, 0].astype(f32), weights[1, c, 0].astype(f32)
-            out[0, pl.ds(c, 1), :half] = jnp.sum(wr * a + wi * b, axis=0, keepdims=True)
-            out[0, pl.ds(c, 1), half:] = jnp.sum(wr * b - wi * a, axis=0, keepdims=True)
+    for ky in range(rows):
+        if not adjoint:
+            real = jnp.zeros((channels, half), f32)
+            imag = jnp.zeros((channels, half), f32)
+            for c in range(channels):
+                a, b = total[ky, pl.ds(c, 1), :half], total[ky, pl.ds(c, 1), half:]
+                wr, wi = weights[0, c, ky].astype(f32), weights[1, c, ky].astype(f32)
+                real = real + (wr * a - wi * b)
+                imag = imag + (wr * b + wi * a)
+            out[ky, :, :half] = real
+            out[ky, :, half:] = imag
+        else:
+            a, b = total[ky, :, :half], total[ky, :, half:]
+            for c in range(channels):
+                wr, wi = weights[0, c, ky].astype(f32), weights[1, c, ky].astype(f32)
+                out[ky, pl.ds(c, 1), :half] = jnp.sum(wr * a + wi * b, axis=0, keepdims=True)
+                out[ky, pl.ds(c, 1), half:] = jnp.sum(wr * b - wi * a, axis=0, keepdims=True)
 
 
 def weight_kernel(weights, out, scr):
     _, kxs, kzs, channels, _ = weights.shape
     modes = kxs * kzs
-    scr[:, :channels] = weights[...].astype(f32).reshape(modes * channels, channels)
+    stride = channels + PAD
+    wide = weights[...].astype(f32).reshape(modes, channels, channels)
+    scr[:, :channels, :channels] = wide
+    flat = scr.reshape(modes * stride, LANES)
     per = LANES // channels
     lane = lax.broadcasted_iota(jnp.int32, (modes, LANES), 1) // channels
     for c in range(0, channels, per):
-        packed = scr[pl.ds(c, modes, stride=channels), :]
+        packed = flat[pl.ds(c, modes, stride=stride), :]
         for q in range(1, per):
-            more = scr[pl.ds(c + q, modes, stride=channels), :]
+            more = flat[pl.ds(c + q, modes, stride=stride), :]
             packed = jnp.where(lane == q, pltpu.roll(more, q * channels, 1), packed)
         turned = packed.T.astype(bf16)
         for q in range(per):
@@ -450,6 +468,8 @@
         col = lax.broadcasted_iota(jnp.int32, (2 * channels, lanes), 1)
         return jnp.where(row == of(col), 1.0, 0.0).astype(bf16)
 
+    stride = channels + PAD
+    flat = scr.reshape(2, modes * stride, LANES)
     by_o = table(LANES, lambda col: col % channels)
     by_c = table(channels * channels, lambda col: col // channels)
     g_all = lax.dot_general(stack(gs), by_o, tn, preferred_element_type=f32)
@@ -467,8 +487,8 @@
         for p, value in enumerate((real, imag)):
             for q in range(per):
                 one = value if q == 0 else pltpu.roll(value, LANES - q * channels, 1)
-                scr[p, pl.ds(n * per + q, modes, stride=channels), :] = one
-    out[...] = scr[:, :, :channels].reshape(out.shape)
+                flat[p, pl.ds(n * per + q, modes, stride=stride), :] = one
+    out[...] = scr[:, :, :channels, :channels].reshape(out.shape)
 
 
 def whole(shape):
@@ -491,7 +511,8 @@
     zf = jnp.asarray(z_forward_table())
     zi = jnp.asarray(z_inverse_table())
     yf, yi = (jnp.asarray(t) for t in y_tables())
-    xf = [jnp.asarray(t) for t in split_bf(x_forward_table())]
+    xf = [jnp.asarray(t) for t in split_bf(x_forward_table(1.0))]
+    xf_grad = [jnp.asarray(t) for t in split_bf(x_forward_table(SLOPE))]
     xf_spec = [pl.BlockSpec((lanes, width), lambda i, at: (at[0], 0))] * 2
     xi_pre = [jnp.asarray(t) for t in split_bf(x_inverse_table(SCALE_INVERSE * GK, ns))]
     xi_back = [jnp.asarray(t) for t in split_bf(x_inverse_table(SCALE_INVERSE, ns))]
@@ -503,7 +524,7 @@
     def some_channels(count):
         return pl.BlockSpec((1, count, rows, NY, NZ), lambda c, *_: (0, c, 0, 0, 0))
 
-    two_rows = pl.BlockSpec((1, channels, 2, NY, NZ), lambda x, *_: (0, 0, x, 0, 0))
+    some_rows = pl.BlockSpec((1, channels, ROWS, NY, NZ), lambda x, *_: (0, 0, x, 0, 0))
     big = jax.ShapeDtypeStruct(shape, bf16)
     cells = channels * rows * NY * NZ
     r_scr = pltpu.VMEM((lanes // LANES, MY * channels, LANES), f32)
@@ -535,9 +556,9 @@
     def point_call(field, point_weight, bias):
         return pl.pallas_call(
             point_kernel,
-            grid=(rows // 2,),
-            in_specs=[two_rows] + tables(point_weight, bias[None]),
-            out_specs=two_rows,
+            grid=(rows // ROWS,),
+            in_specs=[some_rows] + tables(point_weight, bias[None]),
+            out_specs=some_rows,
             out_shape=big,
             scratch_shapes=[kron_scr],
             compiler_params=params(),
@@ -546,13 +567,11 @@
         )(field, point_weight, bias[None])
 
     def mix_call(adjoint, chunks, w):
-        one_ky = pl.BlockSpec((1, channels, width), lambda k: (k, 0, 0))
-        w_spec = pl.BlockSpec((2, channels, 1, channels, MX * MZ), lambda k: (0, 0, k, 0, 0))
         return pl.pallas_call(
             functools.partial(mix_kernel, ns, adjoint),
-            grid=(own_ky,),
-            in_specs=[one_ky] * ns + [w_spec],
-            out_specs=[one_ky, one_ky],
+            grid=(1,),
+            in_specs=[chunk_spec] * ns + tables(w),
+            out_specs=[chunk_spec, chunk_spec],
             out_shape=[chunk, chunk],
             compiler_params=params(),
             name="mix_adjoint" if adjoint else "mix",
@@ -576,18 +595,22 @@
             compiler_params=params(),
             cost_estimate=cost(cells * 1024, cells * 6),
             name="gelu_gradient",
-        )(me_arr, pre, cotangent, *chunks, *xi_pre, yi, zi, zf, yf, *xf)
-
-    def pair_call(field, dpre):
+        )(me_arr, pre, cotangent, *chunks, *xi_pre, yi, zi, zf, yf, *xf_grad)
+
+    def pair_call(field, dpre, part=0, count=1):
+        steps = rows // ROWS // count
+        part_rows = pl.BlockSpec(
+            (1, channels, ROWS, NY, NZ), lambda x: (0, 0, x + part * steps, 0, 0)
+        )
         return pl.pallas_call(
             pair_kernel,
-            grid=(rows // 2,),
-            in_specs=[two_rows, two_rows],
+            grid=(steps,),
+            in_specs=[part_rows, part_rows],
             out_specs=whole((channels, channels)),
             out_shape=jax.ShapeDtypeStruct((channels, channels), f32),
             scratch_shapes=[pltpu.VMEM((size, size), f32)],
             compiler_params=params(),
-            cost_estimate=cost(cells * 512, cells * 4),
+            cost_estimate=cost(cells * 512 // count, cells * 4 // count),
             name="point_gradient",
         )(field, dpre)
 
@@ -596,13 +619,13 @@
             functools.partial(back_kernel, ns),
             grid_spec=pltpu.PrefetchScalarGridSpec(
                 num_scalar_prefetch=1,
-                grid=(rows // 2,),
-                in_specs=[two_rows]
+                grid=(rows // ROWS,),
+                in_specs=[some_rows]
                 + tables(point_weight)
                 + [chunk_spec] * ns
                 + xi_spec
                 + tables(yi, zi),
-                out_specs=two_rows,
+                out_specs=some_rows,
                 scratch_shapes=[b_scr, pltpu.VMEM((channels, NY, GROUP * 2 * MZ), bf16), kron_scr],
             ),
             out_shape=big,
@@ -623,25 +646,26 @@
                 (1, channels, 1, channels, modes), lambda p, k: (p, 0, k, 0, 0)
             ),
             out_shape=jax.ShapeDtypeStruct((2, channels, own_ky, channels, modes), bf16),
-            scratch_shapes=[pltpu.VMEM((modes * channels, LANES), f32)],
+            scratch_shapes=[pltpu.VMEM((modes, channels + PAD, LANES), f32)],
             compiler_params=params(axes=2),
             cost_estimate=cost(0, 2 * own_ky * modes * channels * LANES * 2),
             name="weight_layout",
         )(spec_weight)
 
-    def spec_call(us, gs):
-        one_ky = pl.BlockSpec((1, channels, width), lambda k: (k, 0, 0))
+    def spec_call(every):
+        one_u = pl.BlockSpec((1, channels, width), lambda k: (k, 0, 0))
+        one_g = pl.BlockSpec((1, channels, width), lambda k: (own_ky + k, 0, 0))
         return pl.pallas_call(
-            functools.partial(outer_kernel, len(us)),
+            functools.partial(outer_kernel, len(every)),
             grid=(own_ky,),
-            in_specs=[one_ky] * (2 * len(us)),
+            in_specs=[one_u] * len(every) + [one_g] * len(every),
             out_specs=pl.BlockSpec((2, MX, MZ, channels, channels), lambda k: (0, 0, k, 0, 0)),
             out_shape=jax.ShapeDtypeStruct((2, MX, own_ky * MZ, channels, channels), f32),
-            scratch_shapes=[pltpu.VMEM((2, modes * channels, LANES), f32)],
+            scratch_shapes=[pltpu.VMEM((2, modes, channels + PAD, LANES), f32)],
             compiler_params=params(),
             cost_estimate=cost(0, 2 * own_ky * modes * channels * LANES * 4),
             name="weight_gradient",
-        )(*us, *gs)
+        )(*every, *every)
 
     return {
         "field": field_call,
@@ -674,23 +698,26 @@
     uhat, vhat = calls["mix"](False, swap(field_chunks, "slab", ns), w)
     vhats = swap([vhat] * ns, "slab", ns)
     dpre, *grad_chunks = calls["grad"](me_arr, pre, cotangent, vhats)
-    u_all = swap([uhat] * nchan, "chan", nchan)
-
-    point_part = calls["pair"](field, dpre)
+
+    point_part = calls["pair"](field, dpre, 0, 2)
     ghat, hhat = calls["mix"](True, swap(grad_chunks, "slab", ns), w)
     hhats = swap([hhat] * ns, "slab", ns)
-    g_all = swap([ghat] * nchan, "chan", nchan)
-    field_grad = calls["back"](me_arr, dpre, point_weight, hhats)
-
-    spec_grad = calls["spec"](u_all, g_all)
+    dpre_later, _ = lax.optimization_barrier((dpre, hhat))
+    point_part = point_part + calls["pair"](field, dpre_later, 1, 2)
 
     norm_scale = 1.0 / math.sqrt(nchan * NX * NY * NZ)
     dc = jnp.where(me == 0, ghat[0, :, 0], 0.0) * (1.0 / SCALE_FORWARD)
-    tail = jnp.concatenate([point_part, dc[None, :]], axis=0)
-    for axis, count in (("chan", nchan), ("slab", ns)):
-        tail = sum(swap([tail] * count, axis, count))
-    tail = tail * norm_scale
-    return field_grad, spec_grad, tail[:channels], tail[channels]
+    tail = jnp.concatenate([point_part, dc[:, None]], axis=1)
+    tail = jnp.pad(tail, ((0, 0), (0, ghat.shape[2] - tail.shape[1])))
+    sample = jnp.concatenate([uhat, ghat, tail[None]], axis=0)
+    every = swap([sample] * nchan, "chan", nchan)
+    field_grad = calls["back"](me_arr, dpre, point_weight, hhats)
+    every, field_grad = lax.optimization_barrier((every, field_grad))
+    tails = swap([sum(one[-1, :, : channels + 1] for one in every)] * ns, "slab", ns)
+
+    spec_grad = calls["spec"](every)
+    tail = sum(tails) * norm_scale
+    return field_grad, spec_grad, tail[:, :channels], tail[:, channels]
 
 
 def plain_device(field, cotangent, spec_weight, point_weight, bias):

time: 267 us -> 221 us (0.83)
  Pallas kernels: 219 us -> 187 us
  waiting for transfers between devices: 14.3 us -> 0.05 us
  starting transfers between devices: 24.2 us -> 26.9 us
    pallas_call x5 -> x6, Pallas kernels: 90.1 us -> 72.7 us  [the longest x1 27.2 us: point_call(): pl.pallas_call(point_kernel, grid=(rows // ROWS,), in_specs=[some_rows] +...]
    ppermute x24 -> x18, waiting for transfers between devices: 14.3 us -> 0.05 us  [swap(): got.append(lax.ppermute(chunks[k], axis, pairs))]
    pallas_call x1, Pallas kernels: 60.7 us -> 52.5 us  [grad_call(): pl.pallas_call(functools.partial(grad_kernel, ns, channels), grid_spec=pl...]
    pallas_call x1, Pallas kernels: 14 us -> 9.64 us  [weight_call(): pl.pallas_call(weight_kernel, grid=(2, own_ky), in_specs=[w_block], out_s...]
    ppermute x24 -> x18, starting transfers between devices: 24.2 us -> 26.9 us  [swap(): got.append(lax.ppermute(chunks[k], axis, pairs))]
  transfers between devices with their start and end apart: 24 -> 18, of which waited for: 6 -> 0; matrix products, arithmetic and copies ran while one was open for 0% -> 0% of each run, Pallas kernels for 41% -> 50%
where the time goes in v2:
time: 221 us; the launch traced here: 220 us
  Pallas kernels  187 us (85%)
  starting transfers between devices  26.9 us (12%)
  local copies, waits for them, and re-layouts  4.75 us (2%)
    pallas_call x1, Pallas kernels, grad_call(): pl.pallas_call(functools.partial(grad_kernel, ns, channels), grid_spec=pl...  52.5 us
    pallas_call x1, Pallas kernels, back_call(): pl.pallas_call(functools.partial(back_kernel, ns), grid_spec=pltpu.Prefet...  33.4 us
    pallas_call x1, Pallas kernels, point_call(): pl.pallas_call(point_kernel, grid=(rows // ROWS,), in_specs=[some_rows] +...  27.2 us
    ppermute x18, starting transfers between devices, swap(): got.append(lax.ppermute(chunks[k], axis, pairs))  26.9 us
    pallas_call x2, Pallas kernels, pair_call(): pl.pallas_call(pair_kernel, grid=(steps,), in_specs=[part_rows, part_rows...  26.9 us
    pallas_call x1, Pallas kernels, field_call(): pl.pallas_call(functools.partial(field_kernel, ns, channels), grid_spec=p...  18.5 us
    pallas_call x1, Pallas kernels, spec_call(): pl.pallas_call(functools.partial(outer_kernel, len(every)), grid=(own_ky,...  12.1 us
    pallas_call x1, Pallas kernels, weight_call(): pl.pallas_call(weight_kernel, grid=(2, own_ky), in_specs=[w_block], out_s...  9.64 us
  transfers between devices with their start and end apart: 18, of which 0 were waited for; matrix products, arithmetic and copies ran while one was open for 0% of the time, Pallas kernels for 50%

profile of v2, /device:TPU:0, one launch (start us, length us, event | category | flops | bytes accessed | tf_op | source)
XLA Modules:
  0.0 220.2 jit_solution(15887245725359873425)
XLA Ops:
  0.6 18.5 %field_spectrum.1 = (f32[4,32,256]{2,1,0:T(8,128)}, f32[4,32,256]{2,1,0:T(8,128)}, f32[4,32,256]{2,1,0:T(8,128)}, f32[4,32,256]{2,1,0:T(8,128)}) custom-call(s32[1]{0:T(128)} %bitcast.me_ref, bf16[1,32,32,128,128]{4,3,2,1,0:T(8,128)(2,1)} %field.7, bf16[1024,128]{1,0:T(8,128)(2,1)} %constant.38.clone.zf.rest_8_, bf16[32,128]{1,0:T(8,128)(2,1)} %constant.40.clone.yf.rest_9_, ...), custom_call_target="tpu_custom_call" | custom-call | flops 8589934592 | bytes 33554432 | tf_op jit(solution)/shard_map/field_spectrum/pallas_call | solution.py:541
  19.1 3.0 %collective-permute-start = (f32[4,32,256]{2,1,0:T(8,128)}, f32[4,32,256]{2,1,0:T(8,128)S(1)}, u32[]{:S(2)}, u32[]{:S(2)}) collective-permute-start(f32[4,32,256]{2,1,0:T(8,128)} %get-tuple-element.24), channel_id=1, source_target_pairs={{0,4},{4,8},{8,12},{12,0},{1,5},{5,9},{9,13},{13,1},{2,6},{6,10},{... | collective-permute-start | bytes 393224 | tf_op jit(solution)/shard_map/ppermute | solution.py:692
  22.2 2.6 %collective-permute-start.1 = (f32[4,32,256]{2,1,0:T(8,128)}, f32[4,32,256]{2,1,0:T(8,128)S(1)}, u32[]{:S(2)}, u32[]{:S(2)}) collective-permute-start(f32[4,32,256]{2,1,0:T(8,128)} %get-tuple-element.25), channel_id=1, source_target_pairs={{0,8},{4,12},{8,0},{12,4},{1,9},{5,13},{9,1},{13,5},{2,10},{6,14},... | collective-permute-start | bytes 393224 | tf_op jit(solution)/shard_map/ppermute | solution.py:692
  24.7 1.3 collective-permute-start.2
  26.1 9.6 %weight_layout.1.refs_4_ = bf16[2,32,4,32,128]{4,3,2,1,0:T(8,128)(2,1)} custom-call(bf16[2,16,32,32,32]{4,3,2,1,0:T(8,128)(2,1)} %weights.1), custom_call_target="tpu_custom_call" | custom-call | bytes 8388608 | tf_op jit(solution)/shard_map/weight_layout/pallas_call | solution.py:641
  35.7 0.0 collective-permute-done.refs_1_
  35.7 0.0 collective-permute-done.1.refs_2_
  35.8 0.6 copy-done.12
  36.4 0.1 copy-done.14
  36.4 0.1 copy-done.16
  36.5 3.2 %mix.1 = (f32[4,32,256]{2,1,0:T(8,128)}, f32[4,32,256]{2,1,0:T(8,128)}) custom-call(f32[4,32,256]{2,1,0:T(8,128)} %get-tuple-element.23.refs_0_, f32[4,32,256]{2,1,0:T(8,128)} %copy-done.12, f32[4,32,256]{2,1,0:T(8,128)} %copy-done.14, f32[4,32,256]{2,1,0:T(8,128)} %copy-done.16, bf16[2,32,4,32,128]{4,3,2,1,0:T(8,128)(2,1)} %weight_layout.1.refs_4_), custom_call_target="tpu_custom_call" | custom-call | tf_op jit(solution)/shard_map/mix/pallas_call | solution.py:570
  39.7 1.0 collective-permute-start.3
  40.8 1.7 collective-permute-start.4
  42.4 1.1 collective-permute-start.5
  43.6 27.2 %pointwise.1.pre = bf16[1,32,32,128,128]{4,3,2,1,0:T(8,128)(2,1)} custom-call(bf16[1,32,32,128,128]{4,3,2,1,0:T(8,128)(2,1)} %field.7, bf16[32,32]{1,0:T(8,128)(2,1)} %point.3, f32[1,32]{1,0:T(1,128)} %bitcast.10), custom_call_target="tpu_custom_call" | custom-call | flops 8589934592 | bytes 67108864 | tf_op jit(solution)/shard_map/pointwise/pallas_call | solution.py:557
  70.7 0.0 collective-permute-done.3.rest_1_
  70.7 0.0 collective-permute-done.4.rest_2_
  70.7 0.0 collective-permute-done.5.rest_3_
  70.8 0.6 copy-done.8
  71.4 0.1 copy-done.9
  71.4 0.6 copy-done.10
  72.1 52.5 %gelu_gradient.1 = (bf16[1,32,32,128,128]{4,3,2,1,0:T(8,128)(2,1)}, f32[4,32,256]{2,1,0:T(8,128)}, f32[4,32,256]{2,1,0:T(8,128)}, f32[4,32,256]{2,1,0:T(8,128)}, f32[4,32,256]{2,1,0:T(8,128)}) custom-call(s32[1]{0:T(128)} %bitcast.me_ref, bf16[1,32,32,128,128]{4,3,2,1,0:T(8,128)(2,1)} %pointwise.1.pre, bf16[1,32,32,128,128]{4,3,2,1,0:T(8,128)(2,1)} %cot.1, ...), custom_call_target="tpu_custom_call" | custom-call | flops 17179869184 | bytes 100663296 | tf_op jit(solution)/shard_map/gelu_gradient/pallas_call | solution.py:581
  124.6 1.2 collective-permute-start.6
  125.8 1.3 collective-permute-start.7
  127.1 2.7 %collective-permute-start.8 = (f32[4,32,256]{2,1,0:T(8,128)}, f32[4,32,256]{2,1,0:T(8,128)S(1)}, u32[]{:S(2)}, u32[]{:S(2)}) collective-permute-start(f32[4,32,256]{2,1,0:T(8,128)} %get-tuple-element.32), channel_id=1, source_target_pairs={{0,12},{4,0},{8,4},{12,8},{1,13},{5,1},{9,5},{13,9},{2,14},{6,2},{... | collective-permute-start | bytes 393224 | tf_op jit(solution)/shard_map/ppermute | solution.py:692
  129.8 13.4 %point_gradient.2 = f32[32,32]{1,0:T(8,128)} custom-call(bf16[1,32,32,128,128]{4,3,2,1,0:T(8,128)(2,1)} %field.7, bf16[1,32,32,128,128]{4,3,2,1,0:T(8,128)(2,1)} %get-tuple-element.36.dpre), custom_call_target="tpu_custom_call" | custom-call | flops 4294967296 | bytes 33554432 | tf_op jit(solution)/shard_map/point_gradient/pallas_call | solution.py:605
  143.2 0.6 copy-done.11
  143.9 0.0 copy-done.13
  143.9 0.0 copy-done.15
  143.9 3.4 %mix_adjoint.1 = (f32[4,32,256]{2,1,0:T(8,128)}, f32[4,32,256]{2,1,0:T(8,128)}) custom-call(f32[4,32,256]{2,1,0:T(8,128)} %get-tuple-element.29.refs_0_, f32[4,32,256]{2,1,0:T(8,128)} %copy-done.11, f32[4,32,256]{2,1,0:T(8,128)} %copy-done.13, f32[4,32,256]{2,1,0:T(8,128)} %copy-done.15, bf16[2,32,4,32,128]{4,3,2,1,0:T(8,128)(2,1)} %weight_layout.1.refs_4_), custom_call_target="tpu_custom_call" | custom-call | tf_op jit(solution)/shard_map/mix_adjoint/pallas_call | solution.py:570
  147.3 0.1 collective-permute-start.12
  147.4 1.0 collective-permute-start.13
  148.4 2.9 %collective-permute-start.14 = (f32[4,32,256]{2,1,0:T(8,128)}, f32[4,32,256]{2,1,0:T(8,128)S(1)}, u32[]{:S(2)}, u32[]{:S(2)}) collective-permute-start(f32[4,32,256]{2,1,0:T(8,128)} %get-tuple-element.35.rest_0_), channel_id=1, source_target_pairs={{0,12},{4,0},{8,4},{12,8},{1,13},{5,1},{9,5},{13,9},{2,14},{6,2},{... | collective-permute-start | bytes 393224 | tf_op jit(solution)/shard_map/ppermute | solution.py:692
  151.2 13.4 %point_gradient.3 = f32[32,32]{1,0:T(8,128)} custom-call(bf16[1,32,32,128,128]{4,3,2,1,0:T(8,128)(2,1)} %field.7, bf16[1,32,32,128,128]{4,3,2,1,0:T(8,128)(2,1)} %get-tuple-element.36.dpre), custom_call_target="tpu_custom_call" | custom-call | flops 4294967296 | bytes 33554432 | tf_op jit(solution)/shard_map/point_gradient/pallas_call | solution.py:605
  164.6 0.7 add.28
  165.4 0.1 fusion
  165.5 1.6 collective-permute-start.10
  167.1 0.5 collective-permute-start.9
  167.6 0.1 copy-done.5
  167.7 0.5 copy-done.6
  168.2 0.7 copy-done.7
  168.9 33.4 %field_gradient.1 = bf16[1,32,32,128,128]{4,3,2,1,0:T(8,128)(2,1)} custom-call(s32[1]{0:T(128)} %bitcast.me_ref, bf16[1,32,32,128,128]{4,3,2,1,0:T(8,128)(2,1)} %get-tuple-element.36.dpre, bf16[32,32]{1,0:T(8,128)(2,1)} %point.3, f32[4,32,256]{2,1,0:T(8,128)} %get-tuple-element.35.rest_0_, f32[4,32,256]{2,1,0:T(8,128)} %copy-done.5, ...), custom_call_target="tpu_custom_call" | custom-call | flops 17179869184 | bytes 67108864 | tf_op jit(solution)/shard_map/field_gradient/pallas_call | solution.py:618
  202.3 0.6 collective-permute-start.15
  203.0 1.5 collective-permute-start.16
  204.5 2.8 %collective-permute-start.17 = (f32[32,33]{1,0:T(8,128)S(1)}, f32[32,33]{1,0:T(8,128)S(1)}, u32[]{:S(2)}, u32[]{:S(2)}) collective-permute-start(f32[32,33]{1,0:T(8,128)S(1)} %add_bitcast_fusion), channel_id=1, source_target_pairs={{0,12},{4,0},{8,4},{12,8},{1,13},{5,1},{9,5},{13,9},{2,14},{6,2},{... | collective-permute-start | bytes 12680 | tf_op jit(solution)/shard_map/ppermute | solution.py:692
  207.4 12.1 %weight_gradient.1 = f32[2,16,32,32,32]{4,3,2,1,0:T(8,128)} custom-call(f32[9,32,256]{2,1,0:T(8,128)} %copy-done, f32[9,32,256]{2,1,0:T(8,128)} %copy-done.3, f32[9,32,256]{2,1,0:T(8,128)} %copy-done.1, f32[9,32,256]{2,1,0:T(8,128)} %copy-done.2, f32[9,32,256]{2,1,0:T(8,128)} %copy-done, f32[9,32,256]{2,1,0:T(8,128)} %copy-done.3, f32[9,32,256]{2,1,0:T(8,128)} %copy-done.1, ...), custom_call_target="tpu_custom_call" | custom-call | bytes 16777216 | tf_op jit(solution)/shard_map/weight_gradient/pallas_call | solution.py:658
  219.5 0.0 copy-start.19
  219.5 0.7 slice_reduce_fusion
  (45 shorter events, 0.1 us)
Async XLA Ops:
  19.1 16.6 %collective-permute-start = (f32[4,32,256]{2,1,0:T(8,128)}, f32[4,32,256]{2,1,0:T(8,128)S(1)}, u32[]{:S(2)}, u32[]{:S(2)}) collective-permute-start(f32[4,32,256]{2,1,0:T(8,128)} %get-tuple-element.24), channel_id=1, source_target_pairs={{0,4},{4,8},{8,12},{12,0},{1,5},{5,9},{9,13},{13,1},{2,6},{6,10},{... | collective-permute-start | bytes 393224 | tf_op jit(solution)/shard_map/ppermute | solution.py:692
  22.2 13.6 %collective-permute-start.1 = (f32[4,32,256]{2,1,0:T(8,128)}, f32[4,32,256]{2,1,0:T(8,128)S(1)}, u32[]{:S(2)}, u32[]{:S(2)}) collective-permute-start(f32[4,32,256]{2,1,0:T(8,128)} %get-tuple-element.25), channel_id=1, source_target_pairs={{0,8},{4,12},{8,0},{12,4},{1,9},{5,13},{9,1},{13,5},{2,10},{6,14},... | collective-permute-start | bytes 393224 | tf_op jit(solution)/shard_map/ppermute | solution.py:692
  24.7 11.0 %collective-permute-start.2 = (f32[4,32,256]{2,1,0:T(8,128)}, f32[4,32,256]{2,1,0:T(8,128)S(1)}, u32[]{:S(2)}, u32[]{:S(2)}) collective-permute-start(f32[4,32,256]{2,1,0:T(8,128)} %get-tuple-element.26), channel_id=1, source_target_pairs={{0,12},{4,0},{8,4},{12,8},{1,13},{5,1},{9,5},{13,9},{2,14},{6,2},{... | collective-permute-start | bytes 393224 | tf_op jit(solution)/shard_map/ppermute | solution.py:692
  35.7 0.6 copy-start.12
  35.7 0.7 copy-start.14
  35.8 0.7 copy-start.16
  39.7 31.0 %collective-permute-start.3 = (f32[4,32,256]{2,1,0:T(8,128)}, f32[4,32,256]{2,1,0:T(8,128)S(1)}, u32[]{:S(2)}, u32[]{:S(2)}) collective-permute-start(f32[4,32,256]{2,1,0:T(8,128)} %get-tuple-element.28.rest_0_), channel_id=1, source_target_pairs={{0,4},{4,8},{8,12},{12,0},{1,5},{5,9},{9,13},{13,1},{2,6},{6,10},{... | collective-permute-start | bytes 393224 | tf_op jit(solution)/shard_map/ppermute | solution.py:692
  40.8 30.0 %collective-permute-start.4 = (f32[4,32,256]{2,1,0:T(8,128)}, f32[4,32,256]{2,1,0:T(8,128)S(1)}, u32[]{:S(2)}, u32[]{:S(2)}) collective-permute-start(f32[4,32,256]{2,1,0:T(8,128)} %get-tuple-element.28.rest_0_), channel_id=1, source_target_pairs={{0,8},{4,12},{8,0},{12,4},{1,9},{5,13},{9,1},{13,5},{2,10},{6,14},... | collective-permute-start | bytes 393224 | tf_op jit(solution)/shard_map/ppermute | solution.py:692
  42.4 28.3 %collective-permute-start.5 = (f32[4,32,256]{2,1,0:T(8,128)}, f32[4,32,256]{2,1,0:T(8,128)S(1)}, u32[]{:S(2)}, u32[]{:S(2)}) collective-permute-start(f32[4,32,256]{2,1,0:T(8,128)} %get-tuple-element.28.rest_0_), channel_id=1, source_target_pairs={{0,12},{4,0},{8,4},{12,8},{1,13},{5,1},{9,5},{13,9},{2,14},{6,2},{... | collective-permute-start | bytes 393224 | tf_op jit(solution)/shard_map/ppermute | solution.py:692
  70.7 0.6 copy-start.8
  70.7 0.7 copy-start.9
  71.4 0.6 copy-start.10
  124.6 18.6 %collective-permute-start.6 = (f32[4,32,256]{2,1,0:T(8,128)}, f32[4,32,256]{2,1,0:T(8,128)S(1)}, u32[]{:S(2)}, u32[]{:S(2)}) collective-permute-start(f32[4,32,256]{2,1,0:T(8,128)} %get-tuple-element.30), channel_id=1, source_target_pairs={{0,4},{4,8},{8,12},{12,0},{1,5},{5,9},{9,13},{13,1},{2,6},{6,10},{... | collective-permute-start | bytes 393224 | tf_op jit(solution)/shard_map/ppermute | solution.py:692
  125.8 17.4 %collective-permute-start.7 = (f32[4,32,256]{2,1,0:T(8,128)}, f32[4,32,256]{2,1,0:T(8,128)S(1)}, u32[]{:S(2)}, u32[]{:S(2)}) collective-permute-start(f32[4,32,256]{2,1,0:T(8,128)} %get-tuple-element.31), channel_id=1, source_target_pairs={{0,8},{4,12},{8,0},{12,4},{1,9},{5,13},{9,1},{13,5},{2,10},{6,14},... | collective-permute-start | bytes 393224 | tf_op jit(solution)/shard_map/ppermute | solution.py:692
  127.1 16.1 %collective-permute-start.8 = (f32[4,32,256]{2,1,0:T(8,128)}, f32[4,32,256]{2,1,0:T(8,128)S(1)}, u32[]{:S(2)}, u32[]{:S(2)}) collective-permute-start(f32[4,32,256]{2,1,0:T(8,128)} %get-tuple-element.32), channel_id=1, source_target_pairs={{0,12},{4,0},{8,4},{12,8},{1,13},{5,1},{9,5},{13,9},{2,14},{6,2},{... | collective-permute-start | bytes 393224 | tf_op jit(solution)/shard_map/ppermute | solution.py:692
  143.2 0.7 copy-start.11
  143.2 0.7 copy-start.13
  143.2 0.7 copy-start.15
  147.3 17.3 %copy-start.18 = (f32[32,32]{1,0:T(8,128)S(1)}, f32[32,32]{1,0:T(8,128)}, u32[]{:S(2)}) copy-start(f32[32,32]{1,0:T(8,128)} %point_gradient.2) | copy-start | bytes 12292
  147.3 18.0 %copy-start.4 = (f32[4,32,256]{2,1,0:T(8,128)S(1)}, f32[4,32,256]{2,1,0:T(8,128)}, u32[]{:S(2)}) copy-start(f32[4,32,256]{2,1,0:T(8,128)} %get-tuple-element.33) | copy-start | bytes 393220
  147.3 18.1 %copy-start.17 = (f32[4,32,256]{2,1,0:T(8,128)S(1)}, f32[4,32,256]{2,1,0:T(8,128)}, u32[]{:S(2)}) copy-start(f32[4,32,256]{2,1,0:T(8,128)} %get-tuple-element.27) | copy-start | bytes 393220
  147.3 19.7 %collective-permute-start.12 = (f32[4,32,256]{2,1,0:T(8,128)}, f32[4,32,256]{2,1,0:T(8,128)S(1)}, u32[]{:S(2)}, u32[]{:S(2)}) collective-permute-start(f32[4,32,256]{2,1,0:T(8,128)} %get-tuple-element.35.rest_0_), channel_id=1, source_target_pairs={{0,4},{4,8},{8,12},{12,0},{1,5},{5,9},{9,13},{13,1},{2,6},{6,10},{... | collective-permute-start | bytes 393224 | tf_op jit(solution)/shard_map/ppermute | solution.py:692
  147.4 20.2 %collective-permute-start.13 = (f32[4,32,256]{2,1,0:T(8,128)}, f32[4,32,256]{2,1,0:T(8,128)S(1)}, u32[]{:S(2)}, u32[]{:S(2)}) collective-permute-start(f32[4,32,256]{2,1,0:T(8,128)} %get-tuple-element.35.rest_0_), channel_id=1, source_target_pairs={{0,8},{4,12},{8,0},{12,4},{1,9},{5,13},{9,1},{13,5},{2,10},{6,14},... | collective-permute-start | bytes 393224 | tf_op jit(solution)/shard_map/ppermute | solution.py:692
  148.4 19.2 %collective-permute-start.14 = (f32[4,32,256]{2,1,0:T(8,128)}, f32[4,32,256]{2,1,0:T(8,128)S(1)}, u32[]{:S(2)}, u32[]{:S(2)}) collective-permute-start(f32[4,32,256]{2,1,0:T(8,128)} %get-tuple-element.35.rest_0_), channel_id=1, source_target_pairs={{0,12},{4,0},{8,4},{12,8},{1,13},{5,1},{9,5},{13,9},{2,14},{6,2},{... | collective-permute-start | bytes 393224 | tf_op jit(solution)/shard_map/ppermute | solution.py:692
  165.5 36.8 %copy-start = (f32[9,32,256]{2,1,0:T(8,128)}, f32[9,32,256]{2,1,0:T(8,128)S(1)}, u32[]{:S(2)}) copy-start(f32[9,32,256]{2,1,0:T(8,128)S(1)} %pad_maximum_fusion.refs_0_.refs_4_) | copy-start | bytes 884740
  165.5 36.8 %collective-permute-start.10 = (f32[9,32,256]{2,1,0:T(8,128)S(1)}, f32[9,32,256]{2,1,0:T(8,128)S(1)}, u32[]{:S(2)}, u32[]{:S(2)}) collective-permute-start(f32[9,32,256]{2,1,0:T(8,128)S(1)} %pad_maximum_fusion.refs_0_.refs_4_), channel_id=1, source_target_pairs={{0,2},{1,3},{2,0},{3,1},{4,6},{5,7},{6,4},{7,5},{8,10},{9,11},{10,... | collective-permute-start | bytes 884744 | tf_op jit(solution)/shard_map/ppermute | solution.py:692
  167.1 35.2 %collective-permute-start.11 = (f32[9,32,256]{2,1,0:T(8,128)S(1)}, f32[9,32,256]{2,1,0:T(8,128)S(1)}, u32[]{:S(2)}, u32[]{:S(2)}) collective-permute-start(f32[9,32,256]{2,1,0:T(8,128)S(1)} %pad_maximum_fusion.refs_0_.refs_4_), channel_id=1, source_target_pairs={{0,3},{1,0},{2,1},{3,2},{4,7},{5,4},{6,5},{7,6},{8,11},{9,8},{10,9... | collective-permute-start | bytes 884744 | tf_op jit(solution)/shard_map/ppermute | solution.py:692
  167.1 0.7 copy-start.5
  167.1 35.2 %collective-permute-start.9 = (f32[9,32,256]{2,1,0:T(8,128)S(1)}, f32[9,32,256]{2,1,0:T(8,128)S(1)}, u32[]{:S(2)}, u32[]{:S(2)}) collective-permute-start(f32[9,32,256]{2,1,0:T(8,128)S(1)} %pad_maximum_fusion.refs_0_.refs_4_), channel_id=1, source_target_pairs={{0,1},{1,2},{2,3},{3,0},{4,5},{5,6},{6,7},{7,4},{8,9},{9,10},{10,1... | collective-permute-start | bytes 884744 | tf_op jit(solution)/shard_map/ppermute | solution.py:692
  167.6 0.6 copy-start.6
  168.2 0.7 copy-start.7
  202.3 5.1 %copy-start.1 = (f32[9,32,256]{2,1,0:T(8,128)}, f32[9,32,256]{2,1,0:T(8,128)S(1)}, u32[]{:S(2)}) copy-start(f32[9,32,256]{2,1,0:T(8,128)S(1)} %collective-permute-done.10.refs_2_.refs_6_) | copy-start | bytes 884740
  202.3 5.1 %copy-start.2 = (f32[9,32,256]{2,1,0:T(8,128)}, f32[9,32,256]{2,1,0:T(8,128)S(1)}, u32[]{:S(2)}) copy-start(f32[9,32,256]{2,1,0:T(8,128)S(1)} %collective-permute-done.11.refs_3_.refs_7_) | copy-start | bytes 884740
  202.3 5.0 %copy-start.3 = (f32[9,32,256]{2,1,0:T(8,128)}, f32[9,32,256]{2,1,0:T(8,128)S(1)}, u32[]{:S(2)}) copy-start(f32[9,32,256]{2,1,0:T(8,128)S(1)} %collective-permute-done.9.refs_1_.refs_5_) | copy-start | bytes 884740
  202.3 17.1 %collective-permute-start.15 = (f32[32,33]{1,0:T(8,128)S(1)}, f32[32,33]{1,0:T(8,128)S(1)}, u32[]{:S(2)}, u32[]{:S(2)}) collective-permute-start(f32[32,33]{1,0:T(8,128)S(1)} %add_bitcast_fusion), channel_id=1, source_target_pairs={{0,4},{4,8},{8,12},{12,0},{1,5},{5,9},{9,13},{13,1},{2,6},{6,10},{... | collective-permute-start | bytes 12680 | tf_op jit(solution)/shard_map/ppermute | solution.py:692
  203.0 16.5 %collective-permute-start.16 = (f32[32,33]{1,0:T(8,128)S(1)}, f32[32,33]{1,0:T(8,128)S(1)}, u32[]{:S(2)}, u32[]{:S(2)}) collective-permute-start(f32[32,33]{1,0:T(8,128)S(1)} %add_bitcast_fusion), channel_id=1, source_target_pairs={{0,8},{4,12},{8,0},{12,4},{1,9},{5,13},{9,1},{13,5},{2,10},{6,14},... | collective-permute-start | bytes 12680 | tf_op jit(solution)/shard_map/ppermute | solution.py:692
  204.5 15.0 %collective-permute-start.17 = (f32[32,33]{1,0:T(8,128)S(1)}, f32[32,33]{1,0:T(8,128)S(1)}, u32[]{:S(2)}, u32[]{:S(2)}) collective-permute-start(f32[32,33]{1,0:T(8,128)S(1)} %add_bitcast_fusion), channel_id=1, source_target_pairs={{0,12},{4,0},{8,4},{12,8},{1,13},{5,1},{9,5},{13,9},{2,14},{6,2},{... | collective-permute-start | bytes 12680 | tf_op jit(solution)/shard_map/ppermute | solution.py:692
  219.5 0.7 copy-start.19

commit v3 on v2

--- a/solution.py
+++ b/solution.py
@@ -18,7 +18,7 @@
 LANES = 128
 GROUP = 8
 
-FIELD_CB = 4
+FIELD_CB = 8
 PAD = 8
 ROWS = 4
 GRAD_CB = 4
@@ -161,13 +161,13 @@
 
 def x_inverse_in(me, ns, channels, ins, xih, xil, b_scr):
     rows = (MY // ns) * channels
+    h = jnp.concatenate([ref[...].reshape(rows, -1) for ref in ins], axis=0)
+    b = dot3(h, xih[0], xil[0])
     for k in range(ns):
         owner = lax.rem(me + ns - k, ns)
-        h = ins[k][...].reshape(rows, -1)
-        b = dot3(h, xih[0], xil[0])
+        at = pl.ds(pl.multiple_of(owner * rows, rows), rows)
         for i in range(b_scr.shape[0]):
-            at = pl.ds(pl.multiple_of(owner * rows, rows), rows)
-            b_scr[i, at, :] = b[:, i * LANES : (i + 1) * LANES]
+            b_scr[i, at, :] = b[k * rows : (k + 1) * rows, i * LANES : (i + 1) * LANES]
 
 
 def put_channel(scr, c, channels, value):
@@ -307,13 +307,17 @@
     def inverse(i, j):
         first = i * groups * width
         rows_of = [wide[:, first + g * width : first + (g + 1) * width] for g in range(groups)]
-        return dot(jnp.concatenate(rows_of, axis=0), zi[j])
+        point = [
+            jnp.concatenate([pre[0, i, g * GROUP + 2 * j + h] for h in range(2)], axis=1)
+            for g in range(groups)
+        ]
+        both = [jnp.concatenate(point, axis=0), jnp.concatenate(rows_of, axis=0)]
+        return dot(jnp.concatenate(both, axis=1), zi[j])
 
     def slope(i, j, v_all):
         for g in range(groups):
             x = g * GROUP + 2 * j
             v = v_all[g * NY : (g + 1) * NY]
-            v = v + jnp.concatenate([pre[0, i, x], pre[0, i, x + 1]], axis=1).astype(f32)
             w = jnp.concatenate([cot[0, i, x], cot[0, i, x + 1]], axis=1)
             d = (w.astype(f32) * gelu_slope(v)).astype(bf16)
             dpre[0, i, x] = d[:, :NZ]
@@ -510,6 +514,8 @@
 
     zf = jnp.asarray(z_forward_table())
     zi = jnp.asarray(z_inverse_table())
+    same = np.broadcast_to(bf(np.eye(2 * NZ)), (GROUP // 2, 2 * NZ, 2 * NZ))
+    zi_pre = jnp.asarray(np.concatenate([same, z_inverse_table()], axis=1))
     yf, yi = (jnp.asarray(t) for t in y_tables())
     xf = [jnp.asarray(t) for t in split_bf(x_forward_table(1.0))]
     xf_grad = [jnp.asarray(t) for t in split_bf(x_forward_table(SLOPE))]
@@ -586,7 +592,7 @@
                 in_specs=[some_channels(GRAD_CB)] * 2
                 + [chunk_spec] * ns
                 + xi_spec
-                + tables(yi, zi, zf, yf)
+                + tables(yi, zi_pre, zf, yf)
                 + xf_spec,
                 out_specs=[some_channels(GRAD_CB)] + [chunk_spec] * ns,
                 scratch_shapes=[b_scr, r_scr],
@@ -595,7 +601,7 @@
             compiler_params=params(),
             cost_estimate=cost(cells * 1024, cells * 6),
             name="gelu_gradient",
-        )(me_arr, pre, cotangent, *chunks, *xi_pre, yi, zi, zf, yf, *xf_grad)
+        )(me_arr, pre, cotangent, *chunks, *xi_pre, yi, zi_pre, zf, yf, *xf_grad)
 
     def pair_call(field, dpre, part=0, count=1):
         steps = rows // ROWS // count

time: 221 us -> 217 us (0.982)
  Pallas kernels: 187 us -> 183 us
    pallas_call x1, Pallas kernels: 52.5 us -> 50.2 us  [grad_call(): pl.pallas_call(functools.partial(grad_kernel, ns, channels), grid_spec=pl...]
  transfers between devices with their start and end apart: 18 -> 18, of which waited for: 0 -> 0; matrix products, arithmetic and copies ran while one was open for 0% -> 0% of each run, Pallas kernels for 50% -> 51%
where the time goes in v3:
time: 217 us; the launch traced here: 216 us
  Pallas kernels  183 us (84%)
  starting transfers between devices  26.9 us (12%)
  local copies, waits for them, and re-layouts  4.75 us (2%)
    pallas_call x1, Pallas kernels, grad_call(): pl.pallas_call(functools.partial(grad_kernel, ns, channels), grid_spec=pl...  50.2 us
    pallas_call x1, Pallas kernels, back_call(): pl.pallas_call(functools.partial(back_kernel, ns), grid_spec=pltpu.Prefet...  33.5 us
    pallas_call x1, Pallas kernels, point_call(): pl.pallas_call(point_kernel, grid=(rows // ROWS,), in_specs=[some_rows] +...  27.2 us
    ppermute x18, starting transfers between devices, swap(): got.append(lax.ppermute(chunks[k], axis, pairs))  26.9 us
    pallas_call x2, Pallas kernels, pair_call(): pl.pallas_call(pair_kernel, grid=(steps,), in_specs=[part_rows, part_rows...  26.8 us
    pallas_call x1, Pallas kernels, field_call(): pl.pallas_call(functools.partial(field_kernel, ns, channels), grid_spec=p...  16.6 us
    pallas_call x1, Pallas kernels, spec_call(): pl.pallas_call(functools.partial(outer_kernel, len(every)), grid=(own_ky,...  12.1 us
    pallas_call x1, Pallas kernels, weight_call(): pl.pallas_call(weight_kernel, grid=(2, own_ky), in_specs=[w_block], out_s...  9.64 us
  transfers between devices with their start and end apart: 18, of which 0 were waited for; matrix products, arithmetic and copies ran while one was open for 0% of the time, Pallas kernels for 51%

profile of v3, /device:TPU:0, one launch (start us, length us, event | category | flops | bytes accessed | tf_op | source)
XLA Modules:
  0.0 216.1 jit_solution(3075645809196562733)
XLA Ops:
  0.6 16.6 %field_spectrum.1 = (f32[4,32,256]{2,1,0:T(8,128)}, f32[4,32,256]{2,1,0:T(8,128)}, f32[4,32,256]{2,1,0:T(8,128)}, f32[4,32,256]{2,1,0:T(8,128)}) custom-call(s32[1]{0:T(128)} %bitcast.me_ref, bf16[1,32,32,128,128]{4,3,2,1,0:T(8,128)(2,1)} %field.7, bf16[1024,128]{1,0:T(8,128)(2,1)} %constant.40.clone.zf.rest_8_, bf16[32,128]{1,0:T(8,128)(2,1)} %constant.43.clone.yf.rest_9_, ...), custom_call_target="tpu_custom_call" | custom-call | flops 8589934592 | bytes 33554432 | tf_op jit(solution)/shard_map/field_spectrum/pallas_call | solution.py:547
  17.3 3.0 %collective-permute-start = (f32[4,32,256]{2,1,0:T(8,128)}, f32[4,32,256]{2,1,0:T(8,128)S(1)}, u32[]{:S(2)}, u32[]{:S(2)}) collective-permute-start(f32[4,32,256]{2,1,0:T(8,128)} %get-tuple-element.24), channel_id=1, source_target_pairs={{0,4},{4,8},{8,12},{12,0},{1,5},{5,9},{9,13},{13,1},{2,6},{6,10},{... | collective-permute-start | bytes 393224 | tf_op jit(solution)/shard_map/ppermute | solution.py:698
  20.3 2.6 %collective-permute-start.1 = (f32[4,32,256]{2,1,0:T(8,128)}, f32[4,32,256]{2,1,0:T(8,128)S(1)}, u32[]{:S(2)}, u32[]{:S(2)}) collective-permute-start(f32[4,32,256]{2,1,0:T(8,128)} %get-tuple-element.25), channel_id=1, source_target_pairs={{0,8},{4,12},{8,0},{12,4},{1,9},{5,13},{9,1},{13,5},{2,10},{6,14},... | collective-permute-start | bytes 393224 | tf_op jit(solution)/shard_map/ppermute | solution.py:698
  22.9 1.3 collective-permute-start.2
  24.2 9.6 %weight_layout.1.refs_4_ = bf16[2,32,4,32,128]{4,3,2,1,0:T(8,128)(2,1)} custom-call(bf16[2,16,32,32,32]{4,3,2,1,0:T(8,128)(2,1)} %weights.1), custom_call_target="tpu_custom_call" | custom-call | bytes 8388608 | tf_op jit(solution)/shard_map/weight_layout/pallas_call | solution.py:647
  33.9 0.0 collective-permute-done.refs_1_
  33.9 0.0 collective-permute-done.1.refs_2_
  33.9 0.6 copy-done.12
  34.5 0.1 copy-done.14
  34.6 0.1 copy-done.16
  34.6 3.2 %mix.1 = (f32[4,32,256]{2,1,0:T(8,128)}, f32[4,32,256]{2,1,0:T(8,128)}) custom-call(f32[4,32,256]{2,1,0:T(8,128)} %get-tuple-element.23.refs_0_, f32[4,32,256]{2,1,0:T(8,128)} %copy-done.12, f32[4,32,256]{2,1,0:T(8,128)} %copy-done.14, f32[4,32,256]{2,1,0:T(8,128)} %copy-done.16, bf16[2,32,4,32,128]{4,3,2,1,0:T(8,128)(2,1)} %weight_layout.1.refs_4_), custom_call_target="tpu_custom_call" | custom-call | tf_op jit(solution)/shard_map/mix/pallas_call | solution.py:576
  37.9 1.0 collective-permute-start.3
  38.9 1.7 collective-permute-start.4
  40.6 1.1 collective-permute-start.5
  41.7 27.2 %pointwise.1.pre = bf16[1,32,32,128,128]{4,3,2,1,0:T(8,128)(2,1)} custom-call(bf16[1,32,32,128,128]{4,3,2,1,0:T(8,128)(2,1)} %field.7, bf16[32,32]{1,0:T(8,128)(2,1)} %point.3, f32[1,32]{1,0:T(1,128)} %bitcast.10), custom_call_target="tpu_custom_call" | custom-call | flops 8589934592 | bytes 67108864 | tf_op jit(solution)/shard_map/pointwise/pallas_call | solution.py:563
  68.9 0.0 collective-permute-done.5.rest_3_
  68.9 0.6 copy-done.8
  69.5 0.1 copy-done.9
  69.6 0.6 copy-done.10
  70.2 50.2 %gelu_gradient.1 = (bf16[1,32,32,128,128]{4,3,2,1,0:T(8,128)(2,1)}, f32[4,32,256]{2,1,0:T(8,128)}, f32[4,32,256]{2,1,0:T(8,128)}, f32[4,32,256]{2,1,0:T(8,128)}, f32[4,32,256]{2,1,0:T(8,128)}) custom-call(s32[1]{0:T(128)} %bitcast.me_ref, bf16[1,32,32,128,128]{4,3,2,1,0:T(8,128)(2,1)} %pointwise.1.pre, bf16[1,32,32,128,128]{4,3,2,1,0:T(8,128)(2,1)} %cot.1, ...), custom_call_target="tpu_custom_call" | custom-call | flops 17179869184 | bytes 100663296 | tf_op jit(solution)/shard_map/gelu_gradient/pallas_call | solution.py:587
  120.4 1.1 collective-permute-start.6
  121.5 1.3 collective-permute-start.7
  122.8 2.8 %collective-permute-start.8 = (f32[4,32,256]{2,1,0:T(8,128)}, f32[4,32,256]{2,1,0:T(8,128)S(1)}, u32[]{:S(2)}, u32[]{:S(2)}) collective-permute-start(f32[4,32,256]{2,1,0:T(8,128)} %get-tuple-element.32), channel_id=1, source_target_pairs={{0,12},{4,0},{8,4},{12,8},{1,13},{5,1},{9,5},{13,9},{2,14},{6,2},{... | collective-permute-start | bytes 393224 | tf_op jit(solution)/shard_map/ppermute | solution.py:698
  125.6 13.4 %point_gradient.2 = f32[32,32]{1,0:T(8,128)} custom-call(bf16[1,32,32,128,128]{4,3,2,1,0:T(8,128)(2,1)} %field.7, bf16[1,32,32,128,128]{4,3,2,1,0:T(8,128)(2,1)} %get-tuple-element.36.dpre), custom_call_target="tpu_custom_call" | custom-call | flops 4294967296 | bytes 33554432 | tf_op jit(solution)/shard_map/point_gradient/pallas_call | solution.py:611
  139.0 0.0 collective-permute-done.7.refs_2_
  139.1 0.0 collective-permute-done.8.refs_3_
  139.1 0.6 copy-done.11
  139.7 0.0 copy-done.13
  139.7 0.0 copy-done.15
  139.8 3.4 %mix_adjoint.1 = (f32[4,32,256]{2,1,0:T(8,128)}, f32[4,32,256]{2,1,0:T(8,128)}) custom-call(f32[4,32,256]{2,1,0:T(8,128)} %get-tuple-element.29.refs_0_, f32[4,32,256]{2,1,0:T(8,128)} %copy-done.11, f32[4,32,256]{2,1,0:T(8,128)} %copy-done.13, f32[4,32,256]{2,1,0:T(8,128)} %copy-done.15, bf16[2,32,4,32,128]{4,3,2,1,0:T(8,128)(2,1)} %weight_layout.1.refs_4_), custom_call_target="tpu_custom_call" | custom-call | tf_op jit(solution)/shard_map/mix_adjoint/pallas_call | solution.py:576
  143.2 0.1 collective-permute-start.12
  143.2 0.8 collective-permute-start.13
  144.1 3.0 %collective-permute-start.14 = (f32[4,32,256]{2,1,0:T(8,128)}, f32[4,32,256]{2,1,0:T(8,128)S(1)}, u32[]{:S(2)}, u32[]{:S(2)}) collective-permute-start(f32[4,32,256]{2,1,0:T(8,128)} %get-tuple-element.35.rest_0_), channel_id=1, source_target_pairs={{0,12},{4,0},{8,4},{12,8},{1,13},{5,1},{9,5},{13,9},{2,14},{6,2},{... | collective-permute-start | bytes 393224 | tf_op jit(solution)/shard_map/ppermute | solution.py:698
  147.1 13.4 %point_gradient.3 = f32[32,32]{1,0:T(8,128)} custom-call(bf16[1,32,32,128,128]{4,3,2,1,0:T(8,128)(2,1)} %field.7, bf16[1,32,32,128,128]{4,3,2,1,0:T(8,128)(2,1)} %get-tuple-element.36.dpre), custom_call_target="tpu_custom_call" | custom-call | flops 4294967296 | bytes 33554432 | tf_op jit(solution)/shard_map/point_gradient/pallas_call | solution.py:611
  160.5 0.7 add.28
  161.2 0.1 fusion
  161.3 1.6 collective-permute-start.10
  162.9 0.5 collective-permute-start.9
  163.4 0.1 copy-done.5
  163.5 0.5 copy-done.6
  164.0 0.7 copy-done.7
  164.7 33.5 %field_gradient.1 = bf16[1,32,32,128,128]{4,3,2,1,0:T(8,128)(2,1)} custom-call(s32[1]{0:T(128)} %bitcast.me_ref, bf16[1,32,32,128,128]{4,3,2,1,0:T(8,128)(2,1)} %get-tuple-element.36.dpre, bf16[32,32]{1,0:T(8,128)(2,1)} %point.3, f32[4,32,256]{2,1,0:T(8,128)} %get-tuple-element.35.rest_0_, f32[4,32,256]{2,1,0:T(8,128)} %copy-done.5, ...), custom_call_target="tpu_custom_call" | custom-call | flops 17179869184 | bytes 67108864 | tf_op jit(solution)/shard_map/field_gradient/pallas_call | solution.py:624
  198.2 0.6 collective-permute-start.15
  198.9 1.5 collective-permute-start.16
  200.4 2.8 %collective-permute-start.17 = (f32[32,33]{1,0:T(8,128)S(1)}, f32[32,33]{1,0:T(8,128)S(1)}, u32[]{:S(2)}, u32[]{:S(2)}) collective-permute-start(f32[32,33]{1,0:T(8,128)S(1)} %add_bitcast_fusion), channel_id=1, source_target_pairs={{0,12},{4,0},{8,4},{12,8},{1,13},{5,1},{9,5},{13,9},{2,14},{6,2},{... | collective-permute-start | bytes 12680 | tf_op jit(solution)/shard_map/ppermute | solution.py:698
  203.2 12.1 %weight_gradient.1 = f32[2,16,32,32,32]{4,3,2,1,0:T(8,128)} custom-call(f32[9,32,256]{2,1,0:T(8,128)} %copy-done, f32[9,32,256]{2,1,0:T(8,128)} %copy-done.3, f32[9,32,256]{2,1,0:T(8,128)} %copy-done.1, f32[9,32,256]{2,1,0:T(8,128)} %copy-done.2, f32[9,32,256]{2,1,0:T(8,128)} %copy-done, f32[9,32,256]{2,1,0:T(8,128)} %copy-done.3, f32[9,32,256]{2,1,0:T(8,128)} %copy-done.1, ...), custom_call_target="tpu_custom_call" | custom-call | bytes 16777216 | tf_op jit(solution)/shard_map/weight_gradient/pallas_call | solution.py:664
  215.4 0.0 copy-start.19
  215.4 0.7 slice_reduce_fusion
  (45 shorter events, 0.1 us)
Async XLA Ops:
  17.3 16.6 %collective-permute-start = (f32[4,32,256]{2,1,0:T(8,128)}, f32[4,32,256]{2,1,0:T(8,128)S(1)}, u32[]{:S(2)}, u32[]{:S(2)}) collective-permute-start(f32[4,32,256]{2,1,0:T(8,128)} %get-tuple-element.24), channel_id=1, source_target_pairs={{0,4},{4,8},{8,12},{12,0},{1,5},{5,9},{9,13},{13,1},{2,6},{6,10},{... | collective-permute-start | bytes 393224 | tf_op jit(solution)/shard_map/ppermute | solution.py:698
  20.3 13.6 %collective-permute-start.1 = (f32[4,32,256]{2,1,0:T(8,128)}, f32[4,32,256]{2,1,0:T(8,128)S(1)}, u32[]{:S(2)}, u32[]{:S(2)}) collective-permute-start(f32[4,32,256]{2,1,0:T(8,128)} %get-tuple-element.25), channel_id=1, source_target_pairs={{0,8},{4,12},{8,0},{12,4},{1,9},{5,13},{9,1},{13,5},{2,10},{6,14},... | collective-permute-start | bytes 393224 | tf_op jit(solution)/shard_map/ppermute | solution.py:698
  22.9 11.0 %collective-permute-start.2 = (f32[4,32,256]{2,1,0:T(8,128)}, f32[4,32,256]{2,1,0:T(8,128)S(1)}, u32[]{:S(2)}, u32[]{:S(2)}) collective-permute-start(f32[4,32,256]{2,1,0:T(8,128)} %get-tuple-element.26), channel_id=1, source_target_pairs={{0,12},{4,0},{8,4},{12,8},{1,13},{5,1},{9,5},{13,9},{2,14},{6,2},{... | collective-permute-start | bytes 393224 | tf_op jit(solution)/shard_map/ppermute | solution.py:698
  33.9 0.6 copy-start.12
  33.9 0.7 copy-start.14
  33.9 0.7 copy-start.16
  37.9 31.0 %collective-permute-start.3 = (f32[4,32,256]{2,1,0:T(8,128)}, f32[4,32,256]{2,1,0:T(8,128)S(1)}, u32[]{:S(2)}, u32[]{:S(2)}) collective-permute-start(f32[4,32,256]{2,1,0:T(8,128)} %get-tuple-element.28.rest_0_), channel_id=1, source_target_pairs={{0,4},{4,8},{8,12},{12,0},{1,5},{5,9},{9,13},{13,1},{2,6},{6,10},{... | collective-permute-start | bytes 393224 | tf_op jit(solution)/shard_map/ppermute | solution.py:698
  38.9 30.0 %collective-permute-start.4 = (f32[4,32,256]{2,1,0:T(8,128)}, f32[4,32,256]{2,1,0:T(8,128)S(1)}, u32[]{:S(2)}, u32[]{:S(2)}) collective-permute-start(f32[4,32,256]{2,1,0:T(8,128)} %get-tuple-element.28.rest_0_), channel_id=1, source_target_pairs={{0,8},{4,12},{8,0},{12,4},{1,9},{5,13},{9,1},{13,5},{2,10},{6,14},... | collective-permute-start | bytes 393224 | tf_op jit(solution)/shard_map/ppermute | solution.py:698
  40.6 28.3 %collective-permute-start.5 = (f32[4,32,256]{2,1,0:T(8,128)}, f32[4,32,256]{2,1,0:T(8,128)S(1)}, u32[]{:S(2)}, u32[]{:S(2)}) collective-permute-start(f32[4,32,256]{2,1,0:T(8,128)} %get-tuple-element.28.rest_0_), channel_id=1, source_target_pairs={{0,12},{4,0},{8,4},{12,8},{1,13},{5,1},{9,5},{13,9},{2,14},{6,2},{... | collective-permute-start | bytes 393224 | tf_op jit(solution)/shard_map/ppermute | solution.py:698
  68.9 0.6 copy-start.8
  68.9 0.7 copy-start.9
  69.6 0.6 copy-start.10
  120.4 18.6 %collective-permute-start.6 = (f32[4,32,256]{2,1,0:T(8,128)}, f32[4,32,256]{2,1,0:T(8,128)S(1)}, u32[]{:S(2)}, u32[]{:S(2)}) collective-permute-start(f32[4,32,256]{2,1,0:T(8,128)} %get-tuple-element.30), channel_id=1, source_target_pairs={{0,4},{4,8},{8,12},{12,0},{1,5},{5,9},{9,13},{13,1},{2,6},{6,10},{... | collective-permute-start | bytes 393224 | tf_op jit(solution)/shard_map/ppermute | solution.py:698
  121.5 17.5 %collective-permute-start.7 = (f32[4,32,256]{2,1,0:T(8,128)}, f32[4,32,256]{2,1,0:T(8,128)S(1)}, u32[]{:S(2)}, u32[]{:S(2)}) collective-permute-start(f32[4,32,256]{2,1,0:T(8,128)} %get-tuple-element.31), channel_id=1, source_target_pairs={{0,8},{4,12},{8,0},{12,4},{1,9},{5,13},{9,1},{13,5},{2,10},{6,14},... | collective-permute-start | bytes 393224 | tf_op jit(solution)/shard_map/ppermute | solution.py:698
  122.8 16.3 %collective-permute-start.8 = (f32[4,32,256]{2,1,0:T(8,128)}, f32[4,32,256]{2,1,0:T(8,128)S(1)}, u32[]{:S(2)}, u32[]{:S(2)}) collective-permute-start(f32[4,32,256]{2,1,0:T(8,128)} %get-tuple-element.32), channel_id=1, source_target_pairs={{0,12},{4,0},{8,4},{12,8},{1,13},{5,1},{9,5},{13,9},{2,14},{6,2},{... | collective-permute-start | bytes 393224 | tf_op jit(solution)/shard_map/ppermute | solution.py:698
  139.0 0.7 copy-start.11
  139.1 0.7 copy-start.13
  139.1 0.7 copy-start.15
  143.2 17.3 %copy-start.18 = (f32[32,32]{1,0:T(8,128)S(1)}, f32[32,32]{1,0:T(8,128)}, u32[]{:S(2)}) copy-start(f32[32,32]{1,0:T(8,128)} %point_gradient.2) | copy-start | bytes 12292
  143.2 18.0 %copy-start.4 = (f32[4,32,256]{2,1,0:T(8,128)S(1)}, f32[4,32,256]{2,1,0:T(8,128)}, u32[]{:S(2)}) copy-start(f32[4,32,256]{2,1,0:T(8,128)} %get-tuple-element.33) | copy-start | bytes 393220
  143.2 18.1 %copy-start.17 = (f32[4,32,256]{2,1,0:T(8,128)S(1)}, f32[4,32,256]{2,1,0:T(8,128)}, u32[]{:S(2)}) copy-start(f32[4,32,256]{2,1,0:T(8,128)} %get-tuple-element.27) | copy-start | bytes 393220
  143.2 19.7 %collective-permute-start.12 = (f32[4,32,256]{2,1,0:T(8,128)}, f32[4,32,256]{2,1,0:T(8,128)S(1)}, u32[]{:S(2)}, u32[]{:S(2)}) collective-permute-start(f32[4,32,256]{2,1,0:T(8,128)} %get-tuple-element.35.rest_0_), channel_id=1, source_target_pairs={{0,4},{4,8},{8,12},{12,0},{1,5},{5,9},{9,13},{13,1},{2,6},{6,10},{... | collective-permute-start | bytes 393224 | tf_op jit(solution)/shard_map/ppermute | solution.py:698
  143.2 20.2 %collective-permute-start.13 = (f32[4,32,256]{2,1,0:T(8,128)}, f32[4,32,256]{2,1,0:T(8,128)S(1)}, u32[]{:S(2)}, u32[]{:S(2)}) collective-permute-start(f32[4,32,256]{2,1,0:T(8,128)} %get-tuple-element.35.rest_0_), channel_id=1, source_target_pairs={{0,8},{4,12},{8,0},{12,4},{1,9},{5,13},{9,1},{13,5},{2,10},{6,14},... | collective-permute-start | bytes 393224 | tf_op jit(solution)/shard_map/ppermute | solution.py:698
  144.1 19.3 %collective-permute-start.14 = (f32[4,32,256]{2,1,0:T(8,128)}, f32[4,32,256]{2,1,0:T(8,128)S(1)}, u32[]{:S(2)}, u32[]{:S(2)}) collective-permute-start(f32[4,32,256]{2,1,0:T(8,128)} %get-tuple-element.35.rest_0_), channel_id=1, source_target_pairs={{0,12},{4,0},{8,4},{12,8},{1,13},{5,1},{9,5},{13,9},{2,14},{6,2},{... | collective-permute-start | bytes 393224 | tf_op jit(solution)/shard_map/ppermute | solution.py:698
  161.3 36.9 %copy-start = (f32[9,32,256]{2,1,0:T(8,128)}, f32[9,32,256]{2,1,0:T(8,128)S(1)}, u32[]{:S(2)}) copy-start(f32[9,32,256]{2,1,0:T(8,128)S(1)} %pad_maximum_fusion.refs_0_.refs_4_) | copy-start | bytes 884740
  161.3 36.8 %collective-permute-start.10 = (f32[9,32,256]{2,1,0:T(8,128)S(1)}, f32[9,32,256]{2,1,0:T(8,128)S(1)}, u32[]{:S(2)}, u32[]{:S(2)}) collective-permute-start(f32[9,32,256]{2,1,0:T(8,128)S(1)} %pad_maximum_fusion.refs_0_.refs_4_), channel_id=1, source_target_pairs={{0,2},{1,3},{2,0},{3,1},{4,6},{5,7},{6,4},{7,5},{8,10},{9,11},{10,... | collective-permute-start | bytes 884744 | tf_op jit(solution)/shard_map/ppermute | solution.py:698
  162.9 35.3 %collective-permute-start.11 = (f32[9,32,256]{2,1,0:T(8,128)S(1)}, f32[9,32,256]{2,1,0:T(8,128)S(1)}, u32[]{:S(2)}, u32[]{:S(2)}) collective-permute-start(f32[9,32,256]{2,1,0:T(8,128)S(1)} %pad_maximum_fusion.refs_0_.refs_4_), channel_id=1, source_target_pairs={{0,3},{1,0},{2,1},{3,2},{4,7},{5,4},{6,5},{7,6},{8,11},{9,8},{10,9... | collective-permute-start | bytes 884744 | tf_op jit(solution)/shard_map/ppermute | solution.py:698
  162.9 0.7 copy-start.5
  162.9 35.3 %collective-permute-start.9 = (f32[9,32,256]{2,1,0:T(8,128)S(1)}, f32[9,32,256]{2,1,0:T(8,128)S(1)}, u32[]{:S(2)}, u32[]{:S(2)}) collective-permute-start(f32[9,32,256]{2,1,0:T(8,128)S(1)} %pad_maximum_fusion.refs_0_.refs_4_), channel_id=1, source_target_pairs={{0,1},{1,2},{2,3},{3,0},{4,5},{5,6},{6,7},{7,4},{8,9},{9,10},{10,1... | collective-permute-start | bytes 884744 | tf_op jit(solution)/shard_map/ppermute | solution.py:698
  163.4 0.6 copy-start.6
  164.0 0.7 copy-start.7
  198.2 5.1 %copy-start.1 = (f32[9,32,256]{2,1,0:T(8,128)}, f32[9,32,256]{2,1,0:T(8,128)S(1)}, u32[]{:S(2)}) copy-start(f32[9,32,256]{2,1,0:T(8,128)S(1)} %collective-permute-done.10.refs_2_.refs_6_) | copy-start | bytes 884740
  198.2 5.1 %copy-start.2 = (f32[9,32,256]{2,1,0:T(8,128)}, f32[9,32,256]{2,1,0:T(8,128)S(1)}, u32[]{:S(2)}) copy-start(f32[9,32,256]{2,1,0:T(8,128)S(1)} %collective-permute-done.11.refs_3_.refs_7_) | copy-start | bytes 884740
  198.2 5.0 %copy-start.3 = (f32[9,32,256]{2,1,0:T(8,128)}, f32[9,32,256]{2,1,0:T(8,128)S(1)}, u32[]{:S(2)}) copy-start(f32[9,32,256]{2,1,0:T(8,128)S(1)} %collective-permute-done.9.refs_1_.refs_5_) | copy-start | bytes 884740
  198.2 17.1 %collective-permute-start.15 = (f32[32,33]{1,0:T(8,128)S(1)}, f32[32,33]{1,0:T(8,128)S(1)}, u32[]{:S(2)}, u32[]{:S(2)}) collective-permute-start(f32[32,33]{1,0:T(8,128)S(1)} %add_bitcast_fusion), channel_id=1, source_target_pairs={{0,4},{4,8},{8,12},{12,0},{1,5},{5,9},{9,13},{13,1},{2,6},{6,10},{... | collective-permute-start | bytes 12680 | tf_op jit(solution)/shard_map/ppermute | solution.py:698
  198.9 16.5 %collective-permute-start.16 = (f32[32,33]{1,0:T(8,128)S(1)}, f32[32,33]{1,0:T(8,128)S(1)}, u32[]{:S(2)}, u32[]{:S(2)}) collective-permute-start(f32[32,33]{1,0:T(8,128)S(1)} %add_bitcast_fusion), channel_id=1, source_target_pairs={{0,8},{4,12},{8,0},{12,4},{1,9},{5,13},{9,1},{13,5},{2,10},{6,14},... | collective-permute-start | bytes 12680 | tf_op jit(solution)/shard_map/ppermute | solution.py:698
  200.4 15.0 %collective-permute-start.17 = (f32[32,33]{1,0:T(8,128)S(1)}, f32[32,33]{1,0:T(8,128)S(1)}, u32[]{:S(2)}, u32[]{:S(2)}) collective-permute-start(f32[32,33]{1,0:T(8,128)S(1)} %add_bitcast_fusion), channel_id=1, source_target_pairs={{0,12},{4,0},{8,4},{12,8},{1,13},{5,1},{9,5},{13,9},{2,14},{6,2},{... | collective-permute-start | bytes 12680 | tf_op jit(solution)/shard_map/ppermute | solution.py:698
  215.4 0.7 copy-start.19

commit v4 on v3

--- a/solution.py
+++ b/solution.py
@@ -20,7 +20,8 @@
 
 FIELD_CB = 8
 PAD = 8
-ROWS = 4
+ROWS = 8
+PAIR_ROWS = 4
 GRAD_CB = 4
 
 f32 = jnp.float32
@@ -304,30 +305,33 @@
     )
     pairs = GROUP // 2
 
-    def inverse(i, j):
-        first = i * groups * width
-        rows_of = [wide[:, first + g * width : first + (g + 1) * width] for g in range(groups)]
-        point = [
-            jnp.concatenate([pre[0, i, g * GROUP + 2 * j + h] for h in range(2)], axis=1)
-            for g in range(groups)
-        ]
-        both = [jnp.concatenate(point, axis=0), jnp.concatenate(rows_of, axis=0)]
-        return dot(jnp.concatenate(both, axis=1), zi[j])
-
-    def slope(i, j, v_all):
-        for g in range(groups):
+    def inverse(i, j, part):
+        both = []
+        for g in part:
+            at = (i * groups + g) * width
             x = g * GROUP + 2 * j
-            v = v_all[g * NY : (g + 1) * NY]
+            both.append(
+                jnp.concatenate([pre[0, i, x], pre[0, i, x + 1], wide[:, at : at + width]], axis=1)
+            )
+        return dot(jnp.concatenate(both, axis=0), zi[j])
+
+    def slope(i, j, part, v_all):
+        for n, g in enumerate(part):
+            x = g * GROUP + 2 * j
+            v = v_all[n * NY : (n + 1) * NY]
             w = jnp.concatenate([cot[0, i, x], cot[0, i, x + 1]], axis=1)
             d = (w.astype(f32) * gelu_slope(v)).astype(bf16)
             dpre[0, i, x] = d[:, :NZ]
             dpre[0, i, x + 1] = d[:, NZ:]
 
+    together = 1
     done = []
     for i in range(GRAD_CB + 1):
         for j in range(pairs):
             if i < GRAD_CB:
-                slope(i, j, inverse(i, j))
+                for g in range(0, groups, together):
+                    part = range(g, g + together)
+                    slope(i, j, part, inverse(i, j, part))
             if i and j == 0:
                 done += z_forward([dpre[0, i - 1, x] for x in range(rows)], zf[...])
     spectra = y_forward(done, yf[...])
@@ -604,9 +608,9 @@
         )(me_arr, pre, cotangent, *chunks, *xi_pre, yi, zi_pre, zf, yf, *xf_grad)
 
     def pair_call(field, dpre, part=0, count=1):
-        steps = rows // ROWS // count
+        steps = rows // PAIR_ROWS // count
         part_rows = pl.BlockSpec(
-            (1, channels, ROWS, NY, NZ), lambda x: (0, 0, x + part * steps, 0, 0)
+            (1, channels, PAIR_ROWS, NY, NZ), lambda x: (0, 0, x + part * steps, 0, 0)
         )
         return pl.pallas_call(
             pair_kernel,

time: 217 us -> 211 us (0.972)
  Pallas kernels: 183 us -> 177 us
    pallas_call x1, Pallas kernels: 27.2 us -> 24.5 us  [point_call(): pl.pallas_call(point_kernel, grid=(rows // ROWS,), in_specs=[some_rows] +...]
    pallas_call x1, Pallas kernels: 33.5 us -> 30.9 us  [back_call(): pl.pallas_call(functools.partial(back_kernel, ns), grid_spec=pltpu.Prefet...]
  transfers between devices with their start and end apart: 18 -> 18, of which waited for: 0 -> 0; matrix products, arithmetic and copies ran while one was open for 0% -> 0% of each run, Pallas kernels for 51% -> 49%
where the time goes in v4:
time: 211 us
  Pallas kernels  177 us (84%)
  starting transfers between devices  27.1 us (13%)
  local copies, waits for them, and re-layouts  4.75 us (2%)
    pallas_call x1, Pallas kernels, grad_call(): pl.pallas_call(functools.partial(grad_kernel, ns, channels), grid_spec=pl...  49.8 us
    pallas_call x1, Pallas kernels, back_call(): pl.pallas_call(functools.partial(back_kernel, ns), grid_spec=pltpu.Prefet...  30.9 us
    ppermute x18, starting transfers between devices, swap(): got.append(lax.ppermute(chunks[k], axis, pairs))  27.1 us
    pallas_call x2, Pallas kernels, pair_call(): pl.pallas_call(pair_kernel, grid=(steps,), in_specs=[part_rows, part_rows...  26.8 us
    pallas_call x1, Pallas kernels, point_call(): pl.pallas_call(point_kernel, grid=(rows // ROWS,), in_specs=[some_rows] +...  24.5 us
    pallas_call x1, Pallas kernels, field_call(): pl.pallas_call(functools.partial(field_kernel, ns, channels), grid_spec=p...  16.6 us
    pallas_call x1, Pallas kernels, spec_call(): pl.pallas_call(functools.partial(outer_kernel, len(every)), grid=(own_ky,...  12.1 us
    pallas_call x1, Pallas kernels, weight_call(): pl.pallas_call(weight_kernel, grid=(2, own_ky), in_specs=[w_block], out_s...  9.64 us
  transfers between devices with their start and end apart: 18, of which 0 were waited for; matrix products, arithmetic and copies ran while one was open for 0% of the time, Pallas kernels for 49%

profile of v4, /device:TPU:0, one launch (start us, length us, event | category | flops | bytes accessed | tf_op | source)
XLA Modules:
  0.0 210.6 jit_solution(7521194510656416949)
XLA Ops:
  0.6 16.6 %field_spectrum.1 = (f32[4,32,256]{2,1,0:T(8,128)}, f32[4,32,256]{2,1,0:T(8,128)}, f32[4,32,256]{2,1,0:T(8,128)}, f32[4,32,256]{2,1,0:T(8,128)}) custom-call(s32[1]{0:T(128)} %bitcast.me_ref, bf16[1,32,32,128,128]{4,3,2,1,0:T(8,128)(2,1)} %field.7, bf16[1024,128]{1,0:T(8,128)(2,1)} %constant.40.clone.zf.rest_8_, bf16[32,128]{1,0:T(8,128)(2,1)} %constant.43.clone.yf.rest_9_, ...), custom_call_target="tpu_custom_call" | custom-call | flops 8589934592 | bytes 33554432 | tf_op jit(solution)/shard_map/field_spectrum/pallas_call | solution.py:551
  17.3 3.0 %collective-permute-start = (f32[4,32,256]{2,1,0:T(8,128)}, f32[4,32,256]{2,1,0:T(8,128)S(1)}, u32[]{:S(2)}, u32[]{:S(2)}) collective-permute-start(f32[4,32,256]{2,1,0:T(8,128)} %get-tuple-element.24), channel_id=1, source_target_pairs={{0,4},{4,8},{8,12},{12,0},{1,5},{5,9},{9,13},{13,1},{2,6},{6,10},{... | collective-permute-start | bytes 393224 | tf_op jit(solution)/shard_map/ppermute | solution.py:702
  20.3 2.6 %collective-permute-start.1 = (f32[4,32,256]{2,1,0:T(8,128)}, f32[4,32,256]{2,1,0:T(8,128)S(1)}, u32[]{:S(2)}, u32[]{:S(2)}) collective-permute-start(f32[4,32,256]{2,1,0:T(8,128)} %get-tuple-element.25), channel_id=1, source_target_pairs={{0,8},{4,12},{8,0},{12,4},{1,9},{5,13},{9,1},{13,5},{2,10},{6,14},... | collective-permute-start | bytes 393224 | tf_op jit(solution)/shard_map/ppermute | solution.py:702
  22.9 1.3 collective-permute-start.2
  24.2 9.6 %weight_layout.1.refs_4_ = bf16[2,32,4,32,128]{4,3,2,1,0:T(8,128)(2,1)} custom-call(bf16[2,16,32,32,32]{4,3,2,1,0:T(8,128)(2,1)} %weights.1), custom_call_target="tpu_custom_call" | custom-call | bytes 8388608 | tf_op jit(solution)/shard_map/weight_layout/pallas_call | solution.py:651
  33.9 0.0 collective-permute-done.refs_1_
  33.9 0.0 collective-permute-done.1.refs_2_
  33.9 0.6 copy-done.12
  34.5 0.1 copy-done.14
  34.6 0.1 copy-done.16
  34.6 3.2 %mix.1 = (f32[4,32,256]{2,1,0:T(8,128)}, f32[4,32,256]{2,1,0:T(8,128)}) custom-call(f32[4,32,256]{2,1,0:T(8,128)} %get-tuple-element.23.refs_0_, f32[4,32,256]{2,1,0:T(8,128)} %copy-done.12, f32[4,32,256]{2,1,0:T(8,128)} %copy-done.14, f32[4,32,256]{2,1,0:T(8,128)} %copy-done.16, bf16[2,32,4,32,128]{4,3,2,1,0:T(8,128)(2,1)} %weight_layout.1.refs_4_), custom_call_target="tpu_custom_call" | custom-call | tf_op jit(solution)/shard_map/mix/pallas_call | solution.py:580
  37.9 1.0 collective-permute-start.3
  38.9 1.7 collective-permute-start.4
  40.6 1.1 collective-permute-start.5
  41.7 24.5 %pointwise.1.pre = bf16[1,32,32,128,128]{4,3,2,1,0:T(8,128)(2,1)} custom-call(bf16[1,32,32,128,128]{4,3,2,1,0:T(8,128)(2,1)} %field.7, bf16[32,32]{1,0:T(8,128)(2,1)} %point.3, f32[1,32]{1,0:T(1,128)} %bitcast.10), custom_call_target="tpu_custom_call" | custom-call | flops 8589934592 | bytes 67108864 | tf_op jit(solution)/shard_map/pointwise/pallas_call | solution.py:567
  66.2 0.0 collective-permute-done.3.rest_1_
  66.2 0.0 collective-permute-done.5.rest_3_
  66.2 0.6 copy-done.8
  66.8 0.1 copy-done.9
  66.9 0.6 copy-done.10
  67.5 49.8 %gelu_gradient.1 = (bf16[1,32,32,128,128]{4,3,2,1,0:T(8,128)(2,1)}, f32[4,32,256]{2,1,0:T(8,128)}, f32[4,32,256]{2,1,0:T(8,128)}, f32[4,32,256]{2,1,0:T(8,128)}, f32[4,32,256]{2,1,0:T(8,128)}) custom-call(s32[1]{0:T(128)} %bitcast.me_ref, bf16[1,32,32,128,128]{4,3,2,1,0:T(8,128)(2,1)} %pointwise.1.pre, bf16[1,32,32,128,128]{4,3,2,1,0:T(8,128)(2,1)} %cot.1, ...), custom_call_target="tpu_custom_call" | custom-call | flops 17179869184 | bytes 100663296 | tf_op jit(solution)/shard_map/gelu_gradient/pallas_call | solution.py:591
  117.3 1.1 collective-permute-start.6
  118.4 1.3 collective-permute-start.7
  119.6 2.8 %collective-permute-start.8 = (f32[4,32,256]{2,1,0:T(8,128)}, f32[4,32,256]{2,1,0:T(8,128)S(1)}, u32[]{:S(2)}, u32[]{:S(2)}) collective-permute-start(f32[4,32,256]{2,1,0:T(8,128)} %get-tuple-element.32), channel_id=1, source_target_pairs={{0,12},{4,0},{8,4},{12,8},{1,13},{5,1},{9,5},{13,9},{2,14},{6,2},{... | collective-permute-start | bytes 393224 | tf_op jit(solution)/shard_map/ppermute | solution.py:702
  122.5 13.4 %point_gradient.2 = f32[32,32]{1,0:T(8,128)} custom-call(bf16[1,32,32,128,128]{4,3,2,1,0:T(8,128)(2,1)} %field.7, bf16[1,32,32,128,128]{4,3,2,1,0:T(8,128)(2,1)} %get-tuple-element.36.dpre), custom_call_target="tpu_custom_call" | custom-call | flops 4294967296 | bytes 33554432 | tf_op jit(solution)/shard_map/point_gradient/pallas_call | solution.py:615
  135.9 0.0 collective-permute-done.6.refs_1_
  135.9 0.6 copy-done.11
  136.5 0.0 copy-done.13
  136.6 0.0 copy-done.15
  136.6 3.4 %mix_adjoint.1 = (f32[4,32,256]{2,1,0:T(8,128)}, f32[4,32,256]{2,1,0:T(8,128)}) custom-call(f32[4,32,256]{2,1,0:T(8,128)} %get-tuple-element.29.refs_0_, f32[4,32,256]{2,1,0:T(8,128)} %copy-done.11, f32[4,32,256]{2,1,0:T(8,128)} %copy-done.13, f32[4,32,256]{2,1,0:T(8,128)} %copy-done.15, bf16[2,32,4,32,128]{4,3,2,1,0:T(8,128)(2,1)} %weight_layout.1.refs_4_), custom_call_target="tpu_custom_call" | custom-call | tf_op jit(solution)/shard_map/mix_adjoint/pallas_call | solution.py:580
  140.0 0.3 collective-permute-start.12
  140.3 0.8 collective-permute-start.13
  141.1 3.0 %collective-permute-start.14 = (f32[4,32,256]{2,1,0:T(8,128)}, f32[4,32,256]{2,1,0:T(8,128)S(1)}, u32[]{:S(2)}, u32[]{:S(2)}) collective-permute-start(f32[4,32,256]{2,1,0:T(8,128)} %get-tuple-element.35.rest_0_), channel_id=1, source_target_pairs={{0,12},{4,0},{8,4},{12,8},{1,13},{5,1},{9,5},{13,9},{2,14},{6,2},{... | collective-permute-start | bytes 393224 | tf_op jit(solution)/shard_map/ppermute | solution.py:702
  144.1 13.4 %point_gradient.3 = f32[32,32]{1,0:T(8,128)} custom-call(bf16[1,32,32,128,128]{4,3,2,1,0:T(8,128)(2,1)} %field.7, bf16[1,32,32,128,128]{4,3,2,1,0:T(8,128)(2,1)} %get-tuple-element.36.dpre), custom_call_target="tpu_custom_call" | custom-call | flops 4294967296 | bytes 33554432 | tf_op jit(solution)/shard_map/point_gradient/pallas_call | solution.py:615
  157.5 0.7 add.28
  158.3 0.1 fusion
  158.4 1.6 collective-permute-start.10
  160.0 0.5 collective-permute-start.9
  160.5 0.1 copy-done.5
  160.6 0.5 copy-done.6
  161.1 0.7 copy-done.7
  161.8 30.9 %field_gradient.1 = bf16[1,32,32,128,128]{4,3,2,1,0:T(8,128)(2,1)} custom-call(s32[1]{0:T(128)} %bitcast.me_ref, bf16[1,32,32,128,128]{4,3,2,1,0:T(8,128)(2,1)} %get-tuple-element.36.dpre, bf16[32,32]{1,0:T(8,128)(2,1)} %point.3, f32[4,32,256]{2,1,0:T(8,128)} %get-tuple-element.35.rest_0_, f32[4,32,256]{2,1,0:T(8,128)} %copy-done.5, ...), custom_call_target="tpu_custom_call" | custom-call | flops 17179869184 | bytes 67108864 | tf_op jit(solution)/shard_map/field_gradient/pallas_call | solution.py:628
  192.7 0.6 collective-permute-start.15
  193.3 1.5 collective-permute-start.16
  194.9 2.8 %collective-permute-start.17 = (f32[32,33]{1,0:T(8,128)S(1)}, f32[32,33]{1,0:T(8,128)S(1)}, u32[]{:S(2)}, u32[]{:S(2)}) collective-permute-start(f32[32,33]{1,0:T(8,128)S(1)} %add_bitcast_fusion), channel_id=1, source_target_pairs={{0,12},{4,0},{8,4},{12,8},{1,13},{5,1},{9,5},{13,9},{2,14},{6,2},{... | collective-permute-start | bytes 12680 | tf_op jit(solution)/shard_map/ppermute | solution.py:702
  197.7 12.1 %weight_gradient.1 = f32[2,16,32,32,32]{4,3,2,1,0:T(8,128)} custom-call(f32[9,32,256]{2,1,0:T(8,128)} %copy-done, f32[9,32,256]{2,1,0:T(8,128)} %copy-done.3, f32[9,32,256]{2,1,0:T(8,128)} %copy-done.1, f32[9,32,256]{2,1,0:T(8,128)} %copy-done.2, f32[9,32,256]{2,1,0:T(8,128)} %copy-done, f32[9,32,256]{2,1,0:T(8,128)} %copy-done.3, f32[9,32,256]{2,1,0:T(8,128)} %copy-done.1, ...), custom_call_target="tpu_custom_call" | custom-call | bytes 16777216 | tf_op jit(solution)/shard_map/weight_gradient/pallas_call | solution.py:668
  209.9 0.0 copy-start.19
  209.9 0.7 slice_reduce_fusion
  (45 shorter events, 0.1 us)
Async XLA Ops:
  17.3 16.6 %collective-permute-start = (f32[4,32,256]{2,1,0:T(8,128)}, f32[4,32,256]{2,1,0:T(8,128)S(1)}, u32[]{:S(2)}, u32[]{:S(2)}) collective-permute-start(f32[4,32,256]{2,1,0:T(8,128)} %get-tuple-element.24), channel_id=1, source_target_pairs={{0,4},{4,8},{8,12},{12,0},{1,5},{5,9},{9,13},{13,1},{2,6},{6,10},{... | collective-permute-start | bytes 393224 | tf_op jit(solution)/shard_map/ppermute | solution.py:702
  20.3 13.6 %collective-permute-start.1 = (f32[4,32,256]{2,1,0:T(8,128)}, f32[4,32,256]{2,1,0:T(8,128)S(1)}, u32[]{:S(2)}, u32[]{:S(2)}) collective-permute-start(f32[4,32,256]{2,1,0:T(8,128)} %get-tuple-element.25), channel_id=1, source_target_pairs={{0,8},{4,12},{8,0},{12,4},{1,9},{5,13},{9,1},{13,5},{2,10},{6,14},... | collective-permute-start | bytes 393224 | tf_op jit(solution)/shard_map/ppermute | solution.py:702
  22.9 11.0 %collective-permute-start.2 = (f32[4,32,256]{2,1,0:T(8,128)}, f32[4,32,256]{2,1,0:T(8,128)S(1)}, u32[]{:S(2)}, u32[]{:S(2)}) collective-permute-start(f32[4,32,256]{2,1,0:T(8,128)} %get-tuple-element.26), channel_id=1, source_target_pairs={{0,12},{4,0},{8,4},{12,8},{1,13},{5,1},{9,5},{13,9},{2,14},{6,2},{... | collective-permute-start | bytes 393224 | tf_op jit(solution)/shard_map/ppermute | solution.py:702
  33.9 0.6 copy-start.12
  33.9 0.7 copy-start.14
  33.9 0.7 copy-start.16
  37.9 28.3 %collective-permute-start.3 = (f32[4,32,256]{2,1,0:T(8,128)}, f32[4,32,256]{2,1,0:T(8,128)S(1)}, u32[]{:S(2)}, u32[]{:S(2)}) collective-permute-start(f32[4,32,256]{2,1,0:T(8,128)} %get-tuple-element.28.rest_0_), channel_id=1, source_target_pairs={{0,4},{4,8},{8,12},{12,0},{1,5},{5,9},{9,13},{13,1},{2,6},{6,10},{... | collective-permute-start | bytes 393224 | tf_op jit(solution)/shard_map/ppermute | solution.py:702
  38.9 27.3 %collective-permute-start.4 = (f32[4,32,256]{2,1,0:T(8,128)}, f32[4,32,256]{2,1,0:T(8,128)S(1)}, u32[]{:S(2)}, u32[]{:S(2)}) collective-permute-start(f32[4,32,256]{2,1,0:T(8,128)} %get-tuple-element.28.rest_0_), channel_id=1, source_target_pairs={{0,8},{4,12},{8,0},{12,4},{1,9},{5,13},{9,1},{13,5},{2,10},{6,14},... | collective-permute-start | bytes 393224 | tf_op jit(solution)/shard_map/ppermute | solution.py:702
  40.6 25.6 %collective-permute-start.5 = (f32[4,32,256]{2,1,0:T(8,128)}, f32[4,32,256]{2,1,0:T(8,128)S(1)}, u32[]{:S(2)}, u32[]{:S(2)}) collective-permute-start(f32[4,32,256]{2,1,0:T(8,128)} %get-tuple-element.28.rest_0_), channel_id=1, source_target_pairs={{0,12},{4,0},{8,4},{12,8},{1,13},{5,1},{9,5},{13,9},{2,14},{6,2},{... | collective-permute-start | bytes 393224 | tf_op jit(solution)/shard_map/ppermute | solution.py:702
  66.2 0.6 copy-start.8
  66.2 0.7 copy-start.9
  66.9 0.6 copy-start.10
  117.3 18.6 %collective-permute-start.6 = (f32[4,32,256]{2,1,0:T(8,128)}, f32[4,32,256]{2,1,0:T(8,128)S(1)}, u32[]{:S(2)}, u32[]{:S(2)}) collective-permute-start(f32[4,32,256]{2,1,0:T(8,128)} %get-tuple-element.30), channel_id=1, source_target_pairs={{0,4},{4,8},{8,12},{12,0},{1,5},{5,9},{9,13},{13,1},{2,6},{6,10},{... | collective-permute-start | bytes 393224 | tf_op jit(solution)/shard_map/ppermute | solution.py:702
  118.4 17.5 %collective-permute-start.7 = (f32[4,32,256]{2,1,0:T(8,128)}, f32[4,32,256]{2,1,0:T(8,128)S(1)}, u32[]{:S(2)}, u32[]{:S(2)}) collective-permute-start(f32[4,32,256]{2,1,0:T(8,128)} %get-tuple-element.31), channel_id=1, source_target_pairs={{0,8},{4,12},{8,0},{12,4},{1,9},{5,13},{9,1},{13,5},{2,10},{6,14},... | collective-permute-start | bytes 393224 | tf_op jit(solution)/shard_map/ppermute | solution.py:702
  119.6 16.3 %collective-permute-start.8 = (f32[4,32,256]{2,1,0:T(8,128)}, f32[4,32,256]{2,1,0:T(8,128)S(1)}, u32[]{:S(2)}, u32[]{:S(2)}) collective-permute-start(f32[4,32,256]{2,1,0:T(8,128)} %get-tuple-element.32), channel_id=1, source_target_pairs={{0,12},{4,0},{8,4},{12,8},{1,13},{5,1},{9,5},{13,9},{2,14},{6,2},{... | collective-permute-start | bytes 393224 | tf_op jit(solution)/shard_map/ppermute | solution.py:702
  135.9 0.7 copy-start.11
  135.9 0.7 copy-start.13
  135.9 0.7 copy-start.15
  140.0 17.5 %copy-start.18 = (f32[32,32]{1,0:T(8,128)S(1)}, f32[32,32]{1,0:T(8,128)}, u32[]{:S(2)}) copy-start(f32[32,32]{1,0:T(8,128)} %point_gradient.2) | copy-start | bytes 12292
  140.0 18.3 %copy-start.4 = (f32[4,32,256]{2,1,0:T(8,128)S(1)}, f32[4,32,256]{2,1,0:T(8,128)}, u32[]{:S(2)}) copy-start(f32[4,32,256]{2,1,0:T(8,128)} %get-tuple-element.33) | copy-start | bytes 393220
  140.0 18.3 %copy-start.17 = (f32[4,32,256]{2,1,0:T(8,128)S(1)}, f32[4,32,256]{2,1,0:T(8,128)}, u32[]{:S(2)}) copy-start(f32[4,32,256]{2,1,0:T(8,128)} %get-tuple-element.27) | copy-start | bytes 393220
  140.0 19.9 %collective-permute-start.12 = (f32[4,32,256]{2,1,0:T(8,128)}, f32[4,32,256]{2,1,0:T(8,128)S(1)}, u32[]{:S(2)}, u32[]{:S(2)}) collective-permute-start(f32[4,32,256]{2,1,0:T(8,128)} %get-tuple-element.35.rest_0_), channel_id=1, source_target_pairs={{0,4},{4,8},{8,12},{12,0},{1,5},{5,9},{9,13},{13,1},{2,6},{6,10},{... | collective-permute-start | bytes 393224 | tf_op jit(solution)/shard_map/ppermute | solution.py:702
  140.3 20.2 %collective-permute-start.13 = (f32[4,32,256]{2,1,0:T(8,128)}, f32[4,32,256]{2,1,0:T(8,128)S(1)}, u32[]{:S(2)}, u32[]{:S(2)}) collective-permute-start(f32[4,32,256]{2,1,0:T(8,128)} %get-tuple-element.35.rest_0_), channel_id=1, source_target_pairs={{0,8},{4,12},{8,0},{12,4},{1,9},{5,13},{9,1},{13,5},{2,10},{6,14},... | collective-permute-start | bytes 393224 | tf_op jit(solution)/shard_map/ppermute | solution.py:702
  141.1 19.3 %collective-permute-start.14 = (f32[4,32,256]{2,1,0:T(8,128)}, f32[4,32,256]{2,1,0:T(8,128)S(1)}, u32[]{:S(2)}, u32[]{:S(2)}) collective-permute-start(f32[4,32,256]{2,1,0:T(8,128)} %get-tuple-element.35.rest_0_), channel_id=1, source_target_pairs={{0,12},{4,0},{8,4},{12,8},{1,13},{5,1},{9,5},{13,9},{2,14},{6,2},{... | collective-permute-start | bytes 393224 | tf_op jit(solution)/shard_map/ppermute | solution.py:702
  158.4 34.3 %copy-start = (f32[9,32,256]{2,1,0:T(8,128)}, f32[9,32,256]{2,1,0:T(8,128)S(1)}, u32[]{:S(2)}) copy-start(f32[9,32,256]{2,1,0:T(8,128)S(1)} %pad_maximum_fusion.refs_0_.refs_4_) | copy-start | bytes 884740
  158.4 34.3 %collective-permute-start.10 = (f32[9,32,256]{2,1,0:T(8,128)S(1)}, f32[9,32,256]{2,1,0:T(8,128)S(1)}, u32[]{:S(2)}, u32[]{:S(2)}) collective-permute-start(f32[9,32,256]{2,1,0:T(8,128)S(1)} %pad_maximum_fusion.refs_0_.refs_4_), channel_id=1, source_target_pairs={{0,2},{1,3},{2,0},{3,1},{4,6},{5,7},{6,4},{7,5},{8,10},{9,11},{10,... | collective-permute-start | bytes 884744 | tf_op jit(solution)/shard_map/ppermute | solution.py:702
  159.9 32.7 %collective-permute-start.11 = (f32[9,32,256]{2,1,0:T(8,128)S(1)}, f32[9,32,256]{2,1,0:T(8,128)S(1)}, u32[]{:S(2)}, u32[]{:S(2)}) collective-permute-start(f32[9,32,256]{2,1,0:T(8,128)S(1)} %pad_maximum_fusion.refs_0_.refs_4_), channel_id=1, source_target_pairs={{0,3},{1,0},{2,1},{3,2},{4,7},{5,4},{6,5},{7,6},{8,11},{9,8},{10,9... | collective-permute-start | bytes 884744 | tf_op jit(solution)/shard_map/ppermute | solution.py:702
  160.0 0.7 copy-start.5
  160.0 32.7 %collective-permute-start.9 = (f32[9,32,256]{2,1,0:T(8,128)S(1)}, f32[9,32,256]{2,1,0:T(8,128)S(1)}, u32[]{:S(2)}, u32[]{:S(2)}) collective-permute-start(f32[9,32,256]{2,1,0:T(8,128)S(1)} %pad_maximum_fusion.refs_0_.refs_4_), channel_id=1, source_target_pairs={{0,1},{1,2},{2,3},{3,0},{4,5},{5,6},{6,7},{7,4},{8,9},{9,10},{10,1... | collective-permute-start | bytes 884744 | tf_op jit(solution)/shard_map/ppermute | solution.py:702
  160.5 0.6 copy-start.6
  161.1 0.7 copy-start.7
  192.6 5.1 %copy-start.1 = (f32[9,32,256]{2,1,0:T(8,128)}, f32[9,32,256]{2,1,0:T(8,128)S(1)}, u32[]{:S(2)}) copy-start(f32[9,32,256]{2,1,0:T(8,128)S(1)} %collective-permute-done.10.refs_2_.refs_6_) | copy-start | bytes 884740
  192.7 5.1 %copy-start.2 = (f32[9,32,256]{2,1,0:T(8,128)}, f32[9,32,256]{2,1,0:T(8,128)S(1)}, u32[]{:S(2)}) copy-start(f32[9,32,256]{2,1,0:T(8,128)S(1)} %collective-permute-done.11.refs_3_.refs_7_) | copy-start | bytes 884740
  192.7 5.0 %copy-start.3 = (f32[9,32,256]{2,1,0:T(8,128)}, f32[9,32,256]{2,1,0:T(8,128)S(1)}, u32[]{:S(2)}) copy-start(f32[9,32,256]{2,1,0:T(8,128)S(1)} %collective-permute-done.9.refs_1_.refs_5_) | copy-start | bytes 884740
  192.7 17.1 %collective-permute-start.15 = (f32[32,33]{1,0:T(8,128)S(1)}, f32[32,33]{1,0:T(8,128)S(1)}, u32[]{:S(2)}, u32[]{:S(2)}) collective-permute-start(f32[32,33]{1,0:T(8,128)S(1)} %add_bitcast_fusion), channel_id=1, source_target_pairs={{0,4},{4,8},{8,12},{12,0},{1,5},{5,9},{9,13},{13,1},{2,6},{6,10},{... | collective-permute-start | bytes 12680 | tf_op jit(solution)/shard_map/ppermute | solution.py:702
  193.3 16.5 %collective-permute-start.16 = (f32[32,33]{1,0:T(8,128)S(1)}, f32[32,33]{1,0:T(8,128)S(1)}, u32[]{:S(2)}, u32[]{:S(2)}) collective-permute-start(f32[32,33]{1,0:T(8,128)S(1)} %add_bitcast_fusion), channel_id=1, source_target_pairs={{0,8},{4,12},{8,0},{12,4},{1,9},{5,13},{9,1},{13,5},{2,10},{6,14},... | collective-permute-start | bytes 12680 | tf_op jit(solution)/shard_map/ppermute | solution.py:702
  194.9 14.9 %collective-permute-start.17 = (f32[32,33]{1,0:T(8,128)S(1)}, f32[32,33]{1,0:T(8,128)S(1)}, u32[]{:S(2)}, u32[]{:S(2)}) collective-permute-start(f32[32,33]{1,0:T(8,128)S(1)} %add_bitcast_fusion), channel_id=1, source_target_pairs={{0,12},{4,0},{8,4},{12,8},{1,13},{5,1},{9,5},{13,9},{2,14},{6,2},{... | collective-permute-start | bytes 12680 | tf_op jit(solution)/shard_map/ppermute | solution.py:702
  209.9 0.7 copy-start.19
